TPU v7x, 32 devices: a whole 2x2x4 slice. The times are simulated.
32 devices in a mesh: slot: 8 (over y, x, core), replica: 4 (over z).
Axes of the slice: x: 2, y: 2, z: 4, core: 2. Of those that a mesh axis runs over, the one named last changes fastest.
Arguments:
- layer_in: bfloat16 [4, 2432, 2560], P('replica', 'slot'), may hold values from -36 to 36
- seg_starts: int32 [4, 13], P('replica'), may hold values from 0 to 2304, as said below
- seg_parents: int32 [4, 13], P('replica'), may hold values from 0 to 4, as said below
- w_query: bfloat16 [2560, 2560], P('slot'), may hold values from -0.125 to 0.125
- w_key: bfloat16 [2560, 640], P('slot'), may hold values from -0.125 to 0.125
- w_value: bfloat16 [2560, 640], P('slot'), may hold values from -0.125 to 0.125
- w_out: bfloat16 [2560, 2560], P('slot'), may hold values from -2 to 2
- w_gate: bfloat16 [2560, 6912], P('slot'), may hold values from -0.125 to 0.125
- w_up: bfloat16 [2560, 6912], P('slot'), may hold values from -0.125 to 0.125
- w_down: bfloat16 [6912, 2560], P('slot'), may hold values from -0.078125 to 0.078125
- gain_attn: bfloat16 [2560], P('slot'), may hold values from 0.5 to 1.5
- gain_ffn: bfloat16 [2560], P('slot'), may hold values from 0.5 to 1.5
- out_cotangent: bfloat16 [4, 2432, 2560], P('replica', 'slot'), may hold values from -6 to 6
Outputs:
- layer_out: bfloat16 [4, 2432, 2560], P('replica', 'slot')
- grad_in: bfloat16 [4, 2432, 2560], P('replica', 'slot')
- grad_query: float32 [2560, 2560], P('slot')
- grad_key: float32 [2560, 640], P('slot')
- grad_value: float32 [2560, 640], P('slot')
- grad_proj: float32 [2560, 2560], P('slot')
- grad_gate: float32 [2560, 6912], P('slot')
- grad_up: float32 [2560, 6912], P('slot')
- grad_down: float32 [6912, 2560], P('slot')
- grad_gain_attn: float32 [2560], P('slot')
- grad_gain_ffn: float32 [2560], P('slot')
Inputs may be any that keep to these rules, and one draw needn't show every extreme that they name: `seg_starts`: segments of one tree never intersect; the trunk starts at slot 0 and some segment ends at slot 2431. `seg_parents`: the trunk's and every branch's entry is 0; each leaf's entry is a branch, and each branch is the parent of 2 leaves.
All inputs are finite; a program needn't handle non-finite values.
Results may differ from a plain program's by a relative error of at most 0.023.
Values may be sent and summed in bfloat16 or wider, within the bound.
No kernel may reach another device: no remote copies, remote signals or barrier semaphores. Data moves between devices by JAX's collectives and lax.ppermute only.
A program may use at most 576 MiB of HBM per device.

v0:
```python
import jax
import jax.numpy as jnp
from jax import lax
from jax.sharding import PartitionSpec as P

HEAD_DIM = 80
TRUNK = 768
BRANCH = 128
LEAF = 128
NBRANCH = 4
SEGS = 13


epsilon = 1e-05
rope_theta = 10000.0
masked_score = -1e30
block_split = 4


def normed(values):
    inverse = lax.rsqrt(jnp.mean(values * values, axis=-1, keepdims=True) + epsilon)
    return (values * inverse, inverse)


def norm_back(upward, unit_rows, inverse):
    return inverse * (upward - unit_rows * jnp.mean(upward * unit_rows, axis=-1, keepdims=True))


def rotate(values, position, direction):
    half_dim = values.shape[-1] // 2
    frequency = jnp.power(rope_theta, -2.0 * lax.iota(jnp.float32, half_dim) / values.shape[-1])
    angle = position.astype(jnp.float32)[:, None] * frequency[None, :]
    cosine = jnp.cos(angle)[:, None, :]
    sine = direction * jnp.sin(angle)[:, None, :]
    former = values[..., :half_dim]
    latter = values[..., half_dim:]
    return jnp.concatenate(
        [former * cosine - latter * sine, latter * cosine + former * sine], axis=-1
    )


def layout(starts, parents, slot_count):
    slot_index = lax.iota(jnp.int32, slot_count)
    segment_ids = lax.iota(jnp.int32, SEGS)
    segment_len = jnp.where(
        segment_ids == 0, TRUNK, jnp.where(segment_ids <= NBRANCH, BRANCH, LEAF)
    )
    depth_base = jnp.where(
        segment_ids == 0, 0, jnp.where(segment_ids <= NBRANCH, TRUNK, TRUNK + BRANCH)
    )
    inside = (slot_index[None, :] >= starts[:, None]) & (
        slot_index[None, :] < (starts + segment_len)[:, None]
    )
    live_slot = jnp.any(inside, axis=0)
    segment = jnp.sum(jnp.where(inside, segment_ids[:, None], 0), axis=0) + jnp.where(
        live_slot, 0, SEGS
    )
    position = jnp.sum(
        jnp.where(inside, slot_index[None, :] - starts[:, None] + depth_base[:, None], 0), axis=0
    )
    grandparent = jnp.sum(
        jnp.where(parents[:, None] == segment_ids[None, :], parents[None, :], 0), axis=1
    )
    own_bits = (
        jnp.left_shift(1, segment_ids) | jnp.left_shift(1, parents) | jnp.left_shift(1, grandparent)
    )
    path_bits = jnp.sum(jnp.where(inside, own_bits[:, None], 0), axis=0)
    key_bit = jnp.left_shift(1, segment)
    return (position, path_bits, key_bit, live_slot)


def permitted(query_slots, query_bits, query_pos, key_slots, key_bit, key_pos):
    same_slot = query_slots[:, None] == key_slots[None, :]
    on_path = jnp.bitwise_and(query_bits[:, None], key_bit[None, :]) != 0
    return same_slot | on_path & (key_pos[None, :] <= query_pos[:, None])


def score(queries, key_block, score_scale):
    return (
        jnp.einsum("rkgd,tkd->kgrt", queries, key_block, preferred_element_type=jnp.float32)
        * score_scale
    )


def keep_carry(carry):
    return carry


def fetch_attn(w_query, w_key, w_value, gain_attn):
    return (
        lax.all_gather(w_query, "slot", axis=0, tiled=True),
        lax.all_gather(w_key, "slot", axis=0, tiled=True),
        lax.all_gather(w_value, "slot", axis=0, tiled=True),
        lax.all_gather(gain_attn, "slot", axis=0, tiled=True),
    )


def fetch_out(w_out):
    return lax.all_gather(w_out, "slot", axis=0, tiled=True)


def fetch_ffn(w_gate, w_up, gain_ffn):
    return (
        lax.all_gather(w_gate, "slot", axis=0, tiled=True),
        lax.all_gather(w_up, "slot", axis=0, tiled=True),
        lax.all_gather(gain_ffn, "slot", axis=0, tiled=True),
    )


def fetch_down(w_down):
    return lax.all_gather(w_down, "slot", axis=0, tiled=True)


def transpose_dot(left, right):
    return lax.dot_general(
        left, right, (((1,), (1,)), ((), ())), preferred_element_type=jnp.float32
    )


def rows_dot(left, right):
    return lax.dot_general(
        left, right, (((0,), (0,)), ((), ())), preferred_element_type=jnp.float32
    )


def shards(
    layer_in,
    seg_starts,
    seg_parents,
    w_query,
    w_key,
    w_value,
    w_out,
    w_gate,
    w_up,
    w_down,
    gain_attn,
    gain_ffn,
    out_cotangent,
):
    row_count = layer_in.shape[1]
    slot_count = row_count * lax.axis_size("slot")
    first_slot = lax.axis_index("slot") * row_count
    heads = w_query.shape[1] // HEAD_DIM
    kv_heads = w_key.shape[1] // HEAD_DIM
    head_group = heads // kv_heads
    score_scale = HEAD_DIM ** (-0.5)
    block_len = slot_count // block_split
    position, path_bits, key_bit, live_slot = layout(seg_starts[0], seg_parents[0], slot_count)
    all_slots = lax.iota(jnp.int32, slot_count)
    my_slots = first_slot + lax.iota(jnp.int32, row_count)
    my_pos = lax.dynamic_slice_in_dim(position, first_slot, row_count)
    my_bits = lax.dynamic_slice_in_dim(path_bits, first_slot, row_count)
    my_live = lax.dynamic_slice_in_dim(live_slot, first_slot, row_count)
    residual = layer_in[0].astype(jnp.float32)
    full_query, full_key, full_value, full_gain_attn = fetch_attn(
        w_query, w_key, w_value, gain_attn
    )
    unit_attn, rms_attn = normed(residual)
    attn_input = (unit_attn * full_gain_attn.astype(jnp.float32)).astype(jnp.bfloat16)
    query_pre = jnp.dot(attn_input, full_query, preferred_element_type=jnp.float32)
    key_pre = jnp.dot(attn_input, full_key, preferred_element_type=jnp.float32)
    value_pre = jnp.dot(attn_input, full_value, preferred_element_type=jnp.float32)
    queries = (
        rotate(query_pre.reshape(row_count, heads, HEAD_DIM), my_pos, 1.0)
        .astype(jnp.bfloat16)
        .reshape(row_count, kv_heads, head_group, HEAD_DIM)
    )
    keys_mine = (
        rotate(key_pre.reshape(row_count, kv_heads, HEAD_DIM), my_pos, 1.0)
        .astype(jnp.bfloat16)
        .reshape(row_count, kv_heads * HEAD_DIM)
    )
    values_mine = value_pre.astype(jnp.bfloat16)
    keys_all, values_all = (
        lax.all_gather(keys_mine, "slot", axis=0, tiled=True),
        lax.all_gather(values_mine, "slot", axis=0, tiled=True),
    )
    keys_all = keys_all.reshape(slot_count, kv_heads, HEAD_DIM)
    values_all = values_all.reshape(slot_count, kv_heads, HEAD_DIM)
    key_blocks = []
    for block_index in range(block_split):
        offset = block_index * block_len
        allowed = permitted(
            my_slots,
            my_bits,
            my_pos,
            all_slots[offset : offset + block_len],
            key_bit[offset : offset + block_len],
            position[offset : offset + block_len],
        )
        key_blocks.append(
            (
                keys_all[offset : offset + block_len],
                values_all[offset : offset + block_len],
                allowed,
            )
        )
    running_top = jnp.full((kv_heads, head_group, row_count), masked_score, jnp.float32)
    running_sum = jnp.zeros((kv_heads, head_group, row_count), jnp.float32)
    for key_block, value_block, allowed in key_blocks:

        def update(carry, key_block=key_block, allowed=allowed):
            top_now, sum_now = carry
            logits = jnp.where(allowed, score(queries, key_block, score_scale), masked_score)
            top_new = jnp.maximum(top_now, jnp.max(logits, axis=-1))
            weights = jnp.where(allowed, jnp.exp(logits - top_new[..., None]), 0.0)
            return (top_new, sum_now * jnp.exp(top_now - top_new) + jnp.sum(weights, axis=-1))

        running_top, running_sum = lax.cond(
            jnp.any(allowed), update, keep_carry, (running_top, running_sum)
        )
    log_total = running_top + jnp.log(running_sum)
    attn_acc = jnp.zeros((row_count, kv_heads, head_group, HEAD_DIM), jnp.float32)
    for key_block, value_block, allowed in key_blocks:

        def accumulate(carry, key_block=key_block, value_block=value_block, allowed=allowed):
            logits = jnp.where(allowed, score(queries, key_block, score_scale), masked_score)
            probs = jnp.where(allowed, jnp.exp(logits - log_total[..., None]), 0.0).astype(
                jnp.bfloat16
            )
            return carry + jnp.einsum(
                "kgrt,tkd->rkgd", probs, value_block, preferred_element_type=jnp.float32
            )

        attn_acc = lax.cond(jnp.any(allowed), accumulate, keep_carry, attn_acc)
    attended = attn_acc.reshape(row_count, heads * HEAD_DIM).astype(jnp.bfloat16)
    full_out = fetch_out(w_out)
    middle = residual + jnp.dot(attended, full_out, preferred_element_type=jnp.float32)
    full_gate, full_up, full_gain_ffn = fetch_ffn(w_gate, w_up, gain_ffn)
    unit_ffn, rms_ffn = normed(middle)
    ffn_input = (unit_ffn * full_gain_ffn.astype(jnp.float32)).astype(jnp.bfloat16)
    gate_proj = jnp.dot(ffn_input, full_gate, preferred_element_type=jnp.float32)
    up_proj = jnp.dot(ffn_input, full_up, preferred_element_type=jnp.float32)
    sigmoid_gate = jax.nn.sigmoid(gate_proj)
    silu_gate = gate_proj * sigmoid_gate
    activated = (silu_gate * up_proj).astype(jnp.bfloat16)
    full_down = fetch_down(w_down)
    layer_out = (middle + jnp.dot(activated, full_down, preferred_element_type=jnp.float32)).astype(
        jnp.bfloat16
    )
    upstream = out_cotangent[0].astype(jnp.float32) * my_live.astype(jnp.float32)[:, None]
    down_input = upstream.astype(jnp.bfloat16)
    activated_grad = transpose_dot(down_input, full_down)
    grad_down = lax.psum_scatter(
        rows_dot(activated, down_input).astype(jnp.bfloat16),
        "slot",
        scatter_dimension=0,
        tiled=True,
    ).astype(jnp.float32)
    gate_grad = (
        activated_grad * up_proj * sigmoid_gate * (1.0 + gate_proj * (1.0 - sigmoid_gate))
    ).astype(jnp.bfloat16)
    up_grad = (activated_grad * silu_gate).astype(jnp.bfloat16)
    back_gate, back_up, back_gain_ffn = fetch_ffn(w_gate, w_up, gain_ffn)
    ffn_input_grad = transpose_dot(gate_grad, back_gate) + transpose_dot(up_grad, back_up)
    gain_ffn_term = jnp.sum(ffn_input_grad * unit_ffn, axis=0)
    middle_grad = upstream + norm_back(
        ffn_input_grad * back_gain_ffn.astype(jnp.float32), unit_ffn, rms_ffn
    )
    branch_grad = middle_grad.astype(jnp.bfloat16)
    grad_gate, grad_up, grad_gain_ffn, grad_proj = jax.tree.map(
        lambda part: lax.psum_scatter(
            part.astype(jnp.bfloat16), "slot", scatter_dimension=0, tiled=True
        ).astype(jnp.float32),
        (
            rows_dot(ffn_input, gate_grad),
            rows_dot(ffn_input, up_grad),
            gain_ffn_term,
            rows_dot(attended, branch_grad),
        ),
    )
    back_out = fetch_out(w_out)
    attended_heads = (
        transpose_dot(branch_grad, back_out)
        .astype(jnp.bfloat16)
        .reshape(row_count, kv_heads, head_group, HEAD_DIM)
    )
    row_dot = jnp.einsum("rkgd,rkgd->kgr", attended_heads.astype(jnp.float32), attn_acc)
    query_acc = jnp.zeros((row_count, kv_heads, head_group, HEAD_DIM), jnp.float32)
    key_parts = []
    value_parts = []
    for key_block, value_block, allowed in key_blocks:

        def backward_block(carry, key_block=key_block, value_block=value_block, allowed=allowed):
            logits = jnp.where(allowed, score(queries, key_block, score_scale), masked_score)
            probs = jnp.where(allowed, jnp.exp(logits - log_total[..., None]), 0.0)
            prob_grad = jnp.einsum(
                "rkgd,tkd->kgrt", attended_heads, value_block, preferred_element_type=jnp.float32
            )
            score_grad = (probs * (prob_grad - row_dot[..., None])).astype(jnp.bfloat16)
            updated = carry + jnp.einsum(
                "kgrt,tkd->rkgd", score_grad, key_block, preferred_element_type=jnp.float32
            )
            key_part = jnp.einsum(
                "kgrt,rkgd->tkd", score_grad, queries, preferred_element_type=jnp.float32
            )
            value_part = jnp.einsum(
                "kgrt,rkgd->tkd",
                probs.astype(jnp.bfloat16),
                attended_heads,
                preferred_element_type=jnp.float32,
            )
            return (updated, key_part, value_part)

        def skip_block(carry):
            empty_part = jnp.zeros((block_len, kv_heads, HEAD_DIM), jnp.float32)
            return (carry, empty_part, empty_part)

        query_acc, key_part, value_part = lax.cond(
            jnp.any(allowed), backward_block, skip_block, query_acc
        )
        key_parts.append(key_part)
        value_parts.append(value_part)
    key_grad_all = (
        jnp.concatenate(key_parts, axis=0).reshape(slot_count, kv_heads * HEAD_DIM) * score_scale
    )
    value_grad_all = jnp.concatenate(value_parts, axis=0).reshape(slot_count, kv_heads * HEAD_DIM)
    key_grad_mine, value_grad_mine = (
        lax.psum_scatter(
            key_grad_all.astype(jnp.bfloat16), "slot", scatter_dimension=0, tiled=True
        ).astype(jnp.float32),
        lax.psum_scatter(
            value_grad_all.astype(jnp.bfloat16), "slot", scatter_dimension=0, tiled=True
        ).astype(jnp.float32),
    )
    query_grad = (
        rotate(query_acc.reshape(row_count, heads, HEAD_DIM) * score_scale, my_pos, -1.0)
        .reshape(row_count, heads * HEAD_DIM)
        .astype(jnp.bfloat16)
    )
    key_grad = (
        rotate(key_grad_mine.reshape(row_count, kv_heads, HEAD_DIM), my_pos, -1.0)
        .reshape(row_count, kv_heads * HEAD_DIM)
        .astype(jnp.bfloat16)
    )
    value_grad = value_grad_mine.astype(jnp.bfloat16)
    back_query, back_key, back_value, back_gain_attn = fetch_attn(
        w_query, w_key, w_value, gain_attn
    )
    attn_input_grad = (
        transpose_dot(query_grad, back_query)
        + transpose_dot(key_grad, back_key)
        + transpose_dot(value_grad, back_value)
    )
    gain_attn_term = jnp.sum(attn_input_grad * unit_attn, axis=0)
    input_grad = middle_grad + norm_back(
        attn_input_grad * back_gain_attn.astype(jnp.float32), unit_attn, rms_attn
    )
    grad_query, grad_key, grad_value, grad_gain_attn = jax.tree.map(
        lambda part: lax.psum_scatter(
            part.astype(jnp.bfloat16), "slot", scatter_dimension=0, tiled=True
        ).astype(jnp.float32),
        (
            rows_dot(attn_input, query_grad),
            rows_dot(attn_input, key_grad),
            rows_dot(attn_input, value_grad),
            gain_attn_term,
        ),
    )
    (
        grad_query,
        grad_key,
        grad_value,
        grad_proj,
        grad_gate,
        grad_up,
        grad_down,
        grad_gain_attn,
        grad_gain_ffn,
    ) = (
        lax.psum(grad_query.astype(jnp.bfloat16), "replica").astype(jnp.float32),
        lax.psum(grad_key.astype(jnp.bfloat16), "replica").astype(jnp.float32),
        lax.psum(grad_value.astype(jnp.bfloat16), "replica").astype(jnp.float32),
        lax.psum(grad_proj.astype(jnp.bfloat16), "replica").astype(jnp.float32),
        lax.psum(grad_gate.astype(jnp.bfloat16), "replica").astype(jnp.float32),
        lax.psum(grad_up.astype(jnp.bfloat16), "replica").astype(jnp.float32),
        lax.psum(grad_down.astype(jnp.bfloat16), "replica").astype(jnp.float32),
        lax.psum(grad_gain_attn.astype(jnp.bfloat16), "replica").astype(jnp.float32),
        lax.psum(grad_gain_ffn.astype(jnp.bfloat16), "replica").astype(jnp.float32),
    )
    return (
        layer_out[None],
        input_grad.astype(jnp.bfloat16)[None],
        grad_query,
        grad_key,
        grad_value,
        grad_proj,
        grad_gate,
        grad_up,
        grad_down,
        grad_gain_attn,
        grad_gain_ffn,
    )


def solution(mesh):
    in_specs = (
        P("replica", "slot", None),
        P("replica", None),
        P("replica", None),
        P("slot", None),
        P("slot", None),
        P("slot", None),
        P("slot", None),
        P("slot", None),
        P("slot", None),
        P("slot", None),
        P("slot"),
        P("slot"),
        P("replica", "slot", None),
    )
    out_specs = (
        P("replica", "slot", None),
        P("replica", "slot", None),
        P("slot", None),
        P("slot", None),
        P("slot", None),
        P("slot", None),
        P("slot", None),
        P("slot", None),
        P("slot", None),
        P("slot"),
        P("slot"),
    )
    return jax.shard_map(shards, mesh=mesh, in_specs=in_specs, out_specs=out_specs, check_vma=False)
```

profile of v0, /device:TPU:0, one launch (start us, length us, event | category | flops | bytes accessed | tf_op | source)
XLA Modules:
  0.0 2839.7 jit_solution(15103778608431075453)
XLA Ops:
  12.5 25.9 all-reduce.5
  40.2 5.4 all-gather.16.cloned.1.call-done
  45.6 4.6 convolution_convert_fusion.8
  51.7 28.7 %all-gather.10.cloned.1.call-done = bf16[2560,640]{1,0:T(8,128)(2,1)} async-done(((bf16[320,640]{1,0:T(8,128)(2,1)}), bf16[2560,640]{1,0:T(8,128)(2,1)}) %all-gather.10.cloned.1.call-update) | async-done | bytes 3276816 | tf_op jit(solution)/shard_map/all_gather | solution.py:92
  80.4 5.7 copy.93
  86.0 3.9 fusion.190
  101.6 13.4 all-gather.18.cloned.1.call-done
  125.2 24.4 all-gather.12.cloned.1.call-done
  159.7 66.0 %all-gather.14.cloned.1.call-done = bf16[2560,2560]{1,0:T(8,128)(2,1)} async-done(((bf16[320,2560]{1,0:T(8,128)(2,1)}), bf16[2560,2560]{1,0:T(8,128)(2,1)}) %all-gather.14.cloned.1.call-update) | async-done | bytes 13107216 | tf_op jit(solution)/shard_map/all_gather | solution.py:91
  225.7 18.0 copy.96
  243.7 10.4 fusion.188
  255.3 28.7 %conditional.12 = (f32[8,4,304]{2,1,0:T(4,128)}, f32[8,4,304]{2,1,0:T(4,128)}) conditional(s32[]{:T(128)} %convert_element_type.268, () %tuple.111, (pred[304,608]{1,0:T(8,128)(4,1)S(1)}, bf16[608,8,80]{0,2,1:T(8,128)(2,1)S(1)}, bf16[304,8,4,80]{0,3,2,1:T(8,128)(2,1)S(1)}) %tuple.301), branch_computations={%region_10.11_spmd, %region_11.14_spmd} | conditional | flops 993686016 | bytes 50332688 | solution.py:210
  255.5 13.0 fusion
  269.1 14.2 select_reduce_fusion
  285.8 21.3 conditional.16
  292.5 14.6 fusion.19
  307.3 8.1 conditional.19
  318.1 8.8 multiply_reduce_fusion.2
  329.0 144.5 %all-gather.24.cloned.1.call-done = bf16[2560,6912]{1,0:T(8,128)(2,1)} async-done(((bf16[320,6912]{1,0:T(8,128)(2,1)}), bf16[2560,6912]{1,0:T(8,128)(2,1)}) %all-gather.24.cloned.1.call-update) | async-done | bytes 35389456 | tf_op jit(solution)/shard_map/all_gather | solution.py:105
  473.5 22.5 fusion.231
  495.9 149.2 %all-gather.22.cloned.1.call-done = bf16[2560,6912]{1,0:T(8,128)(2,1)} async-done(((bf16[320,6912]{1,0:T(8,128)(2,1)}), bf16[2560,6912]{1,0:T(8,128)(2,1)}) %all-gather.22.cloned.1.call-update) | async-done | bytes 35389456 | tf_op jit(solution)/shard_map/all_gather | solution.py:104
  645.1 22.5 fusion.230
  667.6 149.2 %all-gather.26.cloned.1.call-done = bf16[6912,2560]{1,0:T(8,128)(2,1)} async-done(((bf16[864,2560]{1,0:T(8,128)(2,1)}), bf16[6912,2560]{1,0:T(8,128)(2,1)}) %all-gather.26.cloned.1.call-update) | async-done | bytes 35389456 | tf_op jit(solution)/shard_map/all_gather | solution.py:111
  816.8 36.5 %multiply_convert_fusion = (bf16[304,6912]{1,0:T(8,128)(2,1)}, bf16[304,6912]{1,0:T(8,128)(2,1)}, bf16[304,6912]{1,0:T(8,128)(2,1)}) fusion(f32[304,6912]{1,0:T(8,128)} %fusion.230, f32[304,6912]{1,0:T(8,128)} %fusion.231, bf16[6912,2560]{1,0:T(8,128)(2,1)} %all-gather.26.cloned.1.call-done, bf16[1,304,2560]{2,1,0:T(8,128)(2,1)S(1)} %copy-done.32, ...), kind=kOutput, calls=%fused_computation.170 | convolution fusion | flops 10792243200 | bytes 66364608 | tf_op jit(solution)/shard_map/dot_general | solution.py:115
  853.3 19.0 fusion.232
  872.3 21.8 multiply_reduce_fusion
  899.1 8.6 convolution_convert_fusion.7
  907.8 4.4 copy.104
  912.1 3.4 fusion.167
  915.9 55.5 %conditional.20 = (f32[304,8,4,80]{0,3,2,1:T(8,128)}, f32[608,8,80]{0,2,1:T(8,128)}, bf16[608,8,80]{0,2,1:T(8,128)(2,1)}) conditional(s32[]{:T(128)} %convert_element_type.268, () %tuple.120, (pred[304,608]{1,0:T(8,128)(4,1)S(1)}, bf16[608,8,80]{0,2,1:T(8,128)(2,1)S(1)}, bf16[304,8,4,80]{0,3,2,1:T(8,128)(2,1)S(1)}, f32[8,4,304]{2,1,0:T(4,128)S(1)}, ...), branch_computations={%region_36.37_spmd, %region_37.38_spmd} | conditional | flops 4803063808 | bytes 171388000 | solution.py:310
  916.8 10.1 fusion.97
  926.8 12.4 fusion.92
  939.2 13.0 fusion.82
  952.3 4.5 copy-done.2
  960.1 11.1 convolution_bitcast_fusion
  973.7 8.8 conditional.22
  982.4 13.5 conditional.23
  996.0 8.9 concatenate.31
  1011.6 5.7 concatenate.33
  1020.8 193.6 %reduce-scatter.28.cloned.1.call-done = bf16[304,640]{1,0:T(8,128)(2,1)} async-done(((bf16[2432,640]{1,0:T(8,128)(2,1)}), bf16[304,640]{1,0:T(8,128)(2,1)}) %reduce-scatter.28.cloned.1.call-update) | async-done | bytes 389136
  1216.7 3.9 convolution_convert_fusion.6
  1220.7 45.2 %reduce-scatter.30.cloned.1.call-done = bf16[304,640]{1,0:T(8,128)(2,1)} async-done(((bf16[2432,640]{1,0:T(8,128)(2,1)}), bf16[304,640]{1,0:T(8,128)(2,1)}) %reduce-scatter.30.cloned.1.call-update) | async-done | bytes 389136
  1265.9 4.9 convolution_convert_fusion.5
  1270.9 11.7 convolution_convert_fusion.3
  1286.5 10.2 convolution_convert_fusion.4
  1297.4 25.3 convolution_convert_fusion
  1323.0 25.3 convolution_convert_fusion.1
  1348.4 25.3 convolution_convert_fusion.2
  1374.0 92.2 %reduce-scatter.20.cloned.1.call-done = bf16[320,2560]{1,0:T(8,128)(2,1)} async-done(((bf16[2560,2560]{1,0:T(8,128)(2,1)}), bf16[320,2560]{1,0:T(8,128)(2,1)}) %reduce-scatter.20.cloned.1.call-update) | async-done | bytes 1638416 | tf_op jit(solution)/shard_map/reduce_scatter | solution.py:263
  1466.1 98.6 %reduce-scatter.14.cloned.1.call-done = bf16[320,2560]{1,0:T(8,128)(2,1)} async-done(((bf16[2560,2560]{1,0:T(8,128)(2,1)}), bf16[320,2560]{1,0:T(8,128)(2,1)}) %reduce-scatter.14.cloned.1.call-update) | async-done | bytes 1638416 | tf_op jit(solution)/shard_map/reduce_scatter | solution.py:351
  1564.8 217.6 %reduce-scatter.26.cloned.1.call-done = bf16[864,2560]{1,0:T(8,128)(2,1)} async-done(((bf16[6912,2560]{1,0:T(8,128)(2,1)}), bf16[864,2560]{1,0:T(8,128)(2,1)}) %reduce-scatter.26.cloned.1.call-update) | async-done | bytes 4423696 | tf_op jit(solution)/shard_map/reduce_scatter | solution.py:245
  1782.4 218.0 %reduce-scatter.24.cloned.1.call-done = bf16[320,6912]{1,0:T(8,128)(2,1)} async-done(((bf16[2560,6912]{1,0:T(8,128)(2,1)}), bf16[320,6912]{1,0:T(8,128)(2,1)}) %reduce-scatter.24.cloned.1.call-update) | async-done | bytes 4423696 | tf_op jit(solution)/shard_map/reduce_scatter | solution.py:263
  2000.4 217.6 %reduce-scatter.22.cloned.1.call-done = bf16[320,6912]{1,0:T(8,128)(2,1)} async-done(((bf16[2560,6912]{1,0:T(8,128)(2,1)}), bf16[320,6912]{1,0:T(8,128)(2,1)}) %reduce-scatter.22.cloned.1.call-update) | async-done | bytes 4423696 | tf_op jit(solution)/shard_map/reduce_scatter | solution.py:263
  2218.6 10.3 fusion.233
  2228.9 20.1 fusion.174
  2249.0 4.6 convolution_add_fusion
  2257.0 24.9 all-reduce.4
  2282.0 14.7 all-reduce.6
  2297.9 4.9 fusion.187
  2302.8 506.6 %all-reduce.10.cloned.1.call-done = (bf16[320,2560]{1,0:T(8,128)(2,1)}, bf16[320,640]{1,0:T(8,128)(2,1)}, bf16[320,640]{1,0:T(8,128)(2,1)}, bf16[320,2560]{1,0:T...) async-done(((bf16[320,2560]{1,0:T(8,128)(2,1)}, bf16[320,640]{1,0:T(8,128)(2,1)}, bf16[320,640]{1,0:T(8,128)(2,1)}, ...) | async-done | bytes 17367056 | tf_op jit(solution)/shard_map/psum | solution.py:372
  2813.5 3.6 convert_element_type.300
  2819.3 4.7 convert_element_type.308
  2824.0 4.1 convert_element_type.310
  2828.1 4.8 convert_element_type.312
  (226 shorter events, 93.3 us)
Async XLA Ops:
  7.2 38.4 %all-gather.16.cloned.1.call-start = ((), (), s32[]{:S(2)}) async-start(), calls=%async_computation.12 | async-start | bytes 3686400 | tf_op jit(solution)/shard_map/all_gather | solution.py:93
  7.9 72.5 %all-gather.10.cloned.1.call-start = ((), (), s32[]{:S(2)}) async-start(), calls=%async_computation.9 | async-start | bytes 3686400 | tf_op jit(solution)/shard_map/all_gather | solution.py:92
  8.7 106.4 %all-gather.18.cloned.1.call-start = ((), (), s32[]{:S(2)}) async-start(), calls=%async_computation.13 | async-start | bytes 3502080 | tf_op jit(solution)/shard_map/all_gather | solution.py:177
  38.3 205.4 %copy-start.43 = (f32[2560]{0:T(1024)}, f32[2560]{0:T(1024)S(1)}, u32[]{:S(2)}) copy-start(f32[2560]{0:T(1024)S(1)} %convert_element_type.270) | copy-start | bytes 30724
  40.2 203.6 %copy-start.46 = (f32[304]{0:T(512)}, f32[304]{0:T(512)S(1)}, u32[]{:S(2)}) copy-start(f32[304]{0:T(512)S(1)} %add_rsqrt_fusion.1) | copy-start | bytes 3652
  40.2 10.1 copy-start.53
  40.2 10.3 copy-start.52
  50.2 35.9 %copy-start.3 = (bf16[1,304,2560]{2,1,0:T(8,128)(2,1)S(1)}, bf16[1,304,2560]{2,1,0:T(8,128)(2,1)}, u32[]{:S(2)}) copy-start(bf16[1,304,2560]{2,1,0:T(8,128)(2,1)} %param.37) | copy-start | bytes 4669444
  50.2 99.4 %all-gather.12.cloned.1.call-start = ((), (), s32[]{:S(2)}) async-start(), calls=%async_computation.10 | async-start | bytes 3502080 | tf_op jit(solution)/shard_map/all_gather | solution.py:176
  51.7 202.4 %copy-start.33 = (f32[304,40]{0,1:T(8,128)}, f32[304,40]{0,1:T(8,128)S(1)}, u32[]{:S(2)}) copy-start(f32[304,40]{0,1:T(8,128)S(1)} %get-tuple-element.544) | copy-start | bytes 145924
  91.1 134.6 %all-gather.14.cloned.1.call-start = ((), (), s32[]{:S(2)}) async-start(), calls=%async_computation.11 | async-start | bytes 14745600 | tf_op jit(solution)/shard_map/all_gather | solution.py:91
  91.7 226.4 %all-gather.20.cloned.1.call-start = ((), (), s32[]{:S(2)}) async-start(), calls=%async_computation.14 | async-start | bytes 14745600 | tf_op jit(solution)/shard_map/all_gather | solution.py:99
  92.3 381.2 %all-gather.24.cloned.1.call-start = ((), (), s32[]{:S(2)}) async-start(), calls=%async_computation.16 | async-start | bytes 39813120 | tf_op jit(solution)/shard_map/all_gather | solution.py:105
  93.0 552.1 %all-gather.22.cloned.1.call-start = ((), (), s32[]{:S(2)}) async-start(), calls=%async_computation.15 | async-start | bytes 39813120 | tf_op jit(solution)/shard_map/all_gather | solution.py:104
  93.8 723.1 %all-gather.26.cloned.1.call-start = ((), (), s32[]{:S(2)}) async-start(), calls=%async_computation.17 | async-start | bytes 39813120 | tf_op jit(solution)/shard_map/all_gather | solution.py:111
  94.5 1119.9 %reduce-scatter.28.cloned.1.call-start = ((), (), s32[]{:S(2)}) async-start(), calls=%async_computation.25 | async-start | bytes 3502080
  255.0 52.4 %copy-start = (bf16[304,8,4,80]{0,3,2,1:T(8,128)(2,1)}, bf16[304,8,4,80]{0,3,2,1:T(8,128)(2,1)S(1)}, u32[]{:S(2)}) copy-start(bf16[304,8,4,80]{0,3,2,1:T(8,128)(2,1)S(1)} %pad_maximum_fusion) | copy-start | bytes 4669444
  318.1 8.9 copy-start.13
  318.1 10.5 copy-start.45
  328.9 316.2 %copy-start.31 = (bf16[304,2560]{1,0:T(8,128)(2,1)}, bf16[304,2560]{1,0:T(8,128)(2,1)S(1)}, u32[]{:S(2)}) copy-start(bf16[304,2560]{1,0:T(8,128)(2,1)S(1)} %multiply_convert_fusion.4) | copy-start | bytes 4669444
  495.9 320.9 %copy-start.32 = (bf16[1,304,2560]{2,1,0:T(8,128)(2,1)S(1)}, bf16[1,304,2560]{2,1,0:T(8,128)(2,1)}, u32[]{:S(2)}) copy-start(bf16[1,304,2560]{2,1,0:T(8,128)(2,1)} %param.49) | copy-start | bytes 4669444
  495.9 320.9 %copy-start.49 = (f32[304]{0:T(512)S(1)}, f32[304]{0:T(512)}, u32[]{:S(2)}) copy-start(f32[304]{0:T(512)} %dynamic-slice_convert_fusion) | copy-start | bytes 3652
  853.3 19.0 copy-start.6
  897.5 1.7 copy-start.12
  907.7 7.8 copy-start.1
  907.8 7.8 copy-start.27
  907.8 7.8 copy-start.48
  912.1 3.4 copy-start.10
  912.1 3.5 copy-start.15
  912.1 3.7 copy-start.40
  915.9 55.5 %copy-start.8 = (bf16[608,640]{0,1:T(8,128)(2,1)S(1)}, bf16[608,640]{0,1:T(8,128)(2,1)}, u32[]{:S(2)}) copy-start(bf16[608,640]{0,1:T(8,128)(2,1)} %copy.147) | copy-start | bytes 2334724
  915.9 55.5 %copy-start.24 = (pred[304,608]{1,0:T(8,128)(4,1)S(1)}, pred[304,608]{1,0:T(8,128)(4,1)}, u32[]{:S(2)}) copy-start(pred[304,608]{1,0:T(8,128)(4,1)} %get-tuple-element.537) | copy-start | bytes 554500
  952.3 4.5 copy-start.2
  971.4 2.3 copy-start.22
  973.7 8.8 copy-start.7
  973.7 8.8 copy-start.20
  1011.5 254.4 %reduce-scatter.30.cloned.1.call-start = ((), (), s32[]{:S(2)}) async-start(), calls=%async_computation.26 | async-start | bytes 3502080
  1020.7 195.0 %copy-start.34 = (f32[304,40]{0,1:T(8,128)S(1)}, f32[304,40]{0,1:T(8,128)}, u32[]{:S(2)}) copy-start(f32[304,40]{0,1:T(8,128)} %copy-done.33) | copy-start | bytes 145924
  1020.7 195.1 %copy-start.41 = (f32[304,40]{0,1:T(8,128)S(1)}, f32[304,40]{0,1:T(8,128)}, u32[]{:S(2)}) copy-start(f32[304,40]{0,1:T(8,128)} %get-tuple-element.542) | copy-start | bytes 145924
  1020.7 196.0 %copy-start.4 = (bf16[1,304,2560]{2,1,0:T(8,128)(2,1)S(1)}, bf16[1,304,2560]{2,1,0:T(8,128)(2,1)}, u32[]{:S(2)}) copy-start(bf16[1,304,2560]{2,1,0:T(8,128)(2,1)} %param.37) | copy-start | bytes 4669444
  1020.7 196.0 %copy-start.44 = (f32[2560]{0:T(1024)S(1)}, f32[2560]{0:T(1024)}, u32[]{:S(2)}) copy-start(f32[2560]{0:T(1024)} %copy-done.43) | copy-start | bytes 30724
  1020.7 196.0 %copy-start.47 = (f32[304]{0:T(512)S(1)}, f32[304]{0:T(512)}, u32[]{:S(2)}) copy-start(f32[304]{0:T(512)} %copy-done.46) | copy-start | bytes 3652
  1020.7 353.2 %reduce-scatter.16.cloned.1.call-start = ((), (), s32[]{:S(2)}) async-start(), calls=%async_computation.19 | async-start | bytes 3686400 | tf_op jit(solution)/shard_map/reduce_scatter | solution.py:351
  1220.7 50.2 %copy-start.14 = (bf16[304,8,4,80]{0,3,2,1:T(8,128)(2,1)S(1)}, bf16[304,8,4,80]{0,3,2,1:T(8,128)(2,1)}, u32[]{:S(2)}) copy-start(bf16[304,8,4,80]{0,3,2,1:T(8,128)(2,1)} %copy-done.13) | copy-start | bytes 4669444
  1220.7 153.3 %reduce-scatter.18.cloned.1.call-start = ((), (), s32[]{:S(2)}) async-start(), calls=%async_computation.20 | async-start | bytes 3686400 | tf_op jit(solution)/shard_map/reduce_scatter | solution.py:351
  1270.8 195.3 %reduce-scatter.20.cloned.1.call-start = ((), (), s32[]{:S(2)}) async-start(), calls=%async_computation.21 | async-start | bytes 14745600 | tf_op jit(solution)/shard_map/reduce_scatter | solution.py:263
  1282.6 282.1 %reduce-scatter.14.cloned.1.call-start = ((), (), s32[]{:S(2)}) async-start(), calls=%async_computation.18 | async-start | bytes 14745600 | tf_op jit(solution)/shard_map/reduce_scatter | solution.py:351
  1283.1 2.6 copy-start.35
  1283.1 2.6 copy-start.42
  1296.7 485.7 %reduce-scatter.26.cloned.1.call-start = ((), (), s32[]{:S(2)}) async-start(), calls=%async_computation.24 | async-start | bytes 39813120 | tf_op jit(solution)/shard_map/reduce_scatter | solution.py:245
  1322.8 677.7 %reduce-scatter.24.cloned.1.call-start = ((), (), s32[]{:S(2)}) async-start(), calls=%async_computation.23 | async-start | bytes 39813120 | tf_op jit(solution)/shard_map/reduce_scatter | solution.py:263
  1348.3 869.7 %reduce-scatter.22.cloned.1.call-start = ((), (), s32[]{:S(2)}) async-start(), calls=%async_computation.22 | async-start | bytes 39813120 | tf_op jit(solution)/shard_map/reduce_scatter | solution.py:263
  1373.7 1435.7 %all-reduce.10.cloned.1.call-start = ((), (), s32[]{:S(2)}) async-start(), calls=%async_computation.27 | async-start | bytes 34734080 | tf_op jit(solution)/shard_map/psum | solution.py:372
  2228.9 20.1 copy-start.29
  2249.0 4.7 copy-start.19
  2249.0 4.7 copy-start.36
  2253.7 3.3 copy-start.51
  2809.4 7.7 copy-start.30
  2811.4 7.8 slice-start.4
  2813.5 5.7 slice-start.5
  2817.1 6.8 slice-start.2
  2819.2 4.7 slice-start.3
  2819.2 8.9 slice-start
  2824.0 4.1 slice-start.1
  (6 other events, 6.3 us)
Sparse Core Ops, SparseCore 0:
  9.9 35.6 all-gather.15
  47.5 32.8 all-gather.9
  82.8 32.1 all-gather.17
  117.4 32.1 all-gather.11
  151.3 74.3 all-gather.13
  227.4 74.3 all-gather.19
  303.7 169.7 all-gather.23
  475.4 169.7 all-gather.21
  647.0 169.7 all-gather.25
  1011.7 202.6 reduce-scatter.27
  1218.8 47.0 reduce-scatter.29
  1269.7 46.8 reduce-scatter.15
  1320.6 46.8 reduce-scatter.17
  1371.0 95.1 reduce-scatter.19
  1469.6 95.1 reduce-scatter.13
  1568.3 214.0 reduce-scatter.25
  1786.4 213.9 reduce-scatter.23
  2004.0 214.0 reduce-scatter.21
  2221.9 587.4 all-reduce.9
where the time goes:
time: 2850 us; the launch traced here: 2840 us
  waiting for transfers between devices  2170 us (76%)
  matrix products  381 us (13%)
  local copies, waits for them, and re-layouts  92.9 us (3%)
  other arithmetic  71.3 us (3%)
  blocking collectives  65.5 us (2%)
  loops' own time  33.6 us (1%)
    reduce_scatter x6, waiting for transfers between devices, shards(): lax.psum_scatter(part.astype(jnp.bfloat16), 'slot', scatter_dimension=0,...  626 us
    psum x1, waiting for transfers between devices, shards(): lax.psum(grad_query.astype(jnp.bfloat16), 'replica').astype(jnp.float32)  507 us
    unnamed x21, waiting for transfers between devices  243 us
    reduce_scatter x1, waiting for transfers between devices, shards(): lax.psum_scatter(rows_dot(activated, down_input).astype(jnp.bfloat16), 's...  218 us
    all_gather x1, waiting for transfers between devices, fetch_down(): return lax.all_gather(w_down, 'slot', axis=0, tiled=True)  149 us
    all_gather x1, waiting for transfers between devices, fetch_ffn(): lax.all_gather(w_gate, 'slot', axis=0, tiled=True)  149 us
    all_gather x1, waiting for transfers between devices, fetch_ffn(): lax.all_gather(w_up, 'slot', axis=0, tiled=True)  145 us
    dot_general x7, matrix products, rows_dot(): lax.dot_general(left, right, (((0,), (0,)), ((), ())), preferred_element_...  107 us
  transfers between devices with their start and end apart: 19, of which 16 were waited for; matrix products, arithmetic and copies ran while one was open for 12% of the time, Pallas kernels for 0%

commit v1 on v0

v1 whole, which is shorter than its diff:
```python
import functools
import jax
import jax.numpy as jnp
from jax import lax
from jax.experimental import pallas as pl
from jax.experimental.pallas import tpu as pltpu
from jax.sharding import PartitionSpec as P

HEAD_DIM = 80
TRUNK = 768
SEGS = 13
TILE = 128
NBRANCH = 4
SEG_TILES = TRUNK // TILE + SEGS - 1
TRUNK_TILES = TRUNK // TILE
LANES = 128
epsilon = 1e-05
masked_score = -1e30
rope_theta = 10000.0
log2e = 1.4426950408889634


def pad_lanes(width):
    return -(-width // LANES) * LANES


def turn_tables():
    half = HEAD_DIM // 2
    frequency = jnp.power(rope_theta, -2.0 * lax.iota(jnp.float32, half) / HEAD_DIM)
    angle = lax.iota(jnp.float32, TRUNK + 2 * TILE)[:, None] * frequency[None, :]
    cosine, sine = jnp.cos(angle), jnp.sin(angle)
    none = jnp.zeros_like(sine)
    tail = jnp.zeros((angle.shape[0], LANES - HEAD_DIM), jnp.float32)
    return jnp.stack(
        [
            jnp.concatenate([cosine, cosine, tail], axis=1),
            jnp.concatenate([none, sine, tail], axis=1),
            jnp.concatenate([-sine, none, tail], axis=1),
        ]
    )


def tile_base(tile):
    return jnp.where(
        tile < TRUNK_TILES,
        tile * TILE,
        jnp.where(tile < TRUNK_TILES + NBRANCH, TRUNK, TRUNK + TILE),
    )


def take_head(rows, head):
    width = rows.shape[1]
    shift = (width - head * HEAD_DIM) % width
    return (pltpu.roll(rows, shift, 1) if shift else rows)[:, :LANES]


def put_head(part, head, width):
    wide = jnp.concatenate(
        [part, jnp.zeros((part.shape[0], width - LANES), part.dtype)], axis=1
    )
    return pltpu.roll(wide, head * HEAD_DIM, 1) if head else wide


def turn(rows, tables, sign):
    half = HEAD_DIM // 2
    cosine, up, down = tables
    swapped = pltpu.roll(rows, half, 1) * up + pltpu.roll(rows, LANES - half, 1) * down
    return rows * cosine + swapped if sign > 0 else rows * cosine - swapped


def head_lanes(rows):
    lane = lax.broadcasted_iota(jnp.int32, rows.shape, 1)
    return jnp.where(lane < HEAD_DIM, rows, 0.0)


def read_rows(ref, start):
    aligned = pl.multiple_of(start // 8 * 8, 8)
    rows = ref[pl.ds(aligned, TILE + 8), :]
    return pltpu.roll(rows, (TILE + 8) - (start - aligned), 0)[:TILE]


def write_rows(ref, start, rows):
    aligned = pl.multiple_of(start // 8 * 8, 8)
    offset = start - aligned
    at = pl.ds(aligned, TILE + 8)
    wide = jnp.concatenate([rows, jnp.zeros((8, rows.shape[1]), rows.dtype)], axis=0)
    wide = pltpu.roll(wide, offset, 0)
    index = lax.broadcasted_iota(jnp.int32, wide.shape, 0)
    inside = (index >= offset) & (index < offset + TILE)
    ref[at, :] = jnp.where(inside, wide, ref[at, :])


def nt(a, b):
    return lax.dot_general(a, b, (((1,), (1,)), ((), ())), preferred_element_type=jnp.float32)


def nn(a, b):
    return lax.dot_general(a, b, (((1,), (0,)), ((), ())), preferred_element_type=jnp.float32)


def causal(columns):
    key = lax.broadcasted_iota(jnp.int32, (TILE, columns), 0)
    query = lax.broadcasted_iota(jnp.int32, (TILE, columns), 1) % TILE
    return key <= query


def each_tile(tile_fn, parent_of):
    for tile in range(TRUNK_TILES):
        tile_fn(tile, tile * TILE, None)

    @pl.loop(TRUNK_TILES, TRUNK_TILES + NBRANCH)
    def _(tile):
        tile_fn(tile, TRUNK, None)

    @pl.loop(TRUNK_TILES + NBRANCH, SEG_TILES)
    def _(tile):
        tile_fn(tile, TRUNK, parent_of(tile) + TRUNK_TILES - 1)


def tile_rows(tile, size=TILE):
    if isinstance(tile, int):
        return pl.ds(tile * size, size)
    return pl.ds(pl.multiple_of(tile * size, size), size)


def forward_kernel(
    group, starts, parents, order, qkv, tables,
    attended, q_keep, k_keep, v_keep, lse_keep,
    slots, v_turned, out_rows,
):
    slot_count = qkv.shape[0] * qkv.shape[1]
    width = slots.shape[1]
    out_width = out_rows.shape[1]
    block = qkv.shape[1]

    @pl.loop(0, qkv.shape[0])
    def _(i):
        slots[pl.ds(pl.multiple_of(order[i] * block, 8), block), :] = qkv[i]

    @pl.loop(0, slot_count // TILE)
    def _(i):
        rows = tile_rows(i)
        own = take_head(slots[rows, :], group + 1)
        own = head_lanes(own).astype(jnp.bfloat16).astype(jnp.float32)
        total = put_head(own, 0, out_width)
        for head in range(1, group):
            total = total + put_head(own, head, out_width)
        out_rows[rows, :] = total

    @pl.loop(0, SEG_TILES)
    def _(tile):
        rows = read_rows(slots, starts[tile])
        base = pl.ds(pl.multiple_of(tile_base(tile), TILE), TILE)
        turns = tuple(tables[t, base, :] for t in range(3))
        for head in range(group):
            turned = turn(take_head(rows, head), turns, 1) * (HEAD_DIM**-0.5 * log2e)
            at = pl.ds(pl.multiple_of(tile * (group * TILE) + head * TILE, TILE), TILE)
            q_keep[at, :] = turned.astype(jnp.bfloat16)
        k_keep[tile_rows(tile), :] = turn(take_head(rows, group), turns, 1).astype(jnp.bfloat16)
        own = head_lanes(take_head(rows, group + 1))
        v_keep[tile_rows(tile), :] = own.astype(jnp.bfloat16)
        v_turned[:, tile_rows(tile)] = own.T.astype(jnp.bfloat16)

    columns = group * TILE

    def attend(tile, full, parent):
        queries = q_keep[tile_rows(tile, columns), :]
        keys = [pl.ds(0, full)] if full else []
        if parent is not None:
            keys.append(tile_rows(parent))
        keys.append(tile_rows(tile))
        scores = [nt(k_keep[at, :], queries) for at in keys]
        scores[-1] = jnp.where(causal(columns), scores[-1], masked_score)
        top = functools.reduce(jnp.maximum, [jnp.max(s, axis=0, keepdims=True) for s in scores])
        weights = [jnp.exp2(s - top) for s in scores]
        total = functools.reduce(jnp.add, [jnp.sum(w, axis=0, keepdims=True) for w in weights])
        mixed = functools.reduce(
            jnp.add,
            [nn(v_turned[:, at], w.astype(jnp.bfloat16)) for at, w in zip(keys, weights)],
        )
        mixed = mixed * (1.0 / total)
        lse_keep[pl.ds(tile, 1)] = (top + jnp.log2(total))[None]
        result = put_head(mixed[:, :TILE].T, 0, out_width)
        for head in range(1, group):
            result = result + put_head(
                mixed[:, head * TILE : (head + 1) * TILE].T, head, out_width
            )
        write_rows(out_rows, starts[tile], result)

    each_tile(attend, lambda tile: parents[tile - TRUNK_TILES + 1])

    kept = attended.shape[-1]

    @pl.loop(0, qkv.shape[0])
    def _(i):
        rows = out_rows[pl.ds(pl.multiple_of(order[i] * block, 8), block), :]
        attended[i] = rows[:, :kept].astype(jnp.bfloat16)


def backward_kernel(
    group, starts, parents, order, attended_grad, q_keep, k_keep, v_keep, lse_keep, tables,
    grads,
    slots, do_keep, k_turned, dk, dv, dq, out_rows,
):
    slot_count = attended_grad.shape[0] * attended_grad.shape[1]
    in_width = slots.shape[1]
    width = out_rows.shape[1]
    block = attended_grad.shape[1]
    kept = attended_grad.shape[2]
    columns = group * TILE

    slots[...] = jnp.zeros_like(slots)

    @pl.loop(0, attended_grad.shape[0])
    def _(i):
        at = pl.ds(pl.multiple_of(order[i] * block, 8), block)
        slots[at, :kept] = attended_grad[i].astype(jnp.float32)

    @pl.loop(0, slot_count // TILE)
    def _(i):
        rows = slots[tile_rows(i), :]
        total = take_head(rows, 0)
        for head in range(1, group):
            total = total + take_head(rows, head)
        out_rows[tile_rows(i), :] = put_head(head_lanes(total), group + 1, width)

    @pl.loop(0, SEG_TILES)
    def _(tile):
        rows = read_rows(slots, starts[tile])
        for head in range(group):
            at = pl.ds(pl.multiple_of(tile * columns + head * TILE, TILE), TILE)
            do_keep[at, :] = head_lanes(take_head(rows, head)).astype(jnp.bfloat16)
        k_turned[:, tile_rows(tile)] = (
            k_keep[tile_rows(tile), :].astype(jnp.float32).T.astype(jnp.bfloat16)
        )

    dk[...] = jnp.zeros_like(dk)
    dv[...] = jnp.zeros_like(dv)

    def attend(tile, full, parent):
        queries = q_keep[tile_rows(tile, columns), :]
        upward = do_keep[tile_rows(tile, columns), :]
        lse = lse_keep[pl.ds(tile, 1)][0]
        keys = [pl.ds(0, full)] if full else []
        if parent is not None:
            keys.append(tile_rows(parent))
        keys.append(tile_rows(tile))
        probs = [jnp.exp2(nt(k_keep[at, :], queries) - lse) for at in keys]
        probs[-1] = jnp.where(causal(columns), probs[-1], 0.0)
        prob_grads = [nt(v_keep[at, :], upward) for at in keys]
        row_dot = functools.reduce(
            jnp.add,
            [jnp.sum(p * g, axis=0, keepdims=True) for p, g in zip(probs, prob_grads)],
        )
        mixed = None
        for at, p, g in zip(keys, probs, prob_grads):
            score_grad = (p * (g - row_dot)).astype(jnp.bfloat16)
            dv[at, :] += nn(p.astype(jnp.bfloat16), upward)
            dk[at, :] += nn(score_grad, queries)
            part = nn(k_turned[:, at], score_grad)
            mixed = part if mixed is None else mixed + part
        base = pl.ds(pl.multiple_of(tile_base(tile), TILE), TILE)
        turns = tuple(tables[t, base, :] for t in range(3))
        result = None
        for head in range(group):
            part = turn(mixed[:, head * TILE : (head + 1) * TILE].T, turns, -1) * HEAD_DIM**-0.5
            part = put_head(part, head, width)
            result = part if result is None else result + part
        dq[tile_rows(tile), :] = result

    each_tile(attend, lambda tile: parents[tile - TRUNK_TILES + 1])

    @pl.loop(0, SEG_TILES)
    def _(tile):
        rows = tile_rows(tile)
        base = pl.ds(pl.multiple_of(tile_base(tile), TILE), TILE)
        turns = tuple(tables[t, base, :] for t in range(3))
        key_part = turn(dk[rows, :], turns, -1) * (1.0 / log2e)
        total = dq[rows, :] + put_head(key_part, group, width)
        total = total + put_head(dv[rows, :], group + 1, width)
        write_rows(out_rows, starts[tile], total)

    @pl.loop(0, attended_grad.shape[0])
    def _(i):
        rows = out_rows[pl.ds(pl.multiple_of(order[i] * block, 8), block), :]
        grads[i] = rows[:, : grads.shape[2]].astype(jnp.bfloat16)


SMEM = pl.BlockSpec(memory_space=pltpu.SMEM)
VMEM = pl.BlockSpec(memory_space=pltpu.VMEM)


def attend_forward(group, qkv, tables, starts, parents, order):
    blocks, block, width = qkv.shape
    slot_count = blocks * block
    wide = pad_lanes(width)
    out_wide = pad_lanes(group * HEAD_DIM)
    live = SEG_TILES * TILE
    return pl.pallas_call(
        functools.partial(forward_kernel, group),
        out_shape=(
            jax.ShapeDtypeStruct((blocks, block, group * HEAD_DIM), jnp.bfloat16),
            jax.ShapeDtypeStruct((group * live, LANES), jnp.bfloat16),
            jax.ShapeDtypeStruct((live, LANES), jnp.bfloat16),
            jax.ShapeDtypeStruct((live, LANES), jnp.bfloat16),
            jax.ShapeDtypeStruct((SEG_TILES, 1, group * TILE), jnp.float32),
        ),
        in_specs=[SMEM, SMEM, SMEM, VMEM, VMEM],
        out_specs=(VMEM,) * 5,
        scratch_shapes=[
            pltpu.VMEM((slot_count + 8, wide), jnp.float32),
            pltpu.VMEM((LANES, live), jnp.bfloat16),
            pltpu.VMEM((slot_count + 8, out_wide), jnp.float32),
        ],
        compiler_params=pltpu.CompilerParams(vmem_limit_bytes=48 * 2**20),
        name="tree_forward",
    )(starts, parents, order, qkv, tables)


def attend_backward(attended_grad, kept, tables, starts, parents, order):
    blocks, block, width = attended_grad.shape
    slot_count = blocks * block
    group = width // HEAD_DIM
    wide = pad_lanes((group + 2) * HEAD_DIM + 2)
    in_wide = pad_lanes(width)
    live = SEG_TILES * TILE
    return pl.pallas_call(
        functools.partial(backward_kernel, group),
        out_shape=jax.ShapeDtypeStruct((blocks, block, wide), jnp.bfloat16),
        in_specs=[SMEM, SMEM, SMEM] + [VMEM] * 6,
        out_specs=VMEM,
        scratch_shapes=[
            pltpu.VMEM((slot_count + 8, in_wide), jnp.float32),
            pltpu.VMEM((group * live, LANES), jnp.bfloat16),
            pltpu.VMEM((LANES, live), jnp.bfloat16),
            pltpu.VMEM((live, LANES), jnp.float32),
            pltpu.VMEM((live, LANES), jnp.float32),
            pltpu.VMEM((live, wide), jnp.float32),
            pltpu.VMEM((slot_count + 8, wide), jnp.float32),
        ],
        compiler_params=pltpu.CompilerParams(vmem_limit_bytes=56 * 2**20),
        name="tree_backward",
    )(starts, parents, order, attended_grad, *kept, tables)


def window(ref, rows, start, size, wide, at):
    full = ref.shape[-1]
    span = min(pad_lanes(size + LANES - 1), full)
    aligned = jnp.minimum(start // LANES * LANES, full - span)
    shift = start - aligned
    values = ref[rows, pl.ds(pl.multiple_of(aligned, LANES), span)].astype(jnp.float32)
    lane = lax.broadcasted_iota(jnp.int32, values.shape, 1)
    values = jnp.where((lane >= shift) & (lane < shift + size), values, 0.0)
    reach = max(span, wide)
    if reach > span:
        filling = jnp.zeros((values.shape[0], reach - span), values.dtype)
        values = jnp.concatenate([values, filling], axis=1)
    return pltpu.roll(values, lax.rem(at - shift + reach, reach), 1)[:, :wide]


def pack_kernel(places, extras, step, me, *refs):
    sources, gains = refs[: len(places)], refs[len(places) : len(places) + extras]
    blocks = refs[len(places) + extras :]
    count = len(blocks)
    wide = blocks[0].shape[1]
    extra_at = sum(size for size, _ in places)

    @pl.loop(0, blocks[0].shape[0] // step)
    def _(i):
        rows = pl.ds(pl.multiple_of(i * step, step), step)
        lane = lax.broadcasted_iota(jnp.int32, (step, wide), 1)
        for way in range(count):
            total = None
            for ref, (size, at) in zip(sources, places):
                part = window(ref, rows, (me[0] ^ way) * size, size, wide, at)
                total = part if total is None else total + part
            for index, gain in enumerate(gains):
                total = jnp.where(lane == extra_at + index, gain[rows, :].astype(jnp.float32), total)
            blocks[way][rows, :] = total.astype(jnp.bfloat16)


def pack(weights, gains, me, places, wide, count):
    rows = weights[0].shape[0]
    return pl.pallas_call(
        functools.partial(pack_kernel, places, len(gains), 16),
        out_shape=(jax.ShapeDtypeStruct((rows, wide), jnp.bfloat16),) * count,
        in_specs=[SMEM] + [VMEM] * (len(weights) + len(gains)),
        out_specs=(VMEM,) * count,
        compiler_params=pltpu.CompilerParams(vmem_limit_bytes=48 * 2**20),
        name="pack_weights",
    )(me[None], *weights, *[gain[:, None] for gain in gains])


def assemble_kernel(count, extra_at, me, *refs):
    blocks, whole = refs[:count], refs[count]
    rows = blocks[0].shape[0]
    for way, block in enumerate(blocks):
        at = pl.ds(pl.multiple_of((me[0] ^ way) * rows, 16), rows)
        whole[at, :] = block[...]
    if extra_at is not None:
        gains = refs[count + 1]
        first = extra_at // LANES * LANES
        for index in range(whole.shape[0] // LANES):
            at = pl.ds(index * LANES, LANES)
            part = whole[at, first : first + LANES].astype(jnp.float32).T
            gains[:, at] = pltpu.roll(part, LANES - extra_at % LANES, 0)[:8]


def assemble(blocks, me, extra_at):
    rows, wide = blocks[0].shape
    shape = (len(blocks) * rows, wide)
    out_shape = (jax.ShapeDtypeStruct(shape, jnp.bfloat16),)
    if extra_at is not None:
        out_shape += (jax.ShapeDtypeStruct((8, shape[0]), jnp.float32),)
    return pl.pallas_call(
        functools.partial(assemble_kernel, len(blocks), extra_at),
        out_shape=out_shape,
        in_specs=[SMEM] + [VMEM] * len(blocks),
        out_specs=(VMEM,) * len(out_shape),
        compiler_params=pltpu.CompilerParams(vmem_limit_bytes=48 * 2**20),
        name="assemble_weights",
    )(me[None], *blocks)


def after(values, *earlier):
    anywhere = pl.BlockSpec(memory_space=pl.ANY)
    return pl.pallas_call(
        lambda *refs: None,
        out_shape=tuple(jax.ShapeDtypeStruct(v.shape, v.dtype) for v in values),
        in_specs=[anywhere] * (len(values) + len(earlier)),
        out_specs=(anywhere,) * len(values),
        input_output_aliases={i: i for i in range(len(values))},
        name="after",
    )(*values, *earlier)


def spread_kernel(places, count, me, *refs):
    blocks = refs[:count]
    weights = refs[count : count + len(places)]
    outs = refs[count + len(places) : count + 2 * len(places)]
    gain, held = refs[count + 2 * len(places) :]
    for way in range(count):
        held[me[0] ^ way] = blocks[way][...].astype(jnp.float32)
    for out in outs:
        out[...] = jnp.zeros_like(out)
    total = jnp.zeros(gain.shape, jnp.float32)
    for (size, at), weight, out in zip(places, weights, outs):
        full = out.shape[1]
        for index in range(count):
            start = index * size
            span = min(pad_lanes(size + start % LANES), full)
            aligned = min(start // LANES * LANES, full - span)
            shift = start - aligned
            low_lane = at // LANES * LANES
            width = pad_lanes(at - low_lane + size)
            values = held[index][:, low_lane : low_lane + width]
            lane = lax.broadcasted_iota(jnp.int32, values.shape, 1)
            inside = (lane >= at - low_lane) & (lane < at - low_lane + size)
            values = jnp.where(inside, values, 0.0)
            reach = max(span, width)
            if reach > width:
                filling = jnp.zeros((values.shape[0], reach - width), values.dtype)
                values = jnp.concatenate([values, filling], axis=1)
            turned = (shift - (at - low_lane)) % reach
            values = (pltpu.roll(values, turned, 1) if turned else values)[:, :span]
            out[:, aligned : aligned + span] += values
        product = out[...] * weight[...].astype(jnp.float32)
        total = total + jnp.sum(product, axis=1, keepdims=True)
    gain[...] = total


def spread(blocks, weights, me, places, step):
    count = len(blocks)
    rows, wide = blocks[0].shape
    tile = lambda width: pl.BlockSpec((step, width), lambda i: (i, 0))
    return pl.pallas_call(
        functools.partial(spread_kernel, places, count),
        grid=(rows // step,),
        out_shape=tuple(jax.ShapeDtypeStruct(w.shape, jnp.float32) for w in weights)
        + (jax.ShapeDtypeStruct((rows, 1), jnp.float32),),
        in_specs=[SMEM] + [tile(wide)] * count + [tile(w.shape[1]) for w in weights],
        out_specs=tuple(tile(w.shape[1]) for w in weights) + (tile(1),),
        scratch_shapes=[pltpu.VMEM((count, step, wide), jnp.float32)],
        compiler_params=pltpu.CompilerParams(vmem_limit_bytes=56 * 2**20),
        name="spread_gradients",
    )(me[None], *blocks, *weights)


def normed(values):
    inverse = lax.rsqrt(jnp.mean(values * values, axis=-1, keepdims=True) + epsilon)
    return (values * inverse, inverse)


def norm_back(upward, unit_rows, inverse):
    return inverse * (upward - unit_rows * jnp.mean(upward * unit_rows, axis=-1, keepdims=True))


def layout(starts, slot_count):
    slot_index = lax.iota(jnp.int32, slot_count)
    segment_ids = lax.iota(jnp.int32, SEGS)
    segment_len = jnp.where(segment_ids == 0, TRUNK, TILE)
    inside = (slot_index[None, :] >= starts[:, None]) & (
        slot_index[None, :] < (starts + segment_len)[:, None]
    )
    return jnp.any(inside, axis=0)


def dot(left, right):
    return jnp.dot(left, right, preferred_element_type=jnp.float32)


def transpose_dot(left, right):
    return lax.dot_general(
        left, right, (((1,), (1,)), ((), ())), preferred_element_type=jnp.float32
    )


def rows_dot(left, right):
    return lax.dot_general(
        left, right, (((0,), (0,)), ((), ())), preferred_element_type=jnp.float32
    )


def low(values):
    return values.astype(jnp.bfloat16)


def plain(count):
    return count != 8


def gather_order(count):
    if plain(count):
        return [list(range(count))] * count
    ways = ((0, 1, 2, 3, 5, 4, 6, 7), (0, 1, 4, 5, 3, 2, 6, 7))
    return [[index ^ way for way in ways[index % 2]] for index in range(count)]


def swap_core(values):
    return lax.ppermute(values, "slot", [(i, i ^ 1) for i in range(8)])


def swap_near(values):
    return lax.ppermute(values, "slot", [(i, i ^ (4 if i % 2 else 2)) for i in range(8)])


def swap_far(values):
    return lax.ppermute(values, "slot", [(i, i ^ (2 if i % 2 else 4)) for i in range(8)])


def gather(own):
    count = lax.axis_size("slot")
    if plain(count):
        return [lax.all_gather(own, "slot", axis=0, tiled=True)]
    block = own.shape[0]
    chip = jnp.concatenate([own, swap_core(own)], axis=0)
    near = swap_near(chip)
    corner = swap_far(near[:block])
    return [chip, near, swap_core(near), jnp.concatenate([corner, swap_core(corner)], axis=0)]


def scatter(parts):
    count = lax.axis_size("slot")
    if plain(count):
        return lax.psum_scatter(parts[0], "slot", scatter_dimension=0, tiled=True).astype(
            jnp.float32
        )
    chip, near, side, corner = parts
    block = chip.shape[0] // 2
    wide = lambda values: values.astype(jnp.float32)
    near_sum = low(wide(near) + wide(swap_core(side)))
    other = low(wide(chip[block:]) + wide(swap_near(near_sum[block:])))
    corner_sum = low(wide(corner[:block]) + wide(swap_core(corner[block:])))
    near_own = low(wide(near_sum[:block]) + wide(swap_far(corner_sum)))
    return wide(chip[:block]) + wide(swap_near(near_own)) + wide(swap_core(other))


def send(block, way):
    count = lax.axis_size("slot")
    if way == 0:
        return block
    return lax.ppermute(block, "slot", [(i, i ^ way) for i in range(count)])


def sum_trees(part):
    count = lax.axis_size("replica")
    if count != 4:
        return lax.psum(part, "replica")
    place = lax.axis_index("replica")
    wide = lambda values: values.astype(jnp.float32)
    pair = low(wide(part) + wide(lax.ppermute(part, "replica", [(0, 1), (3, 2)])))
    total = low(wide(pair) + wide(lax.ppermute(pair, "replica", [(1, 2), (2, 1)])))
    back = lax.ppermute(total, "replica", [(1, 0), (2, 3)])
    return jnp.where((place == 0) | (place == 3), back, total)


def to_columns(weights, gains, places, wide, heads_in, earlier=()):
    count = lax.axis_size("slot")
    me = lax.axis_index("slot")
    extra_at = sum(size for size, _ in places) if gains else None
    if plain(count):
        blocks = jnp.zeros((count, weights[0].shape[0], wide), jnp.bfloat16)
        for weight, (size, at), heads in zip(weights, places, heads_in):
            blocks = blocks.at[:, :, at : at + size].set(split_columns(weight, count, heads))
        for index, gain in enumerate(gains):
            blocks = blocks.at[:, :, extra_at + index].set(gain[None])
        whole = lax.all_to_all(blocks, "slot", 0, 0).reshape(-1, wide)
        if not gains:
            return (whole,)
        return whole, whole[:, extra_at : extra_at + len(gains)].T.astype(jnp.float32)
    blocks = pack(weights, gains, me, places, wide, count)
    if earlier:
        blocks = after(blocks, *earlier)
    return assemble([send(block, way) for way, block in enumerate(blocks)], me, extra_at)


def to_rows(gradient, weights, places, heads_in, group, step):
    count = lax.axis_size("slot")
    me = lax.axis_index("slot")
    rows = gradient.shape[0] // count
    if plain(count):
        blocks = lax.all_to_all(gradient.reshape(count, rows, -1), "slot", 0, 0)
        blocks = sum_trees(blocks).astype(jnp.float32)
        parts = [
            join_columns(blocks[:, :, at : at + size], heads)
            for (size, at), heads in zip(places, heads_in)
        ]
        products = [jnp.sum(p * w.astype(jnp.float32), axis=1) for p, w in zip(parts, weights)]
        return parts, sum(products)
    arrived = [None] * count
    for base in reversed(range(0, count, group)):
        first = (me ^ base) // group * group * rows
        summed = sum_trees(lax.dynamic_slice_in_dim(gradient, first, group * rows))
        for way in range(base, base + group):
            block = summed
            if group > 1:
                block = lax.dynamic_slice_in_dim(summed, (me ^ way) % group * rows, rows)
            arrived[way] = send(block, way)
    *parts, product = spread(arrived, weights, me, places, step)
    return parts, product[:, 0]


def split_columns(weight, count, heads_in=None):
    rows, columns = weight.shape
    if heads_in is not None and heads_in < count:
        weight = weight.reshape(rows, heads_in, columns // heads_in)
        weight = jnp.repeat(weight, count // heads_in, axis=1)
    else:
        weight = weight.reshape(rows, count, columns // count)
    return weight.transpose(1, 0, 2)


def join_columns(blocks, heads_in=None):
    count, rows, columns = blocks.shape
    if heads_in is not None and heads_in < count:
        blocks = jnp.sum(blocks.reshape(heads_in, count // heads_in, rows, columns), axis=1)
        count = heads_in
    return blocks.transpose(1, 0, 2).reshape(rows, count * columns)


def shards(
    layer_in,
    seg_starts,
    seg_parents,
    w_query,
    w_key,
    w_value,
    w_out,
    w_gate,
    w_up,
    w_down,
    gain_attn,
    gain_ffn,
    out_cotangent,
):
    count = lax.axis_size("slot")
    me = lax.axis_index("slot")
    row_count = layer_in.shape[1]
    slot_count = row_count * count
    features = layer_in.shape[2]
    kv_heads = w_key.shape[1] // HEAD_DIM
    q_width = w_query.shape[1] // count
    heads_width = q_width + 2 * HEAD_DIM
    heads_wide = pad_lanes(heads_width + 2)
    hidden = w_down.shape[0]
    hidden_wide = pad_lanes(hidden)
    starts, parents = seg_starts[0], seg_parents[0]
    tile_starts = jnp.concatenate([lax.iota(jnp.int32, TRUNK_TILES) * TILE, starts[1:]])
    order = jnp.asarray(gather_order(count), jnp.int32)[me]
    tables = turn_tables()
    live = layout(starts, slot_count).astype(jnp.float32).reshape(count, row_count)
    my_live = live[me]
    live = live[order].reshape(slot_count)

    def cut(values):
        return jnp.split(values, 1 if plain(count) else 4, axis=0)

    def blocks_of(parts):
        return jnp.concatenate(parts, axis=0).reshape(count, row_count, parts[0].shape[-1])

    layer_parts = gather(layer_in[0])
    head_weights = (w_query, w_key, w_value)
    head_places = ((q_width, 0), (HEAD_DIM, q_width), (HEAD_DIM, q_width + HEAD_DIM))
    head_counts = (None, kv_heads, kv_heads)
    w_heads, gains = to_columns(
        head_weights, (gain_attn, gain_ffn), head_places, heads_wide, head_counts
    )
    full_gain_attn, full_gain_ffn = gains[0], gains[1]
    attn_parts = [
        low(normed(part.astype(jnp.float32))[0] * full_gain_attn) for part in layer_parts
    ]
    qkv = blocks_of([dot(part, w_heads) for part in attn_parts])
    attended, *kept = attend_forward(q_width // HEAD_DIM, qkv, tables, tile_starts, parents, order)
    attended = attended.reshape(slot_count, q_width)
    residual = layer_in[0].astype(jnp.float32)
    middle = residual + scatter([low(dot(part, w_out)) for part in cut(attended)])

    hidden_places = ((hidden, 0), (hidden, hidden_wide))
    (w_hidden,) = to_columns(
        (w_gate, w_up), (), hidden_places, 2 * hidden_wide, (None, None), (w_heads, layer_parts[-1])
    )
    w_lower = jnp.pad(w_down, ((0, hidden_wide - hidden), (0, 0)))
    unit_ffn, rms_ffn = normed(middle)
    ffn_parts = gather(low(unit_ffn * full_gain_ffn))
    late_cotangent = out_cotangent[0]
    if not plain(count):
        (late_cotangent,) = after((late_cotangent,), w_hidden)
    down_parts = [
        low(part.astype(jnp.float32) * mask[:, None])
        for part, mask in zip(gather(late_cotangent), cut(live))
    ]
    active_parts, hidden_grads = [], []
    for ffn_part, down_part in zip(ffn_parts, down_parts):
        both = dot(ffn_part, w_hidden)
        gate, up = both[:, :hidden_wide], both[:, hidden_wide:]
        sigmoid = jax.nn.sigmoid(gate)
        silu = gate * sigmoid
        active_parts.append(low(silu * up))
        active_grad = transpose_dot(down_part, w_lower)
        gate_grad = low(active_grad * up * sigmoid * (1.0 + gate * (1.0 - sigmoid)))
        hidden_grads.append(jnp.concatenate([gate_grad, low(active_grad * silu)], axis=1))
    ffn_input_grad = scatter([low(transpose_dot(part, w_hidden)) for part in hidden_grads])
    layer_out = low(middle + scatter([low(dot(part, w_lower)) for part in active_parts]))
    grad_down = rows_dot(
        jnp.concatenate(active_parts, axis=0), jnp.concatenate(down_parts, axis=0)
    )[:hidden]
    grad_hidden = low(
        rows_dot(jnp.concatenate(ffn_parts, axis=0), jnp.concatenate(hidden_grads, axis=0))
    )
    upstream = out_cotangent[0].astype(jnp.float32) * my_live[:, None]
    middle_grad = upstream + norm_back(ffn_input_grad * full_gain_ffn, unit_ffn, rms_ffn)

    branch_parts = gather(low(middle_grad))
    attended_grad = blocks_of([low(transpose_dot(part, w_out)) for part in branch_parts])
    head_grads = attend_backward(attended_grad, kept, tables, tile_starts, parents, order)
    head_parts = cut(head_grads.reshape(slot_count, heads_wide))
    attn_input_grad = scatter(
        [low(transpose_dot(part, w_heads)) for part in head_parts]
    )
    grad_proj = sum(rows_dot(a, b) for a, b in zip(cut(attended), branch_parts))
    grad_heads = low(sum(rows_dot(a, b) for a, b in zip(attn_parts, head_parts)))
    unit_attn, rms_attn = normed(residual)
    grad_in = low(
        middle_grad + norm_back(attn_input_grad * full_gain_attn, unit_attn, rms_attn)
    )

    grad_down = sum_trees(low(grad_down)).astype(jnp.float32)
    (grad_gate, grad_up), gain_ffn_sum = to_rows(
        grad_hidden, (w_gate, w_up), hidden_places, (None, None), 2, 32
    )
    grad_proj = sum_trees(low(grad_proj)).astype(jnp.float32)
    (grad_query, grad_key, grad_value), gain_attn_sum = to_rows(
        grad_heads, head_weights, head_places, head_counts, 4, 64
    )
    return (
        layer_out[None],
        grad_in[None],
        grad_query,
        grad_key,
        grad_value,
        grad_proj,
        grad_gate,
        grad_up,
        grad_down,
        gain_attn_sum / gain_attn.astype(jnp.float32),
        gain_ffn_sum / gain_ffn.astype(jnp.float32),
    )


def solution(mesh):
    tokens, tree, rows, vector = P("replica", "slot", None), P("replica", None), P("slot", None), P("slot")
    in_specs = (tokens, tree, tree) + (rows,) * 7 + (vector, vector, tokens)
    out_specs = (tokens, tokens) + (rows,) * 7 + (vector, vector)
    return jax.shard_map(shards, mesh=mesh, in_specs=in_specs, out_specs=out_specs, check_vma=False)
```

time: 2850 us -> 1520 us (0.53)
  waiting for transfers between devices: 2170 us -> 789 us
  Pallas kernels: 0 us -> 145 us
  matrix products: 381 us -> 256 us
  starting transfers between devices: 1.73 us -> 118 us
  blocking collectives: 65.5 us -> 0 us
  other arithmetic: 71.3 us -> 127 us
  loops' own time: 33.6 us -> 0 us
    reduce_scatter x7 -> x0, waiting for transfers between devices: 844 us -> none  [the longest x6 626 us: shards(): lax.psum_scatter(part.astype(jnp.bfloat16), 'slot', scatter_dimension=0,...]
    ppermute x0 -> x96, waiting for transfers between devices: none -> 789 us  [the longest x8 252 us: sum_trees(): back = lax.ppermute(total, 'replica', [(1, 0), (2, 3)])]
    all_gather x9 -> x0, waiting for transfers between devices: 581 us -> none  [the longest x1 149 us: fetch_down(): return lax.all_gather(w_down, 'slot', axis=0, tiled=True)]
    psum x1 -> x0, waiting for transfers between devices: 507 us -> none  [shards(): lax.psum(grad_query.astype(jnp.bfloat16), 'replica').astype(jnp.float32)]
    unnamed x21 -> x0, waiting for transfers between devices: 243 us -> none
    pallas_call x0 -> x10, Pallas kernels: none -> 145 us  [the longest x1 50.1 us: attend_backward(): pl.pallas_call(functools.partial(backward_kernel, group), out_shape=jax.S...]
    ppermute x0 -> x96, starting transfers between devices: none -> 118 us  [the longest x8 30.9 us: sum_trees(): lax.ppermute(part, 'replica', [(0, 1), (3, 2)])]
    dot_general x14 -> x16, matrix products: 170 us -> 83.6 us  [dot(): return jnp.dot(left, right, preferred_element_type=jnp.float32)]
  transfers between devices with their start and end apart: 19 -> 96, of which waited for: 16 -> 31; matrix products, arithmetic and copies ran while one was open for 12% -> 28% of each run, Pallas kernels for 0% -> 10%
where the time goes in v1:
time: 1520 us; the launch traced here: 1510 us
  waiting for transfers between devices  789 us (52%)
  matrix products  256 us (17%)
  Pallas kernels  145 us (10%)
  other arithmetic  127 us (8%)
  starting transfers between devices  118 us (8%)
  local copies, waits for them, and re-layouts  75.1 us (5%)
    ppermute x8, waiting for transfers between devices, sum_trees(): back = lax.ppermute(total, 'replica', [(1, 0), (2, 3)])  252 us
    ppermute x8, waiting for transfers between devices, sum_trees(): lax.ppermute(part, 'replica', [(0, 1), (3, 2)])  209 us
    ppermute x28, waiting for transfers between devices, send(): return lax.ppermute(block, 'slot', [(i, i ^ way) for i in range(count)])  159 us
    ppermute x12, waiting for transfers between devices, swap_near(): lax.ppermute(values, 'slot', [(i, i ^ (4 if i % 2 else 2)) for i in range...  113 us
    dot_general x16, matrix products, transpose_dot(): lax.dot_general(left, right, (((1,), (1,)), ((), ())), preferred_element_...  86.6 us
    dot_general x10, matrix products, rows_dot(): lax.dot_general(left, right, (((0,), (0,)), ((), ())), preferred_element_...  85.3 us
    dot_general x16, matrix products, dot(): return jnp.dot(left, right, preferred_element_type=jnp.float32)  83.6 us
    convert_element_type x35, other arithmetic, low(): return values.astype(jnp.bfloat16)  73.7 us
  transfers between devices with their start and end apart: 96, of which 31 were waited for; matrix products, arithmetic and copies ran while one was open for 28% of the time, Pallas kernels for 10%

profile of v1, /device:TPU:0, one launch (start us, length us, event | category | flops | bytes accessed | tf_op | source)
XLA Modules:
  0.0 1512.5 jit_solution(9217577572666316978)
XLA Ops:
  13.4 6.9 pack_weights.2
  26.6 26.7 %collective-permute-done.8 = bf16[608,2560]{1,0:T(8,128)(2,1)} collective-permute-done((bf16[608,2560]{1,0:T(8,128)(2,1)}, bf16[608,2560]{1,0:T(8,128)(2,1)}, u32[]{:S(2)}, u32[]{:S(2)}) %collective-permute-start.8) | collective-permute-done | bytes 3112992 | tf_op jit(solution)/shard_map/ppermute | solution.py:544
  58.1 15.7 %pack_weights.3 = (bf16[320,1792]{1,0:T(8,128)(2,1)S(1)}, bf16[320,1792]{1,0:T(8,128)(2,1)S(1)}, bf16[320,1792]{1,0:T(8,128)(2,1)S(1)}, bf16[320,1792]{1,0:T(8,1...) custom-call(s32[1]{0:T(128)} %bitcast.4.me, ...), custom_call_target="tpu_custom_call" | custom-call | tf_op jit(solution)/shard_map/pack_weights/pallas_call | solution.py:384
  81.6 17.5 %collective-permute-done.5.refs_5_ = bf16[320,512]{1,0:T(8,128)(2,1)S(1)} collective-permute-done((bf16[320,512]{1,0:T(8,128)(2,1)S(1)}, bf16[320,512]{1,0:T(8,128)(2,1)S(1)}, u32[]{:S(2)}, u32[]{:S(2)}) %collective-permute-start.5) | collective-permute-done | bytes 327712 | tf_op jit(solution)/shard_map/ppermute | solution.py:582
  107.4 4.7 fusion.95
  123.3 5.0 fusion.91
  131.3 39.6 %tree_forward.1 = (bf16[8,304,320]{2,1,0:T(8,128)(2,1)S(1)}, bf16[9216,128]{1,0:T(8,128)(2,1)}, bf16[2304,128]{1,0:T(8,128)(2,1)S(1)}, bf16[2304,128]{1,0:T(8,128)(2,1)S(1)}, f32[18,1,512]{2,1,0:T(1,128)S(1)}) custom-call(s32[18]{0:T(128)S(1)} %pad_add_fusion.starts, s32[13]{0:T(128)S(1)} %bitcast.99, s32[8]{0:T(128)S(1)} %fusion.109.order, ...), custom_call_target="tpu_custom_call" | custom-call | tf_op jit(solution)/shard_map/tree_forward/pallas_call | solution.py:299
  182.7 72.0 %collective-permute-done.23.refs_5_ = bf16[320,1792]{1,0:T(8,128)(2,1)S(1)} collective-permute-done((bf16[320,1792]{1,0:T(8,128)(2,1)S(1)}, bf16[320,1792]{1,0:T(8,128)(2,1)S(1)}, u32[]{:S(2)}, u32[]{:S(2)}) %collective-permute-start.23) | collective-permute-done | bytes 1146912 | tf_op jit(solution)/shard_map/ppermute | solution.py:582
  257.0 6.0 assemble_weights.3.refs_1_
  276.2 21.5 %collective-permute-done.14 = bf16[304,2560]{1,0:T(8,128)(2,1)S(1)} collective-permute-done((bf16[304,2560]{1,0:T(8,128)(2,1)S(1)}, bf16[304,2560]{1,0:T(8,128)(2,1)S(1)}, u32[]{:S(2)}, u32[]{:S(2)}) %collective-permute-start.14) | collective-permute-done | bytes 1556512 | tf_op jit(solution)/shard_map/ppermute | solution.py:548
  306.6 28.7 %collective-permute-done.37 = bf16[608,2560]{1,0:T(8,128)(2,1)} collective-permute-done((bf16[608,2560]{1,0:T(8,128)(2,1)}, bf16[608,2560]{1,0:T(8,128)(2,1)}, u32[]{:S(2)}, u32[]{:S(2)}) %collective-permute-start.37) | collective-permute-done | bytes 3112992 | tf_op jit(solution)/shard_map/ppermute | solution.py:544
  337.8 25.8 %collective-permute-done.15 = bf16[304,2560]{1,0:T(8,128)(2,1)} collective-permute-done((bf16[304,2560]{1,0:T(8,128)(2,1)}, bf16[304,2560]{1,0:T(8,128)(2,1)}, u32[]{:S(2)}, u32[]{:S(2)}) %collective-permute-start.15) | collective-permute-done | bytes 1556512 | tf_op jit(solution)/shard_map/ppermute | solution.py:544
  378.4 8.3 fusion.125
  386.7 8.3 multiply_convert_fusion.12
  396.7 7.1 convolution_convert_fusion.4
  403.8 8.5 convolution_convert_fusion.12
  417.6 7.3 fusion.130
  426.8 8.6 multiply_convert_fusion.10
  437.0 8.7 convolution_convert_fusion.11
  445.8 9.2 fusion.52
  454.9 8.1 multiply_convert_fusion.6
  463.0 7.7 convolution_convert_fusion.9
  472.5 5.9 convolution_convert_fusion.1
  480.5 7.5 fusion.131
  488.0 8.3 multiply_convert_fusion.8
  502.1 37.7 %convolution_convert_fusion = bf16[2560,1792]{1,0:T(8,128)(2,1)} fusion(bf16[2432,2560]{1,0:T(8,128)(2,1)} %constant_dynamic-update-slice_fusion.4, bf16[608,896]{1,0:T(8,128)(2,1)} %get-tuple-element.100, bf16[608,896]{1,0:T(8,128)(2,1)} %get-tuple-element.99, bf16[608,896]{1,0:T(8,128)(2,1)} %get-tuple-element.106, ...), kind=kOutput, calls=%fused_computation.9 | convolution fusion | flops 22388015104 | bytes 30343168 | tf_op jit(solution)/shard_map/dot_general | solution.py:519
  539.8 7.4 constant_dynamic-slice_fusion.2
  547.2 4.9 collective-permute-start.88
  552.1 17.5 %fusion = bf16[896,2560]{1,0:T(8,128)(2,1)} fusion(bf16[608,2560]{1,0:T(8,128)(2,1)} %copy-done.76, bf16[608,2560]{1,0:T(8,128)(2,1)} %copy-done.77, bf16[608,2560]{1,0:T(8,128)(2,1)} %copy-done.75, bf16[608,2560]{1,0:T(8,128)(2,1)} %copy-done.74, bf16[608,896]{1,0:T(8,128)(2,1)} %copy-done.129, bf16[608,896]{1,0:T(8,128)(2,1)} %get-tuple-element.110, ...), kind=kOutput, calls=%fused_computation.1 | convolution fusion | flops 11224088576 | bytes 21397504 | tf_op jit(solution)/shard_map/dot_general | solution.py:519
  569.7 10.3 convolution_convert_fusion.10
  581.7 7.3 convolution_convert_fusion.2
  601.2 5.8 collective-permute-start.74
  610.0 40.2 %collective-permute-done.83 = bf16[640,1792]{1,0:T(8,128)(2,1)S(1)} collective-permute-done((bf16[640,1792]{1,0:T(8,128)(2,1)S(1)}, bf16[640,1792]{1,0:T(8,128)(2,1)S(1)}, u32[]{:S(2)}, u32[]{:S(2)}) %collective-permute-start.83) | collective-permute-done | bytes 2293792 | tf_op jit(solution)/shard_map/ppermute | solution.py:591
  651.8 47.6 %collective-permute-done.78 = bf16[640,1792]{1,0:T(8,128)(2,1)S(1)} collective-permute-done((bf16[640,1792]{1,0:T(8,128)(2,1)S(1)}, bf16[640,1792]{1,0:T(8,128)(2,1)S(1)}, u32[]{:S(2)}, u32[]{:S(2)}) %collective-permute-start.78) | collective-permute-done | bytes 2293792 | tf_op jit(solution)/shard_map/ppermute | solution.py:591
  704.7 5.1 add_convert_fusion.4
  712.5 16.6 %collective-permute-done.32 = bf16[304,2560]{1,0:T(8,128)(2,1)} collective-permute-done((bf16[304,2560]{1,0:T(8,128)(2,1)}, bf16[304,2560]{1,0:T(8,128)(2,1)}, u32[]{:S(2)}, u32[]{:S(2)}) %collective-permute-start.32) | collective-permute-done | bytes 1556512 | tf_op jit(solution)/shard_map/ppermute | solution.py:548
  736.0 15.0 collective-permute-done.45
  760.9 6.8 collective-permute-start.93
  767.6 16.7 %collective-permute-done.44 = bf16[304,2560]{1,0:T(8,128)(2,1)S(1)} collective-permute-done((bf16[304,2560]{1,0:T(8,128)(2,1)S(1)}, bf16[304,2560]{1,0:T(8,128)(2,1)S(1)}, u32[]{:S(2)}, u32[]{:S(2)}) %collective-permute-start.44) | collective-permute-done | bytes 1556512 | tf_op jit(solution)/shard_map/ppermute | solution.py:544
  795.4 5.3 fusion.126
  818.0 43.3 %collective-permute-done.93 = bf16[864,2560]{1,0:T(8,128)(2,1)} collective-permute-done((bf16[864,2560]{1,0:T(8,128)(2,1)}, bf16[864,2560]{1,0:T(8,128)(2,1)}, u32[]{:S(2)}, u32[]{:S(2)}) %collective-permute-start.93) | collective-permute-done | bytes 4423712 | tf_op jit(solution)/shard_map/ppermute | solution.py:591
  861.9 5.5 add_convert_fusion.1
  870.1 68.8 %collective-permute-done.85 = bf16[640,1792]{1,0:T(8,128)(2,1)} collective-permute-done((bf16[640,1792]{1,0:T(8,128)(2,1)}, bf16[640,1792]{1,0:T(8,128)(2,1)}, u32[]{:S(2)}, u32[]{:S(2)}) %collective-permute-start.85) | collective-permute-done | bytes 2293792 | tf_op jit(solution)/shard_map/ppermute | solution.py:593
  950.5 39.5 %collective-permute-done.80 = bf16[640,1792]{1,0:T(8,128)(2,1)} collective-permute-done((bf16[640,1792]{1,0:T(8,128)(2,1)}, bf16[640,1792]{1,0:T(8,128)(2,1)}, u32[]{:S(2)}, u32[]{:S(2)}) %collective-permute-start.80) | collective-permute-done | bytes 2293792 | tf_op jit(solution)/shard_map/ppermute | solution.py:593
  991.0 48.2 %collective-permute-done.76 = bf16[640,1792]{1,0:T(8,128)(2,1)} collective-permute-done((bf16[640,1792]{1,0:T(8,128)(2,1)}, bf16[640,1792]{1,0:T(8,128)(2,1)}, u32[]{:S(2)}, u32[]{:S(2)}) %collective-permute-start.76) | collective-permute-done | bytes 2293792 | tf_op jit(solution)/shard_map/ppermute | solution.py:593
  1047.2 18.9 %collective-permute-done.87.refs_5_ = bf16[320,1792]{1,0:T(8,128)(2,1)S(1)} collective-permute-done((bf16[320,1792]{1,0:T(8,128)(2,1)S(1)}, bf16[320,1792]{1,0:T(8,128)(2,1)S(1)}, u32[]{:S(2)}, u32[]{:S(2)}) %collective-permute-start.87) | collective-permute-done | bytes 1146912 | tf_op jit(solution)/shard_map/ppermute | solution.py:582
  1071.6 19.8 %collective-permute-done.86.refs_4_ = bf16[320,1792]{1,0:T(8,128)(2,1)} collective-permute-done((bf16[320,1792]{1,0:T(8,128)(2,1)}, bf16[320,1792]{1,0:T(8,128)(2,1)}, u32[]{:S(2)}, u32[]{:S(2)}) %collective-permute-start.86) | collective-permute-done | bytes 1146912 | tf_op jit(solution)/shard_map/ppermute | solution.py:582
  1094.6 5.0 collective-permute-done.81.refs_2_
  1099.6 18.0 %spread_gradients.3 = (f32[320,6912]{1,0:T(8,128)}, f32[320,6912]{1,0:T(8,128)}, f32[320,1]{1,0:T(8,128)}) custom-call(s32[1]{0:T(128)} %bitcast.4.me, bf16[320,1792]{1,0:T(8,128)(2,1)} %get-tuple-element.125.refs_0_, bf16[320,1792]{1,0:T(8,128)(2,1)} %collective-permute-done.77.refs_1_, bf16[320,1792]{1,0:T(8,128)(2,1)} %collective-permute-done.81.refs_2_, ...), custom_call_target="tpu_custom_call" | custom-call | tf_op jit(solution)/shard_map/spread_gradients/pallas_call | solution.py:476
  1119.4 6.8 add_convert_fusion
  1155.7 50.1 %tree_backward.1 = bf16[8,304,512]{2,1,0:T(8,128)(2,1)} custom-call(s32[18]{0:T(128)} %copy-done.24, s32[13]{0:T(128)} %bitcast.98, s32[8]{0:T(128)} %copy-done.23, bf16[8,304,320]{2,1,0:T(8,128)(2,1)} %bitcast.110, bf16[9216,128]{1,0:T(8,128)(2,1)} %get-tuple-element.76.q_keep, bf16[2304,128]{1,0:T(8,128)(2,1)} %copy-done.13, bf16[2304,128]{1,0:T(8,128)(2,1)} %copy-done.14, ...), custom_call_target="tpu_custom_call" | custom-call | tf_op jit(solution)/shard_map/tree_backward/pallas_call | solution.py:327
  1215.5 4.8 fusion.97
  1220.3 5.3 add_convert_fusion.6
  1225.8 6.8 collective-permute-start.64
  1246.5 14.9 collective-permute-done.64
  1261.8 62.4 %collective-permute-done.58 = bf16[1280,512]{1,0:T(8,128)(2,1)S(1)} collective-permute-done((bf16[1280,512]{1,0:T(8,128)(2,1)S(1)}, bf16[1280,512]{1,0:T(8,128)(2,1)S(1)}, u32[]{:S(2)}, u32[]{:S(2)}) %collective-permute-start.58) | collective-permute-done | bytes 1310752 | tf_op jit(solution)/shard_map/ppermute | solution.py:591
  1333.4 13.5 collective-permute-done.54
  1348.9 70.4 %collective-permute-done.66 = bf16[1280,512]{1,0:T(8,128)(2,1)S(1)} collective-permute-done((bf16[1280,512]{1,0:T(8,128)(2,1)S(1)}, bf16[1280,512]{1,0:T(8,128)(2,1)S(1)}, u32[]{:S(2)}, u32[]{:S(2)}) %collective-permute-start.66) | collective-permute-done | bytes 1310752 | tf_op jit(solution)/shard_map/ppermute | solution.py:593
  1419.3 24.8 %collective-permute-done.60 = bf16[1280,512]{1,0:T(8,128)(2,1)S(1)} collective-permute-done((bf16[1280,512]{1,0:T(8,128)(2,1)S(1)}, bf16[1280,512]{1,0:T(8,128)(2,1)S(1)}, u32[]{:S(2)}, u32[]{:S(2)}) %collective-permute-start.60) | collective-permute-done | bytes 1310752 | tf_op jit(solution)/shard_map/ppermute | solution.py:593
  1462.5 5.5 collective-permute-done.68.refs_5_
  1469.4 5.8 collective-permute-done.67.refs_4_
  1475.7 6.4 select_convert_fusion
  1482.2 8.9 collective-permute-done.62.refs_2_
  1491.9 7.3 spread_gradients.2
  (593 shorter events, 331.4 us)
Async XLA Ops:
  8.3 45.1 %collective-permute-start.8 = (bf16[608,2560]{1,0:T(8,128)(2,1)}, bf16[608,2560]{1,0:T(8,128)(2,1)}, u32[]{:S(2)}, u32[]{:S(2)}) collective-permute-start(bf16[608,2560]{1,0:T(8,128)(2,1)} %pad_maximum_fusion.1), channel_id=1, source_target_pairs={{0,8},{4,20},{8,0},{12,28},{16,24},{20,4},{24,16},{28,12},{1,9},{5... | collective-permute-start | bytes 9338888 | tf_op jit(solution)/shard_map/ppermute | solution.py:544
  23.2 53.2 %collective-permute-start.1 = (bf16[320,512]{1,0:T(8,128)(2,1)}, bf16[320,512]{1,0:T(8,128)(2,1)S(1)}, u32[]{:S(2)}, u32[]{:S(2)}) collective-permute-start(bf16[320,512]{1,0:T(8,128)(2,1)} %get-tuple-element.50), channel_id=1, source_target_pairs={{0,4},{4,0},{8,12},{12,8},{16,20},{20,16},{24,28},{28,24},{1,5},{5... | collective-permute-start | bytes 983048 | tf_op jit(solution)/shard_map/ppermute | solution.py:582
  23.2 53.3 %collective-permute-start.2 = (bf16[320,512]{1,0:T(8,128)(2,1)}, bf16[320,512]{1,0:T(8,128)(2,1)S(1)}, u32[]{:S(2)}, u32[]{:S(2)}) collective-permute-start(bf16[320,512]{1,0:T(8,128)(2,1)} %get-tuple-element.51), channel_id=1, source_target_pairs={{0,8},{4,12},{8,0},{12,4},{16,24},{20,28},{24,16},{28,20},{1,9},{5... | collective-permute-start | bytes 983048 | tf_op jit(solution)/shard_map/ppermute | solution.py:582
  24.5 54.1 %collective-permute-start.3 = (bf16[320,512]{1,0:T(8,128)(2,1)}, bf16[320,512]{1,0:T(8,128)(2,1)S(1)}, u32[]{:S(2)}, u32[]{:S(2)}) collective-permute-start(bf16[320,512]{1,0:T(8,128)(2,1)} %get-tuple-element.52), channel_id=1, source_target_pairs={{0,12},{4,8},{8,4},{12,0},{16,28},{20,24},{24,20},{28,16},{1,13},{... | collective-permute-start | bytes 983048 | tf_op jit(solution)/shard_map/ppermute | solution.py:582
  25.0 56.6 %collective-permute-start.4 = (bf16[320,512]{1,0:T(8,128)(2,1)}, bf16[320,512]{1,0:T(8,128)(2,1)}, u32[]{:S(2)}, u32[]{:S(2)}) collective-permute-start(bf16[320,512]{1,0:T(8,128)(2,1)} %get-tuple-element.53), channel_id=1, source_target_pairs={{0,16},{4,20},{8,24},{12,28},{16,0},{20,4},{24,8},{28,12},{1,17},{... | collective-permute-start | bytes 983048 | tf_op jit(solution)/shard_map/ppermute | solution.py:582
  56.0 45.4 %collective-permute-start.10 = (bf16[304,2560]{1,0:T(8,128)(2,1)}, bf16[304,2560]{1,0:T(8,128)(2,1)}, u32[]{:S(2)}, u32[]{:S(2)}) collective-permute-start(bf16[304,2560]{1,0:T(8,128)(2,1)} %slice.179), channel_id=1, source_target_pairs={{0,16},{4,12},{8,24},{12,4},{16,0},{20,28},{24,8},{28,20},{1,17},{... | collective-permute-start | bytes 4669448 | tf_op jit(solution)/shard_map/ppermute | solution.py:548
  119.7 58.0 %collective-permute-start.19 = (bf16[320,1792]{1,0:T(8,128)(2,1)}, bf16[320,1792]{1,0:T(8,128)(2,1)S(1)}, u32[]{:S(2)}, u32[]{:S(2)}) collective-permute-start(bf16[320,1792]{1,0:T(8,128)(2,1)} %get-tuple-element.69), channel_id=1, source_target_pairs={{0,4},{4,0},{8,12},{12,8},{16,20},{20,16},{24,28},{28,24},{1,5},{5... | collective-permute-start | bytes 3440648 | tf_op jit(solution)/shard_map/ppermute | solution.py:582
  119.8 58.4 %collective-permute-start.20 = (bf16[320,1792]{1,0:T(8,128)(2,1)}, bf16[320,1792]{1,0:T(8,128)(2,1)S(1)}, u32[]{:S(2)}, u32[]{:S(2)}) collective-permute-start(bf16[320,1792]{1,0:T(8,128)(2,1)} %get-tuple-element.70), channel_id=1, source_target_pairs={{0,8},{4,12},{8,0},{12,4},{16,24},{20,28},{24,16},{28,20},{1,9},{5... | collective-permute-start | bytes 3440648 | tf_op jit(solution)/shard_map/ppermute | solution.py:582
  121.8 57.0 %collective-permute-start.21 = (bf16[320,1792]{1,0:T(8,128)(2,1)}, bf16[320,1792]{1,0:T(8,128)(2,1)S(1)}, u32[]{:S(2)}, u32[]{:S(2)}) collective-permute-start(bf16[320,1792]{1,0:T(8,128)(2,1)} %get-tuple-element.71), channel_id=1, source_target_pairs={{0,12},{4,8},{8,4},{12,0},{16,28},{20,24},{24,20},{28,16},{1,13},{... | collective-permute-start | bytes 3440648 | tf_op jit(solution)/shard_map/ppermute | solution.py:582
  121.9 59.2 %collective-permute-start.22 = (bf16[320,1792]{1,0:T(8,128)(2,1)}, bf16[320,1792]{1,0:T(8,128)(2,1)S(1)}, u32[]{:S(2)}, u32[]{:S(2)}) collective-permute-start(bf16[320,1792]{1,0:T(8,128)(2,1)} %get-tuple-element.72), channel_id=1, source_target_pairs={{0,16},{4,20},{8,24},{12,28},{16,0},{20,4},{24,8},{28,12},{1,17},{... | collective-permute-start | bytes 3440648 | tf_op jit(solution)/shard_map/ppermute | solution.py:582
  174.5 91.9 %collective-permute-start.12 = (bf16[608,2560]{1,0:T(8,128)(2,1)}, bf16[608,2560]{1,0:T(8,128)(2,1)}, u32[]{:S(2)}, u32[]{:S(2)}) collective-permute-start(bf16[608,2560]{1,0:T(8,128)(2,1)} %convolution_convert_fusion.14), channel_id=1, source_target_pairs={{0,4},{4,0},{8,12},{12,8},{16,20},{20,16},{24,28},{28,24},{1,5},{5... | collective-permute-start | bytes 9338888 | tf_op jit(solution)/shard_map/ppermute | solution.py:540
  177.7 85.5 %collective-permute-start.13 = (bf16[304,2560]{1,0:T(8,128)(2,1)}, bf16[304,2560]{1,0:T(8,128)(2,1)}, u32[]{:S(2)}, u32[]{:S(2)}) collective-permute-start(bf16[304,2560]{1,0:T(8,128)(2,1)} %slice.183), channel_id=1, source_target_pairs={{0,4},{4,0},{8,12},{12,8},{16,20},{20,16},{24,28},{28,24},{1,5},{5... | collective-permute-start | bytes 4669448 | tf_op jit(solution)/shard_map/ppermute | solution.py:540
  178.2 76.5 %collective-permute-start.23 = (bf16[320,1792]{1,0:T(8,128)(2,1)S(1)}, bf16[320,1792]{1,0:T(8,128)(2,1)S(1)}, u32[]{:S(2)}, u32[]{:S(2)}) collective-permute-start(bf16[320,1792]{1,0:T(8,128)(2,1)S(1)} %copy-done.89), channel_id=1, source_target_pairs={{0,20},{4,16},{8,28},{12,24},{16,4},{20,0},{24,12},{28,8},{1,21},{... | collective-permute-start | bytes 3440648 | tf_op jit(solution)/shard_map/ppermute | solution.py:582
  178.8 75.8 %collective-permute-start.24 = (bf16[320,1792]{1,0:T(8,128)(2,1)S(1)}, bf16[320,1792]{1,0:T(8,128)(2,1)S(1)}, u32[]{:S(2)}, u32[]{:S(2)}) collective-permute-start(bf16[320,1792]{1,0:T(8,128)(2,1)S(1)} %copy-done.90), channel_id=1, source_target_pairs={{0,24},{4,28},{8,16},{12,20},{16,8},{20,12},{24,0},{28,4},{1,25},{... | collective-permute-start | bytes 3440648 | tf_op jit(solution)/shard_map/ppermute | solution.py:582
  181.1 73.6 %collective-permute-start.25 = (bf16[320,1792]{1,0:T(8,128)(2,1)S(1)}, bf16[320,1792]{1,0:T(8,128)(2,1)S(1)}, u32[]{:S(2)}, u32[]{:S(2)}) collective-permute-start(bf16[320,1792]{1,0:T(8,128)(2,1)S(1)} %copy-done.91), channel_id=1, source_target_pairs={{0,28},{4,24},{8,20},{12,16},{16,12},{20,8},{24,4},{28,0},{1,29},{... | collective-permute-start | bytes 3440648 | tf_op jit(solution)/shard_map/ppermute | solution.py:582
  265.4 32.2 %collective-permute-start.14 = (bf16[304,2560]{1,0:T(8,128)(2,1)S(1)}, bf16[304,2560]{1,0:T(8,128)(2,1)S(1)}, u32[]{:S(2)}, u32[]{:S(2)}) collective-permute-start(bf16[304,2560]{1,0:T(8,128)(2,1)S(1)} %add_convert_fusion.29), channel_id=1, source_target_pairs={{0,16},{4,12},{8,24},{12,4},{16,0},{20,28},{24,8},{28,20},{1,17},{... | collective-permute-start | bytes 4669448 | tf_op jit(solution)/shard_map/ppermute | solution.py:548
  275.8 59.4 %collective-permute-start.37 = (bf16[608,2560]{1,0:T(8,128)(2,1)}, bf16[608,2560]{1,0:T(8,128)(2,1)}, u32[]{:S(2)}, u32[]{:S(2)}) collective-permute-start(bf16[608,2560]{1,0:T(8,128)(2,1)} %pad_maximum_fusion.3), channel_id=1, source_target_pairs={{0,8},{4,20},{8,0},{12,28},{16,24},{20,4},{24,16},{28,12},{1,9},{5... | collective-permute-start | bytes 9338888 | tf_op jit(solution)/shard_map/ppermute | solution.py:544
  299.2 64.5 %collective-permute-start.15 = (bf16[304,2560]{1,0:T(8,128)(2,1)}, bf16[304,2560]{1,0:T(8,128)(2,1)}, u32[]{:S(2)}, u32[]{:S(2)}) collective-permute-start(bf16[304,2560]{1,0:T(8,128)(2,1)} %add_convert_fusion.28), channel_id=1, source_target_pairs={{0,8},{4,20},{8,0},{12,28},{16,24},{20,4},{24,16},{28,12},{1,9},{5... | collective-permute-start | bytes 4669448 | tf_op jit(solution)/shard_map/ppermute | solution.py:544
  303.8 59.8 %collective-permute-start.17 = (bf16[304,2560]{1,0:T(8,128)(2,1)}, bf16[304,2560]{1,0:T(8,128)(2,1)}, u32[]{:S(2)}, u32[]{:S(2)}) collective-permute-start(bf16[304,2560]{1,0:T(8,128)(2,1)} %add_convert_fusion.27), channel_id=1, source_target_pairs={{0,4},{4,0},{8,12},{12,8},{16,20},{20,16},{24,28},{28,24},{1,5},{5... | collective-permute-start | bytes 4669448 | tf_op jit(solution)/shard_map/ppermute | solution.py:540
  336.8 39.3 %collective-permute-start.40 = (bf16[304,2560]{1,0:T(8,128)(2,1)S(1)}, bf16[304,2560]{1,0:T(8,128)(2,1)S(1)}, u32[]{:S(2)}, u32[]{:S(2)}) collective-permute-start(bf16[304,2560]{1,0:T(8,128)(2,1)S(1)} %slice.203), channel_id=1, source_target_pairs={{0,16},{4,12},{8,24},{12,4},{16,0},{20,28},{24,8},{28,20},{1,17},{... | collective-permute-start | bytes 4669448 | tf_op jit(solution)/shard_map/ppermute | solution.py:548
  371.4 41.4 %collective-permute-start.38 = (bf16[608,2560]{1,0:T(8,128)(2,1)}, bf16[608,2560]{1,0:T(8,128)(2,1)}, u32[]{:S(2)}, u32[]{:S(2)}) collective-permute-start(bf16[608,2560]{1,0:T(8,128)(2,1)} %collective-permute-done.37), channel_id=1, source_target_pairs={{0,4},{4,0},{8,12},{12,8},{16,20},{20,16},{24,28},{28,24},{1,5},{5... | collective-permute-start | bytes 9338888 | tf_op jit(solution)/shard_map/ppermute | solution.py:540
  376.1 36.2 %collective-permute-start.41 = (bf16[304,2560]{1,0:T(8,128)(2,1)S(1)}, bf16[304,2560]{1,0:T(8,128)(2,1)S(1)}, u32[]{:S(2)}, u32[]{:S(2)}) collective-permute-start(bf16[304,2560]{1,0:T(8,128)(2,1)S(1)} %collective-permute-done.40), channel_id=1, source_target_pairs={{0,4},{4,0},{8,12},{12,8},{16,20},{20,16},{24,28},{28,24},{1,5},{5... | collective-permute-start | bytes 4669448 | tf_op jit(solution)/shard_map/ppermute | solution.py:540
  376.6 39.9 %collective-permute-start.26 = (bf16[608,2560]{1,0:T(8,128)(2,1)S(1)}, bf16[608,2560]{1,0:T(8,128)(2,1)S(1)}, u32[]{:S(2)}, u32[]{:S(2)}) collective-permute-start(bf16[608,2560]{1,0:T(8,128)(2,1)S(1)} %pad_maximum_fusion.2), channel_id=1, source_target_pairs={{0,8},{4,20},{8,0},{12,28},{16,24},{20,4},{24,16},{28,12},{1,9},{5... | collective-permute-start | bytes 9338888 | tf_op jit(solution)/shard_map/ppermute | solution.py:544
  417.6 62.4 %collective-permute-start.27 = (bf16[608,2560]{1,0:T(8,128)(2,1)S(1)}, bf16[608,2560]{1,0:T(8,128)(2,1)S(1)}, u32[]{:S(2)}, u32[]{:S(2)}) collective-permute-start(bf16[608,2560]{1,0:T(8,128)(2,1)S(1)} %collective-permute-done.26), channel_id=1, source_target_pairs={{0,4},{4,0},{8,12},{12,8},{16,20},{20,16},{24,28},{28,24},{1,5},{5... | collective-permute-start | bytes 9338888 | tf_op jit(solution)/shard_map/ppermute | solution.py:540
  472.0 121.5 %collective-permute-start.42 = (bf16[304,2560]{1,0:T(8,128)(2,1)}, bf16[304,2560]{1,0:T(8,128)(2,1)}, u32[]{:S(2)}, u32[]{:S(2)}) collective-permute-start(bf16[304,2560]{1,0:T(8,128)(2,1)} %slice.205), channel_id=1, source_target_pairs={{0,4},{4,0},{8,12},{12,8},{16,20},{20,16},{24,28},{28,24},{1,5},{5... | collective-permute-start | bytes 4669448 | tf_op jit(solution)/shard_map/ppermute | solution.py:540
  479.8 116.9 %collective-permute-start.31 = (bf16[304,2560]{1,0:T(8,128)(2,1)}, bf16[304,2560]{1,0:T(8,128)(2,1)}, u32[]{:S(2)}, u32[]{:S(2)}) collective-permute-start(bf16[304,2560]{1,0:T(8,128)(2,1)} %slice.198), channel_id=1, source_target_pairs={{0,4},{4,0},{8,12},{12,8},{16,20},{20,16},{24,28},{28,24},{1,5},{5... | collective-permute-start | bytes 4669448 | tf_op jit(solution)/shard_map/ppermute | solution.py:540
  547.2 54.0 %collective-permute-start.88 = (bf16[640,1792]{1,0:T(8,128)(2,1)}, bf16[640,1792]{1,0:T(8,128)(2,1)}, u32[]{:S(2)}, u32[]{:S(2)}) collective-permute-start(bf16[640,1792]{1,0:T(8,128)(2,1)} %get-tuple-element.95), channel_id=1, source_target_pairs={{0,1},{3,2},{4,5},{7,6},{8,9},{11,10},{12,13},{15,14},{16,17},{19,... | collective-permute-start | bytes 6881288 | tf_op jit(solution)/shard_map/ppermute | solution.py:591
  580.0 70.3 %collective-permute-start.83 = (bf16[640,1792]{1,0:T(8,128)(2,1)S(1)}, bf16[640,1792]{1,0:T(8,128)(2,1)S(1)}, u32[]{:S(2)}, u32[]{:S(2)}) collective-permute-start(bf16[640,1792]{1,0:T(8,128)(2,1)S(1)} %copy-done.45), channel_id=1, source_target_pairs={{0,1},{3,2},{4,5},{7,6},{8,9},{11,10},{12,13},{15,14},{16,17},{19,... | collective-permute-start | bytes 6881288 | tf_op jit(solution)/shard_map/ppermute | solution.py:591
  589.0 110.4 %collective-permute-start.78 = (bf16[640,1792]{1,0:T(8,128)(2,1)S(1)}, bf16[640,1792]{1,0:T(8,128)(2,1)S(1)}, u32[]{:S(2)}, u32[]{:S(2)}) collective-permute-start(bf16[640,1792]{1,0:T(8,128)(2,1)S(1)} %copy-done.44), channel_id=1, source_target_pairs={{0,1},{3,2},{4,5},{7,6},{8,9},{11,10},{12,13},{15,14},{16,17},{19,... | collective-permute-start | bytes 6881288 | tf_op jit(solution)/shard_map/ppermute | solution.py:591
  593.5 107.4 %collective-permute-start.28 = (bf16[608,2560]{1,0:T(8,128)(2,1)}, bf16[608,2560]{1,0:T(8,128)(2,1)S(1)}, u32[]{:S(2)}, u32[]{:S(2)}) collective-permute-start(bf16[608,2560]{1,0:T(8,128)(2,1)} %convolution_convert_fusion.2), channel_id=1, source_target_pairs={{0,4},{4,0},{8,12},{12,8},{16,20},{20,16},{24,28},{28,24},{1,5},{5... | collective-permute-start | bytes 9338888 | tf_op jit(solution)/shard_map/ppermute | solution.py:540
  596.6 113.2 %collective-permute-start.39 = (bf16[608,2560]{1,0:T(8,128)(2,1)}, bf16[608,2560]{1,0:T(8,128)(2,1)S(1)}, u32[]{:S(2)}, u32[]{:S(2)}) collective-permute-start(bf16[608,2560]{1,0:T(8,128)(2,1)} %convolution_convert_fusion.10), channel_id=1, source_target_pairs={{0,4},{4,0},{8,12},{12,8},{16,20},{20,16},{24,28},{28,24},{1,5},{5... | collective-permute-start | bytes 9338888 | tf_op jit(solution)/shard_map/ppermute | solution.py:540
  601.2 157.3 %collective-permute-start.74 = (bf16[640,1792]{1,0:T(8,128)(2,1)S(1)}, bf16[640,1792]{1,0:T(8,128)(2,1)}, u32[]{:S(2)}, u32[]{:S(2)}) collective-permute-start(bf16[640,1792]{1,0:T(8,128)(2,1)S(1)} %copy-done.43), channel_id=1, source_target_pairs={{0,1},{3,2},{4,5},{7,6},{8,9},{11,10},{12,13},{15,14},{16,17},{19,... | collective-permute-start | bytes 6881288 | tf_op jit(solution)/shard_map/ppermute | solution.py:591
  650.2 81.9 %collective-permute-start.43 = (bf16[304,2560]{1,0:T(8,128)(2,1)}, bf16[304,2560]{1,0:T(8,128)(2,1)}, u32[]{:S(2)}, u32[]{:S(2)}) collective-permute-start(bf16[304,2560]{1,0:T(8,128)(2,1)} %add_convert_fusion.22), channel_id=1, source_target_pairs={{0,16},{4,12},{8,24},{12,4},{16,0},{20,28},{24,8},{28,20},{1,17},{... | collective-permute-start | bytes 4669448 | tf_op jit(solution)/shard_map/ppermute | solution.py:548
  702.6 58.2 %collective-permute-start.89 = (bf16[640,1792]{1,0:T(8,128)(2,1)S(1)}, bf16[640,1792]{1,0:T(8,128)(2,1)}, u32[]{:S(2)}, u32[]{:S(2)}) collective-permute-start(bf16[640,1792]{1,0:T(8,128)(2,1)S(1)} %add_convert_fusion.8), channel_id=1, source_target_pairs={{1,2},{2,1},{5,6},{6,5},{9,10},{10,9},{13,14},{14,13},{17,18},{18,... | collective-permute-start | bytes 6881288 | tf_op jit(solution)/shard_map/ppermute | solution.py:592
  709.9 43.2 %collective-permute-start.34 = (bf16[304,2560]{1,0:T(8,128)(2,1)S(1)}, bf16[304,2560]{1,0:T(8,128)(2,1)}, u32[]{:S(2)}, u32[]{:S(2)}) collective-permute-start(bf16[304,2560]{1,0:T(8,128)(2,1)S(1)} %slice.200), channel_id=1, source_target_pairs={{0,8},{4,20},{8,0},{12,28},{16,24},{20,4},{24,16},{28,12},{1,9},{5... | collective-permute-start | bytes 4669448 | tf_op jit(solution)/shard_map/ppermute | solution.py:544
  732.1 58.6 %collective-permute-start.33 = (bf16[304,2560]{1,0:T(8,128)(2,1)}, bf16[304,2560]{1,0:T(8,128)(2,1)S(1)}, u32[]{:S(2)}, u32[]{:S(2)}) collective-permute-start(bf16[304,2560]{1,0:T(8,128)(2,1)} %add_convert_fusion.25), channel_id=1, source_target_pairs={{0,8},{4,20},{8,0},{12,28},{16,24},{20,4},{24,16},{28,12},{1,9},{5... | collective-permute-start | bytes 4669448 | tf_op jit(solution)/shard_map/ppermute | solution.py:544
  751.0 33.4 %collective-permute-start.44 = (bf16[304,2560]{1,0:T(8,128)(2,1)S(1)}, bf16[304,2560]{1,0:T(8,128)(2,1)S(1)}, u32[]{:S(2)}, u32[]{:S(2)}) collective-permute-start(bf16[304,2560]{1,0:T(8,128)(2,1)S(1)} %add_convert_fusion.21), channel_id=1, source_target_pairs={{0,8},{4,20},{8,0},{12,28},{16,24},{20,4},{24,16},{28,12},{1,9},{5... | collective-permute-start | bytes 4669448 | tf_op jit(solution)/shard_map/ppermute | solution.py:544
  753.1 34.4 %collective-permute-start.46 = (bf16[304,2560]{1,0:T(8,128)(2,1)}, bf16[304,2560]{1,0:T(8,128)(2,1)S(1)}, u32[]{:S(2)}, u32[]{:S(2)}) collective-permute-start(bf16[304,2560]{1,0:T(8,128)(2,1)} %add_convert_fusion.20), channel_id=1, source_target_pairs={{0,4},{4,0},{8,12},{12,8},{16,20},{20,16},{24,28},{28,24},{1,5},{5... | collective-permute-start | bytes 4669448 | tf_op jit(solution)/shard_map/ppermute | solution.py:540
  758.5 34.3 %collective-permute-start.35 = (bf16[304,2560]{1,0:T(8,128)(2,1)}, bf16[304,2560]{1,0:T(8,128)(2,1)S(1)}, u32[]{:S(2)}, u32[]{:S(2)}) collective-permute-start(bf16[304,2560]{1,0:T(8,128)(2,1)} %add_convert_fusion.24), channel_id=1, source_target_pairs={{0,4},{4,0},{8,12},{12,8},{16,20},{20,16},{24,28},{28,24},{1,5},{5... | collective-permute-start | bytes 4669448 | tf_op jit(solution)/shard_map/ppermute | solution.py:540
  760.9 100.5 %collective-permute-start.93 = (bf16[864,2560]{1,0:T(8,128)(2,1)}, bf16[864,2560]{1,0:T(8,128)(2,1)}, u32[]{:S(2)}, u32[]{:S(2)}) collective-permute-start(bf16[864,2560]{1,0:T(8,128)(2,1)} %slice.270), channel_id=1, source_target_pairs={{0,1},{3,2},{4,5},{7,6},{8,9},{11,10},{12,13},{15,14},{16,17},{19,... | collective-permute-start | bytes 13271048 | tf_op jit(solution)/shard_map/ppermute | solution.py:591
  794.0 73.5 %collective-permute-start.90 = (bf16[640,1792]{1,0:T(8,128)(2,1)S(1)}, bf16[640,1792]{1,0:T(8,128)(2,1)}, u32[]{:S(2)}, u32[]{:S(2)}) collective-permute-start(bf16[640,1792]{1,0:T(8,128)(2,1)S(1)} %add_convert_fusion.7), channel_id=1, source_target_pairs={{1,0},{2,3},{5,4},{6,7},{9,8},{10,11},{13,12},{14,15},{17,16},{18,... | collective-permute-start | bytes 6881288 | tf_op jit(solution)/shard_map/ppermute | solution.py:593
  804.9 134.0 %collective-permute-start.85 = (bf16[640,1792]{1,0:T(8,128)(2,1)}, bf16[640,1792]{1,0:T(8,128)(2,1)}, u32[]{:S(2)}, u32[]{:S(2)}) collective-permute-start(bf16[640,1792]{1,0:T(8,128)(2,1)} %add_convert_fusion.9), channel_id=1, source_target_pairs={{1,0},{2,3},{5,4},{6,7},{9,8},{10,11},{13,12},{14,15},{17,16},{18,... | collective-permute-start | bytes 6881288 | tf_op jit(solution)/shard_map/ppermute | solution.py:593
  809.9 180.1 %collective-permute-start.80 = (bf16[640,1792]{1,0:T(8,128)(2,1)}, bf16[640,1792]{1,0:T(8,128)(2,1)}, u32[]{:S(2)}, u32[]{:S(2)}) collective-permute-start(bf16[640,1792]{1,0:T(8,128)(2,1)} %add_convert_fusion.11), channel_id=1, source_target_pairs={{1,0},{2,3},{5,4},{6,7},{9,8},{10,11},{13,12},{14,15},{17,16},{18,... | collective-permute-start | bytes 6881288 | tf_op jit(solution)/shard_map/ppermute | solution.py:593
  814.9 224.2 %collective-permute-start.76 = (bf16[640,1792]{1,0:T(8,128)(2,1)}, bf16[640,1792]{1,0:T(8,128)(2,1)}, u32[]{:S(2)}, u32[]{:S(2)}) collective-permute-start(bf16[640,1792]{1,0:T(8,128)(2,1)} %add_convert_fusion.13), channel_id=1, source_target_pairs={{1,0},{2,3},{5,4},{6,7},{9,8},{10,11},{13,12},{14,15},{17,16},{18,... | collective-permute-start | bytes 6881288 | tf_op jit(solution)/shard_map/ppermute | solution.py:593
  861.3 206.4 %collective-permute-start.48 = (bf16[608,2560]{1,0:T(8,128)(2,1)}, bf16[608,2560]{1,0:T(8,128)(2,1)}, u32[]{:S(2)}, u32[]{:S(2)}) collective-permute-start(bf16[608,2560]{1,0:T(8,128)(2,1)} %pad_maximum_fusion.4), channel_id=1, source_target_pairs={{0,8},{4,20},{8,0},{12,28},{16,24},{20,4},{24,16},{28,12},{1,9},{5... | collective-permute-start | bytes 9338888 | tf_op jit(solution)/shard_map/ppermute | solution.py:544
  867.4 252.0 %collective-permute-start.94 = (bf16[864,2560]{1,0:T(8,128)(2,1)}, bf16[864,2560]{1,0:T(8,128)(2,1)}, u32[]{:S(2)}, u32[]{:S(2)}) collective-permute-start(bf16[864,2560]{1,0:T(8,128)(2,1)} %add_convert_fusion.1), channel_id=1, source_target_pairs={{1,2},{2,1},{5,6},{6,5},{9,10},{10,9},{13,14},{14,13},{17,18},{18,... | collective-permute-start | bytes 13271048 | tf_op jit(solution)/shard_map/ppermute | solution.py:592
  944.7 98.3 %collective-permute-start.92 = (bf16[320,1792]{1,0:T(8,128)(2,1)}, bf16[320,1792]{1,0:T(8,128)(2,1)}, u32[]{:S(2)}, u32[]{:S(2)}) collective-permute-start(bf16[320,1792]{1,0:T(8,128)(2,1)} %get-tuple-element.118), channel_id=1, source_target_pairs={{0,28},{4,24},{8,20},{12,16},{16,12},{20,8},{24,4},{28,0},{1,29},{... | collective-permute-start | bytes 3440648 | tf_op jit(solution)/shard_map/ppermute | solution.py:582
  990.0 57.2 %collective-permute-start.91 = (bf16[320,1792]{1,0:T(8,128)(2,1)S(1)}, bf16[320,1792]{1,0:T(8,128)(2,1)S(1)}, u32[]{:S(2)}, u32[]{:S(2)}) collective-permute-start(bf16[320,1792]{1,0:T(8,128)(2,1)S(1)} %copy-done.92), channel_id=1, source_target_pairs={{0,24},{4,28},{8,16},{12,20},{16,8},{20,12},{24,0},{28,4},{1,25},{... | collective-permute-start | bytes 3440648 | tf_op jit(solution)/shard_map/ppermute | solution.py:582
  1042.9 48.5 %collective-permute-start.86 = (bf16[320,1792]{1,0:T(8,128)(2,1)}, bf16[320,1792]{1,0:T(8,128)(2,1)}, u32[]{:S(2)}, u32[]{:S(2)}) collective-permute-start(bf16[320,1792]{1,0:T(8,128)(2,1)} %get-tuple-element.121), channel_id=1, source_target_pairs={{0,16},{4,20},{8,24},{12,28},{16,0},{20,4},{24,8},{28,12},{1,17},{... | collective-permute-start | bytes 3440648 | tf_op jit(solution)/shard_map/ppermute | solution.py:582
  1047.2 47.4 %collective-permute-start.82 = (bf16[320,1792]{1,0:T(8,128)(2,1)}, bf16[320,1792]{1,0:T(8,128)(2,1)}, u32[]{:S(2)}, u32[]{:S(2)}) collective-permute-start(bf16[320,1792]{1,0:T(8,128)(2,1)} %get-tuple-element.122), channel_id=1, source_target_pairs={{0,12},{4,8},{8,4},{12,0},{16,28},{20,24},{24,20},{28,16},{1,13},{... | collective-permute-start | bytes 3440648 | tf_op jit(solution)/shard_map/ppermute | solution.py:582
  1067.2 32.3 %collective-permute-start.81 = (bf16[320,1792]{1,0:T(8,128)(2,1)}, bf16[320,1792]{1,0:T(8,128)(2,1)}, u32[]{:S(2)}, u32[]{:S(2)}) collective-permute-start(bf16[320,1792]{1,0:T(8,128)(2,1)} %get-tuple-element.123), channel_id=1, source_target_pairs={{0,8},{4,12},{8,0},{12,4},{16,24},{20,28},{24,16},{28,20},{1,9},{5... | collective-permute-start | bytes 3440648 | tf_op jit(solution)/shard_map/ppermute | solution.py:582
  1091.4 36.3 %collective-permute-start.50 = (bf16[304,2560]{1,0:T(8,128)(2,1)}, bf16[304,2560]{1,0:T(8,128)(2,1)}, u32[]{:S(2)}, u32[]{:S(2)}) collective-permute-start(bf16[304,2560]{1,0:T(8,128)(2,1)} %slice.208), channel_id=1, source_target_pairs={{0,16},{4,12},{8,24},{12,4},{16,0},{20,28},{24,8},{28,20},{1,17},{... | collective-permute-start | bytes 4669448 | tf_op jit(solution)/shard_map/ppermute | solution.py:548
  1126.2 323.1 %collective-permute-start.95 = (bf16[864,2560]{1,0:T(8,128)(2,1)}, bf16[864,2560]{1,0:T(8,128)(2,1)}, u32[]{:S(2)}, u32[]{:S(2)}) collective-permute-start(bf16[864,2560]{1,0:T(8,128)(2,1)} %add_convert_fusion), channel_id=1, source_target_pairs={{1,0},{2,3},{5,4},{6,7},{9,8},{10,11},{13,12},{14,15},{17,16},{18,... | collective-permute-start | bytes 13271048 | tf_op jit(solution)/shard_map/ppermute | solution.py:593
  1225.8 35.6 %collective-permute-start.64 = (bf16[1280,512]{1,0:T(8,128)(2,1)S(1)}, bf16[1280,512]{1,0:T(8,128)(2,1)S(1)}, u32[]{:S(2)}, u32[]{:S(2)}) collective-permute-start(bf16[1280,512]{1,0:T(8,128)(2,1)S(1)} %get-tuple-element.112), channel_id=1, source_target_pairs={{0,1},{3,2},{4,5},{7,6},{8,9},{11,10},{12,13},{15,14},{16,17},{19,... | collective-permute-start | bytes 3932168 | tf_op jit(solution)/shard_map/ppermute | solution.py:591
  1237.9 88.6 %collective-permute-start.71 = (bf16[320,2560]{1,0:T(8,128)(2,1)S(1)}, bf16[320,2560]{1,0:T(8,128)(2,1)S(1)}, u32[]{:S(2)}, u32[]{:S(2)}) collective-permute-start(bf16[320,2560]{1,0:T(8,128)(2,1)S(1)} %fusion.43), channel_id=1, source_target_pairs={{0,1},{3,2},{4,5},{7,6},{8,9},{11,10},{12,13},{15,14},{16,17},{19,... | collective-permute-start | bytes 4915208 | tf_op jit(solution)/shard_map/ppermute | solution.py:591
  1239.4 85.9 %collective-permute-start.53 = (bf16[304,2560]{1,0:T(8,128)(2,1)S(1)}, bf16[304,2560]{1,0:T(8,128)(2,1)S(1)}, u32[]{:S(2)}, u32[]{:S(2)}) collective-permute-start(bf16[304,2560]{1,0:T(8,128)(2,1)S(1)} %slice.212), channel_id=1, source_target_pairs={{0,4},{4,0},{8,12},{12,8},{16,20},{20,16},{24,28},{28,24},{1,5},{5... | collective-permute-start | bytes 4669448 | tf_op jit(solution)/shard_map/ppermute | solution.py:540
  1239.6 84.6 %collective-permute-start.58 = (bf16[1280,512]{1,0:T(8,128)(2,1)S(1)}, bf16[1280,512]{1,0:T(8,128)(2,1)S(1)}, u32[]{:S(2)}, u32[]{:S(2)}) collective-permute-start(bf16[1280,512]{1,0:T(8,128)(2,1)S(1)} %get-tuple-element.113), channel_id=1, source_target_pairs={{0,1},{3,2},{4,5},{7,6},{8,9},{11,10},{12,13},{15,14},{16,17},{19,... | collective-permute-start | bytes 3932168 | tf_op jit(solution)/shard_map/ppermute | solution.py:591
  1261.4 69.5 %collective-permute-start.52 = (bf16[608,2560]{1,0:T(8,128)(2,1)S(1)}, bf16[608,2560]{1,0:T(8,128)(2,1)S(1)}, u32[]{:S(2)}, u32[]{:S(2)}) collective-permute-start(bf16[608,2560]{1,0:T(8,128)(2,1)S(1)} %convolution_convert_fusion.6), channel_id=1, source_target_pairs={{0,4},{4,0},{8,12},{12,8},{16,20},{20,16},{24,28},{28,24},{1,5},{5... | collective-permute-start | bytes 9338888 | tf_op jit(solution)/shard_map/ppermute | solution.py:540
  1328.0 116.5 %collective-permute-start.72 = (bf16[320,2560]{1,0:T(8,128)(2,1)S(1)}, bf16[320,2560]{1,0:T(8,128)(2,1)S(1)}, u32[]{:S(2)}, u32[]{:S(2)}) collective-permute-start(bf16[320,2560]{1,0:T(8,128)(2,1)S(1)} %add_convert_fusion.16), channel_id=1, source_target_pairs={{1,2},{2,1},{5,6},{6,5},{9,10},{10,9},{13,14},{14,13},{17,18},{18,... | collective-permute-start | bytes 4915208 | tf_op jit(solution)/shard_map/ppermute | solution.py:592
  1329.2 90.1 %collective-permute-start.66 = (bf16[1280,512]{1,0:T(8,128)(2,1)S(1)}, bf16[1280,512]{1,0:T(8,128)(2,1)S(1)}, u32[]{:S(2)}, u32[]{:S(2)}) collective-permute-start(bf16[1280,512]{1,0:T(8,128)(2,1)S(1)} %add_convert_fusion.30), channel_id=1, source_target_pairs={{1,0},{2,3},{5,4},{6,7},{9,8},{10,11},{13,12},{14,15},{17,16},{18,... | collective-permute-start | bytes 3932168 | tf_op jit(solution)/shard_map/ppermute | solution.py:593
  1330.9 113.1 %collective-permute-start.60 = (bf16[1280,512]{1,0:T(8,128)(2,1)S(1)}, bf16[1280,512]{1,0:T(8,128)(2,1)S(1)}, u32[]{:S(2)}, u32[]{:S(2)}) collective-permute-start(bf16[1280,512]{1,0:T(8,128)(2,1)S(1)} %add_convert_fusion.32), channel_id=1, source_target_pairs={{1,0},{2,3},{5,4},{6,7},{9,8},{10,11},{13,12},{14,15},{17,16},{18,... | collective-permute-start | bytes 3932168 | tf_op jit(solution)/shard_map/ppermute | solution.py:593
  1346.8 109.7 %collective-permute-start.56 = (bf16[304,2560]{1,0:T(8,128)(2,1)S(1)}, bf16[304,2560]{1,0:T(8,128)(2,1)S(1)}, u32[]{:S(2)}, u32[]{:S(2)}) collective-permute-start(bf16[304,2560]{1,0:T(8,128)(2,1)S(1)} %slice.214), channel_id=1, source_target_pairs={{0,8},{4,20},{8,0},{12,28},{16,24},{20,4},{24,16},{28,12},{1,9},{5... | collective-permute-start | bytes 4669448 | tf_op jit(solution)/shard_map/ppermute | solution.py:544
  1446.1 54.8 %collective-permute-start.73 = (bf16[320,2560]{1,0:T(8,128)(2,1)}, bf16[320,2560]{1,0:T(8,128)(2,1)}, u32[]{:S(2)}, u32[]{:S(2)}) collective-permute-start(bf16[320,2560]{1,0:T(8,128)(2,1)} %add_convert_fusion.15), channel_id=1, source_target_pairs={{1,0},{2,3},{5,4},{6,7},{9,8},{10,11},{13,12},{14,15},{17,16},{18,... | collective-permute-start | bytes 4915208 | tf_op jit(solution)/shard_map/ppermute | solution.py:593
  1459.8 44.6 %collective-permute-start.55 = (bf16[304,2560]{1,0:T(8,128)(2,1)}, bf16[304,2560]{1,0:T(8,128)(2,1)}, u32[]{:S(2)}, u32[]{:S(2)}) collective-permute-start(bf16[304,2560]{1,0:T(8,128)(2,1)} %add_convert_fusion.18), channel_id=1, source_target_pairs={{0,8},{4,20},{8,0},{12,28},{16,24},{20,4},{24,16},{28,12},{1,9},{5... | collective-permute-start | bytes 4669448 | tf_op jit(solution)/shard_map/ppermute | solution.py:544
  (173 other events, 3276.6 us)

commit v2 on v1

--- a/solution.py
+++ b/solution.py
@@ -14,6 +14,7 @@
 SEG_TILES = TRUNK // TILE + SEGS - 1
 TRUNK_TILES = TRUNK // TILE
 LANES = 128
+BLOCK = 256
 epsilon = 1e-05
 masked_score = -1e30
 rope_theta = 10000.0
@@ -286,6 +287,111 @@
         grads[i] = rows[:, : grads.shape[2]].astype(jnp.bfloat16)
 
 
+def dense_kernel(
+    chunk, held, order, x_far, down_far, live_far, w_far, lower_far, *refs
+):
+    refs = refs[held:]
+    whole, out_far, back_far, refs = refs[:4], refs[4], refs[5], refs[6:]
+    x, down, live, w, lower, both, upward, active, masked, hidden, back, out, sems = refs
+    wide = lower.shape[0]
+    blocks = order.shape[0] // 4
+    block = x.shape[0] // blocks
+    inside = [pl.ds(i * block, block) for i in range(blocks)]
+    rows = [
+        pl.ds(pl.multiple_of(order[chunk * blocks + i] * block, 16), block) for i in range(blocks)
+    ]
+
+    def copies(near, far, first, inward):
+        ends = [(near.at[a], far.at[b]) for a, b in zip(inside, rows)]
+        return [
+            pltpu.make_async_copy(*(reversed(pair) if inward else pair), sems.at[first + i])
+            for i, pair in enumerate(ends)
+        ]
+
+    arrivals = copies(live, live_far, 0, True)
+    arrivals.append(pltpu.make_async_copy(down_far, down, sems.at[2]))
+    arrivals.append(pltpu.make_async_copy(lower_far, lower, sems.at[3]))
+    later = [pltpu.make_async_copy(x_far, x, sems.at[4]), pltpu.make_async_copy(w_far, w, sems.at[5])]
+    for copy in arrivals + later:
+        copy.start()
+    for copy in arrivals:
+        copy.wait()
+    upward[...] = nt(down[...], lower[...])
+    for copy in later:
+        copy.wait()
+
+    @pl.loop(0, 2 * wide // BLOCK)
+    def _(t):
+        at = tile_rows(t, BLOCK)
+        both[:, at] = nn(x[...], w[:, at])
+
+    @pl.loop(0, x.shape[0] // 32)
+    def _(i):
+        at = tile_rows(i, 32)
+        gate, up = both[at, :wide], both[at, wide:]
+        alive = live[at, :1]
+        grad = upward[at, :] * alive
+        sigmoid = 1.0 / (1.0 + jnp.exp(-gate))
+        silu = gate * sigmoid
+        active_now = silu * up
+        active[at, :] = active_now.astype(jnp.bfloat16)
+        masked[at, :] = (active_now * alive).astype(jnp.bfloat16)
+        gate_grad = grad * up * sigmoid * (1.0 + gate * (1.0 - sigmoid))
+        hidden[at, :wide] = gate_grad.astype(jnp.bfloat16)
+        hidden[at, wide:] = (grad * silu).astype(jnp.bfloat16)
+
+    leaving = []
+    for index, near in enumerate((x, down, masked, hidden)):
+        leaving += copies(near, whole[index], 6 + 2 * index, False)
+    for copy in leaving:
+        copy.start()
+    half = x.shape[1] // 2
+    for first in (0, half):
+        at = pl.ds(first, half)
+        back[:, at] = nt(hidden[...], w[at, :]).astype(jnp.bfloat16)
+    last = [pltpu.make_async_copy(back, back_far, sems.at[14])]
+    last[0].start()
+    for first in (0, half):
+        at = pl.ds(first, half)
+        out[:, at] = nn(active[...], lower[:, at]).astype(jnp.bfloat16)
+    last.append(pltpu.make_async_copy(out, out_far, sems.at[15]))
+    last[1].start()
+    for copy in leaving + last:
+        copy.wait()
+
+
+def dense(chunk, order, x, down, live, w, lower, held):
+    rows, features = x.shape
+    wide = lower.shape[0]
+    slots = 4 * rows
+    low_of = lambda *shape: jax.ShapeDtypeStruct(shape, jnp.bfloat16)
+    far = pl.BlockSpec(memory_space=pl.ANY)
+    keep = lambda *shape: pltpu.VMEM(shape, jnp.bfloat16)
+    aliases = {6 + i: i for i in range(len(held))}
+    results = pl.pallas_call(
+        functools.partial(dense_kernel, chunk, len(held)),
+        out_shape=(
+            low_of(slots, features), low_of(slots, features), low_of(slots, wide),
+            low_of(slots, 2 * wide), low_of(rows, features), low_of(rows, features),
+        ),
+        in_specs=[SMEM] + [far] * (5 + len(held)),
+        out_specs=(far,) * 6,
+        scratch_shapes=[
+            keep(rows, features), keep(rows, features), pltpu.VMEM((rows, LANES), jnp.float32),
+            keep(features, 2 * wide), keep(wide, features),
+            pltpu.VMEM((rows, 2 * wide), jnp.float32), pltpu.VMEM((rows, wide), jnp.float32),
+            keep(rows, wide), keep(rows, wide), keep(rows, 2 * wide),
+            keep(rows, features), keep(rows, features),
+            pltpu.SemaphoreType.DMA((16,)),
+        ],
+        input_output_aliases=aliases,
+        compiler_params=pltpu.CompilerParams(vmem_limit_bytes=60 * 2**20),
+        name="dense",
+    )(order, x, down, live, w, lower, *held)
+    return results[5], results[4], results[:4]
+
+
+LITTLE = pl.CostEstimate(flops=1, bytes_accessed=1, transcendentals=0)
 SMEM = pl.BlockSpec(memory_space=pltpu.SMEM)
 VMEM = pl.BlockSpec(memory_space=pltpu.VMEM)
 
@@ -339,6 +445,7 @@
             pltpu.VMEM((slot_count + 8, wide), jnp.float32),
         ],
         compiler_params=pltpu.CompilerParams(vmem_limit_bytes=56 * 2**20),
+        cost_estimate=LITTLE,
         name="tree_backward",
     )(starts, parents, order, attended_grad, *kept, tables)
 
@@ -358,47 +465,54 @@
     return pltpu.roll(values, lax.rem(at - shift + reach, reach), 1)[:, :wide]
 
 
-def pack_kernel(places, extras, step, me, *refs):
+def pack_kernel(places, extras, step, spot, *refs):
     sources, gains = refs[: len(places)], refs[len(places) : len(places) + extras]
-    blocks = refs[len(places) + extras :]
-    count = len(blocks)
-    wide = blocks[0].shape[1]
+    pairs = refs[len(places) + extras :]
+    half, wide = pairs[0].shape[1:]
     extra_at = sum(size for size, _ in places)
 
-    @pl.loop(0, blocks[0].shape[0] // step)
+    @pl.loop(0, half // step)
     def _(i):
-        rows = pl.ds(pl.multiple_of(i * step, step), step)
+        rows = pl.ds(pl.multiple_of(spot[1] * half + i * step, step), step)
+        there = pl.ds(pl.multiple_of(i * step, step), step)
         lane = lax.broadcasted_iota(jnp.int32, (step, wide), 1)
-        for way in range(count):
+        for way in range(2 * len(pairs)):
             total = None
             for ref, (size, at) in zip(sources, places):
-                part = window(ref, rows, (me[0] ^ way) * size, size, wide, at)
+                part = window(ref, rows, (spot[0] ^ way) * size, size, wide, at)
                 total = part if total is None else total + part
             for index, gain in enumerate(gains):
                 total = jnp.where(lane == extra_at + index, gain[rows, :].astype(jnp.float32), total)
-            blocks[way][rows, :] = total.astype(jnp.bfloat16)
-
-
-def pack(weights, gains, me, places, wide, count):
-    rows = weights[0].shape[0]
+            pairs[way // 2][way % 2, there, :] = total.astype(jnp.bfloat16)
+
+
+def pack(weights, gains, spot, places, wide, count, share):
+    half = weights[0].shape[0] // share
     return pl.pallas_call(
         functools.partial(pack_kernel, places, len(gains), 16),
-        out_shape=(jax.ShapeDtypeStruct((rows, wide), jnp.bfloat16),) * count,
+        out_shape=(jax.ShapeDtypeStruct((2, half, wide), jnp.bfloat16),) * (count // 2),
         in_specs=[SMEM] + [VMEM] * (len(weights) + len(gains)),
-        out_specs=(VMEM,) * count,
+        out_specs=(VMEM,) * (count // 2),
         compiler_params=pltpu.CompilerParams(vmem_limit_bytes=48 * 2**20),
         name="pack_weights",
-    )(me[None], *weights, *[gain[:, None] for gain in gains])
-
-
-def assemble_kernel(count, extra_at, me, *refs):
-    blocks, whole = refs[:count], refs[count]
-    rows = blocks[0].shape[0]
-    for way, block in enumerate(blocks):
-        at = pl.ds(pl.multiple_of((me[0] ^ way) * rows, 16), rows)
-        whole[at, :] = block[...]
+    )(spot, *weights, *[gain[:, None] for gain in gains])
+
+
+def assemble_kernel(count, share, extra_at, spot, *refs):
+    blocks, mates, whole = refs[: count + share - 1], refs[count + share - 1], refs[count + share]
+    rows = mates.shape[1]
+    for index in range(share * count):
+        turn_of, chip = divmod(index, count)
+        for core in range(2):
+            slot = spot[0] ^ (2 * chip + core)
+            first = slot * (share * rows) + (spot[1] ^ turn_of) * rows
+            at = pl.ds(pl.multiple_of(first, 16), rows)
+            if core:
+                whole[at, :] = mates[index]
+            else:
+                whole[at, :] = blocks[count][chip, 0] if turn_of else blocks[chip][0]
     if extra_at is not None:
-        gains = refs[count + 1]
+        gains = refs[-1]
         first = extra_at // LANES * LANES
         for index in range(whole.shape[0] // LANES):
             at = pl.ds(index * LANES, LANES)
@@ -406,20 +520,30 @@
             gains[:, at] = pltpu.roll(part, LANES - extra_at % LANES, 0)[:8]
 
 
-def assemble(blocks, me, extra_at):
-    rows, wide = blocks[0].shape
-    shape = (len(blocks) * rows, wide)
+def assemble(pairs, others, spot, extra_at, *waits):
+    mates = [jnp.stack([pair[1] for pair in pairs])]
+    if others is not None:
+        mates.append(others[:, 1])
+    mates = swap_core(jnp.concatenate(mates))
+    _, rows, wide = pairs[0].shape
+    shape = (2 * mates.shape[0] * rows, wide)
     out_shape = (jax.ShapeDtypeStruct(shape, jnp.bfloat16),)
     if extra_at is not None:
         out_shape += (jax.ShapeDtypeStruct((8, shape[0]), jnp.float32),)
+    own = pl.BlockSpec((1, rows, wide), lambda i: (0, 0, 0))
+    full = lambda *shape: pl.BlockSpec(shape, lambda i: (0,) * len(shape))
+    in_specs = [SMEM] + [own] * len(pairs)
+    if others is not None:
+        in_specs.append(pl.BlockSpec((len(pairs), 1, rows, wide), lambda i: (0, 0, 0, 0)))
     return pl.pallas_call(
-        functools.partial(assemble_kernel, len(blocks), extra_at),
+        functools.partial(assemble_kernel, len(pairs), 1 if others is None else 2, extra_at),
+        grid=(1,),
         out_shape=out_shape,
-        in_specs=[SMEM] + [VMEM] * len(blocks),
-        out_specs=(VMEM,) * len(out_shape),
-        compiler_params=pltpu.CompilerParams(vmem_limit_bytes=48 * 2**20),
+        in_specs=in_specs + [full(*mates.shape)],
+        out_specs=tuple(full(*o.shape) for o in out_shape),
+        compiler_params=pltpu.CompilerParams(vmem_limit_bytes=56 * 2**20),
         name="assemble_weights",
-    )(me[None], *blocks)
+    )(spot, *pairs, *([] if others is None else [others]), mates)
 
 
 def after(values, *earlier):
@@ -432,6 +556,48 @@
         input_output_aliases={i: i for i in range(len(values))},
         name="after",
     )(*values, *earlier)
+
+
+def product_kernel(first, index, x, y, *refs):
+    out, total = refs[-2:]
+    step = pl.program_id(0)
+
+    @pl.when(step == 0)
+    def _():
+        total[...] = jnp.zeros_like(total)
+
+    total[...] += lax.dot_general(
+        x[:, first : first + total.shape[0]], y[...], (((0,), (0,)), ((), ())),
+        preferred_element_type=jnp.float32,
+    )
+
+    @pl.when(step == pl.num_programs(0) - 1)
+    def _():
+        out[...] = total[: out.shape[0], :].astype(jnp.bfloat16)
+
+
+def product(x, y, block, index, first, size, waits):
+    rows, wide = y.shape
+    step = rows // 4
+    held = pad_lanes(size)
+    return pl.pallas_call(
+        functools.partial(product_kernel, first),
+        grid_spec=pltpu.PrefetchScalarGridSpec(
+            num_scalar_prefetch=1,
+            grid=(4,),
+            in_specs=[
+                pl.BlockSpec((step, block), lambda k, at: (k, at[0])),
+                pl.BlockSpec((step, wide), lambda k, at: (k, 0)),
+            ]
+            + [pl.BlockSpec(memory_space=pl.ANY)] * len(waits),
+            out_specs=pl.BlockSpec((size, wide), lambda k, at: (0, 0)),
+            scratch_shapes=[pltpu.VMEM((held, wide), jnp.float32)],
+        ),
+        out_shape=jax.ShapeDtypeStruct((size, wide), jnp.bfloat16),
+        compiler_params=pltpu.CompilerParams(vmem_limit_bytes=48 * 2**20),
+        cost_estimate=LITTLE,
+        name="product",
+    )(index, x, y, *waits)
 
 
 def spread_kernel(places, count, me, *refs):
@@ -471,19 +637,42 @@
 
 def spread(blocks, weights, me, places, step):
     count = len(blocks)
-    rows, wide = blocks[0].shape
-    tile = lambda width: pl.BlockSpec((step, width), lambda i: (i, 0))
+    rows, wide = weights[0].shape[0], blocks[0].shape[1]
+    tile = lambda width: pl.BlockSpec((step, width), lambda i, at: (i, 0))
+    block = pl.BlockSpec((step, wide), lambda i, at: (at[0] % 2 * (rows // step) + i, 0))
     return pl.pallas_call(
         functools.partial(spread_kernel, places, count),
-        grid=(rows // step,),
+        grid_spec=pltpu.PrefetchScalarGridSpec(
+            num_scalar_prefetch=1,
+            grid=(rows // step,),
+            in_specs=[block] * count + [tile(w.shape[1]) for w in weights],
+            out_specs=tuple(tile(w.shape[1]) for w in weights) + (tile(1),),
+            scratch_shapes=[pltpu.VMEM((count, step, wide), jnp.float32)],
+        ),
         out_shape=tuple(jax.ShapeDtypeStruct(w.shape, jnp.float32) for w in weights)
         + (jax.ShapeDtypeStruct((rows, 1), jnp.float32),),
-        in_specs=[SMEM] + [tile(wide)] * count + [tile(w.shape[1]) for w in weights],
-        out_specs=tuple(tile(w.shape[1]) for w in weights) + (tile(1),),
-        scratch_shapes=[pltpu.VMEM((count, step, wide), jnp.float32)],
         compiler_params=pltpu.CompilerParams(vmem_limit_bytes=56 * 2**20),
         name="spread_gradients",
-    )(me[None], *blocks, *weights)
+    )(me[None].astype(jnp.int32), *blocks, *weights)
+
+
+def wait(value, *earlier):
+    return after((value,), *earlier)[0]
+
+
+def mark_kernel(*refs):
+    refs[-1][...] = jnp.zeros_like(refs[-1])
+
+
+def flush(*earlier):
+    token = pl.pallas_call(
+        mark_kernel,
+        out_shape=jax.ShapeDtypeStruct((16, LANES), jnp.bfloat16),
+        in_specs=[pl.BlockSpec(memory_space=pl.ANY)] * len(earlier),
+        out_specs=VMEM,
+        name="mark",
+    )(*earlier)
+    return swap_core(token)
 
 
 def normed(values):
@@ -526,7 +715,7 @@
 
 
 def plain(count):
-    return count != 8
+    return count != 8 or lax.axis_size("replica") != 4
 
 
 def gather_order(count):
@@ -551,7 +740,7 @@
 def gather(own):
     count = lax.axis_size("slot")
     if plain(count):
-        return [lax.all_gather(own, "slot", axis=0, tiled=True)]
+        return jnp.split(lax.all_gather(own, "slot", axis=0, tiled=True), 4, axis=0)
     block = own.shape[0]
     chip = jnp.concatenate([own, swap_core(own)], axis=0)
     near = swap_near(chip)
@@ -559,20 +748,27 @@
     return [chip, near, swap_core(near), jnp.concatenate([corner, swap_core(corner)], axis=0)]
 
 
-def scatter(parts):
+def scatter(parts, *between):
     count = lax.axis_size("slot")
     if plain(count):
-        return lax.psum_scatter(parts[0], "slot", scatter_dimension=0, tiled=True).astype(
+        whole = jnp.concatenate(parts, axis=0)
+        return lax.psum_scatter(whole, "slot", scatter_dimension=0, tiled=True).astype(
             jnp.float32
         )
     chip, near, side, corner = parts
     block = chip.shape[0] // 2
     wide = lambda values: values.astype(jnp.float32)
     near_sum = low(wide(near) + wide(swap_core(side)))
-    other = low(wide(chip[block:]) + wide(swap_near(near_sum[block:])))
     corner_sum = low(wide(corner[:block]) + wide(swap_core(corner[block:])))
-    near_own = low(wide(near_sum[:block]) + wide(swap_far(corner_sum)))
-    return wide(chip[:block]) + wide(swap_near(near_own)) + wide(swap_core(other))
+    arrived = swap_far(corner_sum), swap_near(near_sum[block:])
+    if between:
+        arrived = after(arrived, *between[0](corner_sum))
+    near_own = low(wide(near_sum[:block]) + wide(arrived[0]))
+    other = low(wide(chip[block:]) + wide(arrived[1]))
+    arrived = swap_near(near_own), swap_core(other)
+    if between:
+        arrived = after(arrived, *between[1](near_own))
+    return wide(chip[:block]) + wide(arrived[0]) + wide(arrived[1])
 
 
 def send(block, way):
@@ -583,61 +779,41 @@
 
 
 def sum_trees(part):
-    count = lax.axis_size("replica")
-    if count != 4:
-        return lax.psum(part, "replica")
-    place = lax.axis_index("replica")
-    wide = lambda values: values.astype(jnp.float32)
-    pair = low(wide(part) + wide(lax.ppermute(part, "replica", [(0, 1), (3, 2)])))
-    total = low(wide(pair) + wide(lax.ppermute(pair, "replica", [(1, 2), (2, 1)])))
-    back = lax.ppermute(total, "replica", [(1, 0), (2, 3)])
-    return jnp.where((place == 0) | (place == 3), back, total)
-
-
-def to_columns(weights, gains, places, wide, heads_in, earlier=()):
+    return lax.psum(part, "replica")
+
+
+def plain_columns(weights, gains, places, wide, heads_in):
     count = lax.axis_size("slot")
-    me = lax.axis_index("slot")
-    extra_at = sum(size for size, _ in places) if gains else None
-    if plain(count):
-        blocks = jnp.zeros((count, weights[0].shape[0], wide), jnp.bfloat16)
-        for weight, (size, at), heads in zip(weights, places, heads_in):
-            blocks = blocks.at[:, :, at : at + size].set(split_columns(weight, count, heads))
-        for index, gain in enumerate(gains):
-            blocks = blocks.at[:, :, extra_at + index].set(gain[None])
-        whole = lax.all_to_all(blocks, "slot", 0, 0).reshape(-1, wide)
-        if not gains:
-            return (whole,)
-        return whole, whole[:, extra_at : extra_at + len(gains)].T.astype(jnp.float32)
-    blocks = pack(weights, gains, me, places, wide, count)
-    if earlier:
-        blocks = after(blocks, *earlier)
-    return assemble([send(block, way) for way, block in enumerate(blocks)], me, extra_at)
-
-
-def to_rows(gradient, weights, places, heads_in, group, step):
+    extra_at = sum(size for size, _ in places)
+    blocks = jnp.zeros((count, weights[0].shape[0], wide), jnp.bfloat16)
+    for weight, (size, at), heads in zip(weights, places, heads_in):
+        blocks = blocks.at[:, :, at : at + size].set(split_columns(weight, count, heads))
+    for index, gain in enumerate(gains):
+        blocks = blocks.at[:, :, extra_at + index].set(gain[None])
+    whole = lax.all_to_all(blocks, "slot", 0, 0).reshape(-1, wide)
+    return whole, whole[:, extra_at : extra_at + len(gains)].T.astype(jnp.float32)
+
+
+def send_pairs(pairs):
+    return [send(pair, 2 * chip) for chip, pair in enumerate(pairs)]
+
+
+def swap_halves(pairs):
+    trees = lax.axis_size("replica")
+    return lax.ppermute(pairs, "replica", [(i, i ^ 1) for i in range(trees)])
+
+
+def plain_rows(gradient, weights, places, heads_in):
     count = lax.axis_size("slot")
-    me = lax.axis_index("slot")
     rows = gradient.shape[0] // count
-    if plain(count):
-        blocks = lax.all_to_all(gradient.reshape(count, rows, -1), "slot", 0, 0)
-        blocks = sum_trees(blocks).astype(jnp.float32)
-        parts = [
-            join_columns(blocks[:, :, at : at + size], heads)
-            for (size, at), heads in zip(places, heads_in)
-        ]
-        products = [jnp.sum(p * w.astype(jnp.float32), axis=1) for p, w in zip(parts, weights)]
-        return parts, sum(products)
-    arrived = [None] * count
-    for base in reversed(range(0, count, group)):
-        first = (me ^ base) // group * group * rows
-        summed = sum_trees(lax.dynamic_slice_in_dim(gradient, first, group * rows))
-        for way in range(base, base + group):
-            block = summed
-            if group > 1:
-                block = lax.dynamic_slice_in_dim(summed, (me ^ way) % group * rows, rows)
-            arrived[way] = send(block, way)
-    *parts, product = spread(arrived, weights, me, places, step)
-    return parts, product[:, 0]
+    blocks = lax.all_to_all(gradient.reshape(count, rows, -1), "slot", 0, 0)
+    blocks = sum_trees(blocks).astype(jnp.float32)
+    parts = [
+        join_columns(blocks[:, :, at : at + size], heads)
+        for (size, at), heads in zip(places, heads_in)
+    ]
+    products = [jnp.sum(p * w.astype(jnp.float32), axis=1) for p, w in zip(parts, weights)]
+    return parts, sum(products)
 
 
 def split_columns(weight, count, heads_in=None):
@@ -690,98 +866,201 @@
     tables = turn_tables()
     live = layout(starts, slot_count).astype(jnp.float32).reshape(count, row_count)
     my_live = live[me]
-    live = live[order].reshape(slot_count)
 
     def cut(values):
-        return jnp.split(values, 1 if plain(count) else 4, axis=0)
+        return jnp.split(values, 4, axis=0)
 
     def blocks_of(parts):
         return jnp.concatenate(parts, axis=0).reshape(count, row_count, parts[0].shape[-1])
 
-    layer_parts = gather(layer_in[0])
+    special = not plain(count)
     head_weights = (w_query, w_key, w_value)
     head_places = ((q_width, 0), (HEAD_DIM, q_width), (HEAD_DIM, q_width + HEAD_DIM))
     head_counts = (None, kv_heads, kv_heads)
-    w_heads, gains = to_columns(
-        head_weights, (gain_attn, gain_ffn), head_places, heads_wide, head_counts
-    )
-    full_gain_attn, full_gain_ffn = gains[0], gains[1]
-    attn_parts = [
-        low(normed(part.astype(jnp.float32))[0] * full_gain_attn) for part in layer_parts
-    ]
-    qkv = blocks_of([dot(part, w_heads) for part in attn_parts])
+    hidden_places = ((hidden, 0), (hidden, hidden_wide))
+    gain_pair = (gain_attn, gain_ffn)
+
+    def attn_part(part):
+        return low(normed(part.astype(jnp.float32))[0] * full_gain_attn)
+
+    if special:
+        flat = jnp.stack([me, jnp.zeros_like(me)]).astype(jnp.int32)
+        chip = jnp.concatenate([layer_in[0], swap_core(layer_in[0])], axis=0)
+        near = swap_near(chip)
+        packed = pack(head_weights, gain_pair, flat, head_places, heads_wide, count, 1)
+        hidden_packed = pack((w_gate, w_up), (), flat, hidden_places, 2 * hidden_wide, count, 1)
+        head_pairs = send_pairs(packed)
+        head_pairs = after(head_pairs, flush(hidden_packed[0]))
+        w_heads, gains = assemble(head_pairs, None, flat, heads_width)
+        full_gain_attn, full_gain_ffn = gains[0], gains[1]
+        near = wait(near, head_pairs[1])
+        corner, side = swap_far(near[:row_count]), swap_core(near)
+        hidden_pairs = send_pairs(after(hidden_packed, near))
+        token = flush(near)
+        attn_parts = [attn_part(part) for part in (wait(chip, token), near, side)]
+        parts = [dot(part, w_heads) for part in attn_parts]
+        corner = jnp.concatenate([corner, swap_core(corner)], axis=0)
+        attn_parts.append(attn_part(corner))
+        parts.append(dot(attn_parts[3], w_heads))
+        qkv = blocks_of(parts)
+    else:
+        layer_parts = gather(layer_in[0])
+        w_heads, gains = plain_columns(
+            head_weights, gain_pair, head_places, heads_wide, head_counts
+        )
+        w_hidden, _ = plain_columns(
+            (w_gate, w_up), (), hidden_places, 2 * hidden_wide, (None, None)
+        )
+        full_gain_attn, full_gain_ffn = gains[0], gains[1]
+        attn_parts = [attn_part(part) for part in layer_parts]
+        qkv = blocks_of([dot(part, w_heads) for part in attn_parts])
     attended, *kept = attend_forward(q_width // HEAD_DIM, qkv, tables, tile_starts, parents, order)
     attended = attended.reshape(slot_count, q_width)
+    if special:
+        hidden_pairs = after(hidden_pairs, attended)
+        (w_hidden,) = assemble(hidden_pairs, None, flat, None)
+        attended = wait(attended, hidden_pairs[1])
     residual = layer_in[0].astype(jnp.float32)
     middle = residual + scatter([low(dot(part, w_out)) for part in cut(attended)])
 
-    hidden_places = ((hidden, 0), (hidden, hidden_wide))
-    (w_hidden,) = to_columns(
-        (w_gate, w_up), (), hidden_places, 2 * hidden_wide, (None, None), (w_heads, layer_parts[-1])
-    )
     w_lower = jnp.pad(w_down, ((0, hidden_wide - hidden), (0, 0)))
+    live_rows = jnp.broadcast_to(live.reshape(slot_count, 1), (slot_count, LANES))
     unit_ffn, rms_ffn = normed(middle)
-    ffn_parts = gather(low(unit_ffn * full_gain_ffn))
-    late_cotangent = out_cotangent[0]
-    if not plain(count):
-        (late_cotangent,) = after((late_cotangent,), w_hidden)
-    down_parts = [
-        low(part.astype(jnp.float32) * mask[:, None])
-        for part, mask in zip(gather(late_cotangent), cut(live))
-    ]
-    active_parts, hidden_grads = [], []
-    for ffn_part, down_part in zip(ffn_parts, down_parts):
-        both = dot(ffn_part, w_hidden)
-        gate, up = both[:, :hidden_wide], both[:, hidden_wide:]
-        sigmoid = jax.nn.sigmoid(gate)
-        silu = gate * sigmoid
-        active_parts.append(low(silu * up))
-        active_grad = transpose_dot(down_part, w_lower)
-        gate_grad = low(active_grad * up * sigmoid * (1.0 + gate * (1.0 - sigmoid)))
-        hidden_grads.append(jnp.concatenate([gate_grad, low(active_grad * silu)], axis=1))
-    ffn_input_grad = scatter([low(transpose_dot(part, w_hidden)) for part in hidden_grads])
-    layer_out = low(middle + scatter([low(dot(part, w_lower)) for part in active_parts]))
-    grad_down = rows_dot(
-        jnp.concatenate(active_parts, axis=0), jnp.concatenate(down_parts, axis=0)
-    )[:hidden]
-    grad_hidden = low(
-        rows_dot(jnp.concatenate(ffn_parts, axis=0), jnp.concatenate(hidden_grads, axis=0))
-    )
+    ffn_input = low(unit_ffn * full_gain_ffn)
+    if special:
+        feed = lambda index, part, down, held: dense(
+            index, order, part, down, live_rows, w_hidden, w_lower, held
+        )
+        both = jnp.stack([ffn_input, wait(out_cotangent[0], attended)])
+        chip_both = jnp.concatenate([both, swap_core(both)], axis=1)
+        near_part, near_down = swap_near(chip_both[0]), swap_near(chip_both[1])
+        chip_back, chip_out, held = feed(0, chip_both[0], chip_both[1], ())
+        near_part = wait(near_part, chip_back)
+        near_down = wait(near_down, chip_back)
+        corner, corner_down = swap_far(near_part[:row_count]), swap_far(near_down[:row_count])
+        side_part, side_down = swap_core(near_part), swap_core(near_down)
+        near_back, near_out, held = feed(1, near_part, near_down, held)
+        side_back, side_out, held = feed(2, side_part, side_down, held)
+        corner, corner_down = after((corner, corner_down), near_back)
+        corner_part = jnp.concatenate([corner, swap_core(corner)], axis=0)
+        corner_down = jnp.concatenate([corner_down, swap_core(corner_down)], axis=0)
+        corner_back, corner_out, held = feed(3, corner_part, corner_down, held)
+        back_parts = [chip_back, near_back, side_back, corner_back]
+        out_parts = [chip_out, near_out, side_out, corner_out]
+    else:
+        held, back_parts, out_parts = (), [], []
+        pairs = zip(gather(ffn_input), gather(out_cotangent[0]))
+        for index, (part, down) in enumerate(pairs):
+            back, out, held = dense(
+                index, lax.iota(jnp.int32, 4), part, down, live_rows, w_hidden, w_lower, held
+            )
+            back_parts.append(back)
+            out_parts.append(out)
+    ffn_rows, down_rows, active_rows, hidden_rows = held
     upstream = out_cotangent[0].astype(jnp.float32) * my_live[:, None]
-    middle_grad = upstream + norm_back(ffn_input_grad * full_gain_ffn, unit_ffn, rms_ffn)
-
-    branch_parts = gather(low(middle_grad))
-    attended_grad = blocks_of([low(transpose_dot(part, w_out)) for part in branch_parts])
+
+    def middle_of(ffn_input_grad):
+        return upstream + norm_back(ffn_input_grad * full_gain_ffn, unit_ffn, rms_ffn)
+
+    def hidden_part(chip, *waits):
+        span = 2 * features // count
+        index = ((me ^ chip) // 2)[None].astype(jnp.int32)
+        return product(ffn_rows, hidden_rows, span, index, 0, span, waits)
+
+    def to_heads(part):
+        return low(transpose_dot(part, w_out))
+
+    def proj_part():
+        return low(sum(rows_dot(a, b) for a, b in zip(cut(attended), branch_parts)))
+
+    def heads_part():
+        return low(sum(rows_dot(a, b) for a, b in zip(attn_parts, head_parts)))
+
+    if special:
+        hidden_parts = []
+
+        def all_hidden(mark):
+            for chip in (0, 2, 4, 6):
+                hidden_parts.append(hidden_part(chip, mark, *hidden_parts[-1:]))
+            return hidden_parts[-1:]
+
+        ffn_input_grad = scatter(back_parts, all_hidden, lambda mark: (mark,))
+        middle_grad = middle_of(ffn_input_grad)
+        branch = low(middle_grad)
+        chip_part = jnp.concatenate([branch, swap_core(branch)], axis=0)
+        near_part = swap_near(chip_part)
+        hidden_sums = lax.psum(tuple(hidden_parts), "replica")
+        side_part = swap_core(near_part)
+        corner = swap_far(near_part[:row_count])
+        index = jnp.zeros((1,), jnp.int32)
+        grad_down = product(active_rows, down_rows, hidden_wide, index, 0, hidden, (chip_part,))
+        corner = wait(corner, grad_down)
+        corner_part = jnp.concatenate([corner, swap_core(corner)], axis=0)
+        branch_parts = [chip_part, near_part, side_part, corner_part]
+    else:
+        middle_grad = middle_of(scatter(back_parts))
+        branch_parts = gather(low(middle_grad))
+    attended_grad = blocks_of([to_heads(part) for part in branch_parts])
     head_grads = attend_backward(attended_grad, kept, tables, tile_starts, parents, order)
     head_parts = cut(head_grads.reshape(slot_count, heads_wide))
-    attn_input_grad = scatter(
-        [low(transpose_dot(part, w_heads)) for part in head_parts]
-    )
-    grad_proj = sum(rows_dot(a, b) for a, b in zip(cut(attended), branch_parts))
-    grad_heads = low(sum(rows_dot(a, b) for a, b in zip(attn_parts, head_parts)))
+    input_parts = [low(transpose_dot(part, w_heads)) for part in head_parts]
+    attn_input_grad = scatter(input_parts)
     unit_attn, rms_attn = normed(residual)
     grad_in = low(
         middle_grad + norm_back(attn_input_grad * full_gain_attn, unit_attn, rms_attn)
     )
-
-    grad_down = sum_trees(low(grad_down)).astype(jnp.float32)
-    (grad_gate, grad_up), gain_ffn_sum = to_rows(
-        grad_hidden, (w_gate, w_up), hidden_places, (None, None), 2, 32
-    )
-    grad_proj = sum_trees(low(grad_proj)).astype(jnp.float32)
-    (grad_query, grad_key, grad_value), gain_attn_sum = to_rows(
-        grad_heads, head_weights, head_places, head_counts, 4, 64
-    )
+    grad_proj, grad_heads = proj_part(), heads_part()
+    if special:
+        out_parts = after(out_parts, grad_in)
+    layer_out = low(middle + scatter(out_parts))
+
+    if special:
+
+        def settled(sums):
+            blocks = []
+            for chip, summed in zip(range(0, count, 2), sums):
+                block = send(summed, chip)
+                blocks += [block, swap_core(block)]
+            return blocks
+
+        hidden_sums = after(hidden_sums, grad_in, grad_heads, grad_proj)
+        grad_heads, grad_proj = after((grad_heads, grad_proj), *hidden_sums)
+        grad_heads, grad_proj = lax.psum((grad_heads, grad_proj), "replica")
+        blocks = settled(hidden_sums)
+        grad_gate, grad_up, gain_ffn_sum = spread(blocks, (w_gate, w_up), me, hidden_places, 32)
+        grad_heads, grad_proj = after((grad_heads, grad_proj), grad_gate)
+        grad_down = lax.psum(wait(grad_down, grad_heads), "replica")
+        span = 2 * features // count
+        blocks = settled(
+            [
+                lax.dynamic_slice_in_dim(grad_heads, (me ^ chip) // 2 * span, span)
+                for chip in range(0, count, 2)
+            ]
+        )
+        grad_query, grad_key, grad_value, gain_attn_sum = spread(
+            blocks, head_weights, me, head_places, 64
+        )
+        gain_ffn_sum, gain_attn_sum = gain_ffn_sum[:, 0], gain_attn_sum[:, 0]
+        grad_down = wait(grad_down, grad_query)
+    else:
+        grad_down = sum_trees(low(rows_dot(active_rows, down_rows)[:hidden]))
+        (grad_gate, grad_up), gain_ffn_sum = plain_rows(
+            low(rows_dot(ffn_rows, hidden_rows)), (w_gate, w_up), hidden_places, (None, None)
+        )
+        grad_proj = sum_trees(grad_proj)
+        (grad_query, grad_key, grad_value), gain_attn_sum = plain_rows(
+            grad_heads, head_weights, head_places, head_counts
+        )
     return (
         layer_out[None],
         grad_in[None],
         grad_query,
         grad_key,
         grad_value,
-        grad_proj,
+        grad_proj.astype(jnp.float32),
         grad_gate,
         grad_up,
-        grad_down,
+        grad_down.astype(jnp.float32),
         gain_attn_sum / gain_attn.astype(jnp.float32),
         gain_ffn_sum / gain_ffn.astype(jnp.float32),
     )

time: 1520 us -> 1310 us (0.86)
  Pallas kernels: 145 us -> 324 us
  matrix products: 256 us -> 86.8 us
  waiting for transfers between devices: 789 us -> 653 us
  starting transfers between devices: 118 us -> 47.2 us
  other arithmetic: 127 us -> 96.3 us
    ppermute x24 -> x0, waiting for transfers between devices: 461 us -> none  [the longest x8 252 us: sum_trees(): back = lax.ppermute(total, 'replica', [(1, 0), (2, 3)])]
    psum x0 -> x3, waiting for transfers between devices: none -> 279 us  [the longest x1 154 us: shards(): hidden_sums = lax.psum(tuple(hidden_parts), 'replica')]
    pallas_call x4 -> x15, Pallas kernels: 32.7 us -> 211 us  [the longest x4 110 us: dense(): pl.pallas_call(functools.partial(dense_kernel, chunk, len(held)), out_sha...]
    dot_general x16 -> x8, matrix products: 86.6 us -> 25.8 us  [transpose_dot(): lax.dot_general(left, right, (((1,), (1,)), ((), ())), preferred_element_...]
    dot_general x16 -> x8, matrix products: 83.6 us -> 24.4 us  [dot(): return jnp.dot(left, right, preferred_element_type=jnp.float32)]
    ppermute x24 -> x0, starting transfers between devices: 53.8 us -> none  [the longest x8 30.9 us: sum_trees(): lax.ppermute(part, 'replica', [(0, 1), (3, 2)])]
    dot_general x10 -> x8, matrix products: 85.3 us -> 36.5 us  [rows_dot(): lax.dot_general(left, right, (((0,), (0,)), ((), ())), preferred_element_...]
    convert_element_type x35 -> x17, other arithmetic: 73.7 us -> 36.2 us  [low(): return values.astype(jnp.bfloat16)]
  transfers between devices with their start and end apart: 96 -> 70, of which waited for: 31 -> 25; matrix products, arithmetic and copies ran while one was open for 28% -> 15% of each run, Pallas kernels for 10% -> 25%
where the time goes in v2:
time: 1310 us; the launch traced here: 1290 us
  waiting for transfers between devices  653 us (50%)
  Pallas kernels  324 us (25%)
  other arithmetic  96.3 us (7%)
  matrix products  86.8 us (7%)
  local copies, waits for them, and re-layouts  71 us (5%)
  starting transfers between devices  47.2 us (4%)
  between operations  15.5 us (1%)
    ppermute x12, waiting for transfers between devices, send(): return lax.ppermute(block, 'slot', [(i, i ^ way) for i in range(count)])  176 us
    psum x1, waiting for transfers between devices, shards(): hidden_sums = lax.psum(tuple(hidden_parts), 'replica')  154 us
    pallas_call x4, Pallas kernels, dense(): pl.pallas_call(functools.partial(dense_kernel, chunk, len(held)), out_sha...  110 us
    ppermute x12, waiting for transfers between devices, swap_near(): lax.ppermute(values, 'slot', [(i, i ^ (4 if i % 2 else 2)) for i in range...  96.8 us
    psum x1, waiting for transfers between devices, shards(): grad_down = lax.psum(wait(grad_down, grad_heads), 'replica')  94.3 us
    ppermute x8, waiting for transfers between devices, swap_far(): lax.ppermute(values, 'slot', [(i, i ^ (2 if i % 2 else 4)) for i in range...  74.9 us
    pallas_call x5, Pallas kernels, product(): pl.pallas_call(functools.partial(product_kernel, first), grid_spec=pltpu....  63.9 us
    pallas_call x1, Pallas kernels, attend_backward(): pl.pallas_call(functools.partial(backward_kernel, group), out_shape=jax.S...  50.1 us
  transfers between devices with their start and end apart: 70, of which 25 were waited for; matrix products, arithmetic and copies ran while one was open for 15% of the time, Pallas kernels for 25%

profile of v2, /device:TPU:0, one launch (start us, length us, event | category | flops | bytes accessed | tf_op | source)
XLA Modules:
  0.0 1293.8 jit_solution(9660494834163763983)
XLA Ops:
  19.4 7.8 pack_weights.2
  31.6 16.0 %pack_weights.3 = (bf16[2,320,1792]{2,1,0:T(8,128)(2,1)S(1)}, bf16[2,320,1792]{2,1,0:T(8,128)(2,1)S(1)}, bf16[2,320,1792]{2,1,0:T(8,128)(2,1)}, bf16[2,320,1792]{2,1,0:T(8,128)(2,1)}) custom-call(s32[2]{0:T(128)S(1)} %pad_add_fusion.1.spot, bf16[320,6912]{1,0:T(8,128)(2,1)} %refs_8_.2, bf16[320,6912]{1,0:T(8,128)(2,1)} %refs_9_.2), custom_call_target="tpu_custom_call" | custom-call | tf_op jit(solution)/shard_map/pack_weights/pallas_call | solution.py:491
  52.3 21.0 %collective-permute-done.2.refs_1_ = bf16[2,320,512]{2,1,0:T(8,128)(2,1)S(1)} collective-permute-done((bf16[2,320,512]{2,1,0:T(8,128)(2,1)}, bf16[2,320,512]{2,1,0:T(8,128)(2,1)S(1)}, u32[]{:S(2)}, u32[]{:S(2)}) %collective-permute-start.2) | collective-permute-done | bytes 655392 | tf_op jit(solution)/shard_map/ppermute | solution.py:778
  73.3 8.6 collective-permute-done.4.refs_3_
  95.1 4.0 assemble_weights.2
  105.6 10.8 collective-permute-done.9
  116.4 4.7 fusion.33
  125.4 3.7 fusion.37
  134.3 3.7 fusion.58
  138.0 4.0 fusion.29
  144.9 39.7 %tree_forward.1 = (bf16[8,304,320]{2,1,0:T(8,128)(2,1)S(1)}, bf16[9216,128]{1,0:T(8,128)(2,1)}, bf16[2304,128]{1,0:T(8,128)(2,1)S(1)}, bf16[2304,128]{1,0:T(8,128)(2,1)S(1)}, f32[18,1,512]{2,1,0:T(1,128)S(1)}) custom-call(s32[18]{0:T(128)S(1)} %pad_add_fusion.starts, s32[13]{0:T(128)S(1)} %bitcast.75, s32[8]{0:T(128)S(1)} %fusion.53.order, ...), custom_call_target="tpu_custom_call" | custom-call | tf_op jit(solution)/shard_map/tree_forward/pallas_call | solution.py:405
  188.0 20.7 %collective-permute-done.12.refs_2_ = bf16[2,320,1792]{2,1,0:T(8,128)(2,1)} collective-permute-done((bf16[2,320,1792]{2,1,0:T(8,128)(2,1)}, bf16[2,320,1792]{2,1,0:T(8,128)(2,1)}, u32[]{:S(2)}, u32[]{:S(2)}) %collective-permute-start.12) | collective-permute-done | bytes 2293792 | tf_op jit(solution)/shard_map/ppermute | solution.py:778
  214.2 5.4 collective-permute-done.15
  225.7 28.8 %collective-permute-done.16 = bf16[304,2560]{1,0:T(8,128)(2,1)S(1)} collective-permute-done((bf16[304,2560]{1,0:T(8,128)(2,1)S(1)}, bf16[304,2560]{1,0:T(8,128)(2,1)S(1)}, u32[]{:S(2)}, u32[]{:S(2)}) %collective-permute-start.16) | collective-permute-done | bytes 1556512 | tf_op jit(solution)/shard_map/ppermute | solution.py:737
  261.2 15.9 %collective-permute-done.17 = bf16[304,2560]{1,0:T(8,128)(2,1)} collective-permute-done((bf16[304,2560]{1,0:T(8,128)(2,1)}, bf16[304,2560]{1,0:T(8,128)(2,1)}, u32[]{:S(2)}, u32[]{:S(2)}) %collective-permute-start.17) | collective-permute-done | bytes 1556512 | tf_op jit(solution)/shard_map/ppermute | solution.py:733
  277.0 4.1 multiply_reduce_fusion.1
  291.1 4.1 pad_maximum_fusion
  300.5 4.7 pad.4.lower_far
  305.2 7.8 assemble_weights.3.w_far
  314.4 27.2 %dense.4 = (bf16[2432,2560]{1,0:T(8,128)(2,1)}, bf16[2432,2560]{1,0:T(8,128)(2,1)}, bf16[2432,896]{1,0:T(8,128)(2,1)}, bf16[2432,1792]{1,0:T(8,128)(2,1)}, bf16[...) custom-call(s32[8]{0:T(128)} %copy-done.19, bf16[608,2560]{1,0:T(8,128)(2,1)} %get-tuple-element.176.x_far, ...), custom_call_target="tpu_custom_call" | custom-call | tf_op jit(solution)/shard_map/dense/pallas_call | solution.py:371
  341.7 27.1 %collective-permute-done.23.refs_0_ = bf16[608,2560]{1,0:T(8,128)(2,1)} collective-permute-done((bf16[608,2560]{1,0:T(8,128)(2,1)}, bf16[608,2560]{1,0:T(8,128)(2,1)}, u32[]{:S(2)}, u32[]{:S(2)}) %collective-permute-start.23) | collective-permute-done | bytes 3112992 | tf_op jit(solution)/shard_map/ppermute | solution.py:733
  376.2 27.5 %dense.5 = (bf16[2432,2560]{1,0:T(8,128)(2,1)}, bf16[2432,2560]{1,0:T(8,128)(2,1)}, bf16[2432,896]{1,0:T(8,128)(2,1)}, bf16[2432,1792]{1,0:T(8,128)(2,1)}, bf16[...) custom-call(s32[8]{0:T(128)} %copy-done.19, ...), custom_call_target="tpu_custom_call", output_to_operand_aliasing={{0}: (6, {}), {1}: (7, {}), {2}: (8, {}), {3}: (9, {})} | custom-call | tf_op jit(solution)/shard_map/dense/pallas_call | solution.py:371
  403.7 7.7 collective-permute-done.26.refs_0_
  411.9 28.0 %dense.6 = (bf16[2432,2560]{1,0:T(8,128)(2,1)}, bf16[2432,2560]{1,0:T(8,128)(2,1)}, bf16[2432,896]{1,0:T(8,128)(2,1)}, bf16[2432,1792]{1,0:T(8,128)(2,1)}, bf16[...) custom-call(s32[8]{0:T(128)} %copy-done.19, ...), custom_call_target="tpu_custom_call", output_to_operand_aliasing={{0}: (6, {}), {1}: (7, {}), {2}: (8, {}), {3}: (9, {})} | custom-call | tf_op jit(solution)/shard_map/dense/pallas_call | solution.py:371
  439.9 3.8 pad_maximum_fusion.6.x_far
  445.7 27.4 %dense.7 = (bf16[2432,2560]{1,0:T(8,128)(2,1)}, bf16[2432,2560]{1,0:T(8,128)(2,1)}, bf16[2432,896]{1,0:T(8,128)(2,1)}, bf16[2432,1792]{1,0:T(8,128)(2,1)}, bf16[...) custom-call(s32[8]{0:T(128)} %copy-done.19, ...), custom_call_target="tpu_custom_call", output_to_operand_aliasing={{0}: (6, {}), {1}: (7, {}), {2}: (8, {}), {3}: (9, {})} | custom-call | tf_op jit(solution)/shard_map/dense/pallas_call | solution.py:371
  486.4 10.5 product.5.refs_1_
  496.9 11.3 product.6.refs_1_
  508.2 11.3 product.7.refs_1_
  519.5 10.5 product.8.refs_2_
  532.8 3.5 add_convert_fusion.13.refs_2_
  542.9 17.0 %collective-permute-done.34.refs_0_ = bf16[304,2560]{1,0:T(8,128)(2,1)} collective-permute-done((bf16[304,2560]{1,0:T(8,128)(2,1)}, bf16[304,2560]{1,0:T(8,128)(2,1)}, u32[]{:S(2)}, u32[]{:S(2)}) %collective-permute-start.34) | collective-permute-done | bytes 1556512 | tf_op jit(solution)/shard_map/ppermute | solution.py:733
  559.9 4.4 multiply_reduce_fusion
  565.4 5.1 fusion.60
  574.4 36.8 %collective-permute-done.37 = bf16[608,2560]{1,0:T(8,128)(2,1)} collective-permute-done((bf16[608,2560]{1,0:T(8,128)(2,1)S(1)}, bf16[608,2560]{1,0:T(8,128)(2,1)}, u32[]{:S(2)}, u32[]{:S(2)}) %collective-permute-start.37) | collective-permute-done | bytes 3112992 | tf_op jit(solution)/shard_map/ppermute | solution.py:733
  614.6 20.4 %product.9.refs_1_.refs_0_ = bf16[864,2560]{1,0:T(8,128)(2,1)} custom-call(s32[1]{0:T(128)} %constant.84.clone.1.index, bf16[2432,896]{1,0:T(8,128)(2,1)} %get-tuple-element.138.x, bf16[2432,2560]{1,0:T(8,128)(2,1)} %get-tuple-element.139.y, bf16[608,2560]{1,0:T(8,128)(2,1)S(1)} %pad_maximum_fusion.8.refs_0_), custom_call_target="tpu_custom_call" | custom-call | flops 1 | bytes 1 | tf_op jit(solution)/shard_map/product/pallas_call | solution.py:583
  636.3 3.6 convolution_convert_fusion.10
  639.9 4.9 convolution_convert_fusion.9
  644.8 4.1 fusion.26
  648.9 4.1 convolution_convert_fusion.8
  653.0 4.1 concatenate.51
  657.1 3.6 copy.82
  660.7 50.1 %tree_backward.1 = bf16[8,304,512]{2,1,0:T(8,128)(2,1)} custom-call(s32[18]{0:T(128)} %copy-done.22, s32[13]{0:T(128)} %bitcast.74, s32[8]{0:T(128)} %copy-done.19, bf16[8,304,320]{2,1,0:T(8,128)(2,1)} %bitcast.82, bf16[9216,128]{1,0:T(8,128)(2,1)} %get-tuple-element.140.q_keep, bf16[2304,128]{1,0:T(8,128)(2,1)} %copy-done.16, bf16[2304,128]{1,0:T(8,128)(2,1)} %copy-done.17, ...), custom_call_target="tpu_custom_call" | custom-call | flops 1 | bytes 1 | tf_op jit(solution)/shard_map/tree_backward/pallas_call | solution.py:433
  713.3 3.5 convolution_convert_fusion.1
  725.5 3.4 fusion.22
  730.8 4.3 fusion.31
  741.7 4.6 fusion.13.refs_6_.refs_1_
  746.4 27.6 %collective-permute-done.43 = bf16[304,2560]{1,0:T(8,128)(2,1)S(1)} collective-permute-done((bf16[304,2560]{1,0:T(8,128)(2,1)S(1)}, bf16[304,2560]{1,0:T(8,128)(2,1)S(1)}, u32[]{:S(2)}, u32[]{:S(2)}) %collective-permute-start.43) | collective-permute-done | bytes 1556512 | tf_op jit(solution)/shard_map/ppermute | solution.py:737
  775.4 4.4 fusion.35
  779.8 6.6 fusion.27
  786.5 8.3 add_convert_fusion.4.refs_5_.refs_0_
  799.6 154.1 %all-reduce.11.cloned.1.call-done = (bf16[640,1792]{1,0:T(8,128)(2,1)}, bf16[640,1792]{1,0:T(8,128)(2,1)}, bf16[640,1792]{1,0:T(8,128)(2,1)}, bf16[640,1792]{1,0:T(8,128)(2,1)}) async-done(((bf16[640,1792]{1,0:T(8,128)(2,1)}, bf16[640,1792]{1,0:T(8,128)(2,1)}, bf16[640,1792]{1,0:T(8,128)(2,1)}, bf16[640,1792]{1,0:T(8,128)(2,1)}), (bf16[640,1792]{1,0:T(8,128)(2,1)}, bf16[640,1792]{1,0:T(8,128)(2,1)}, ...) | async-done | bytes 9175056 | tf_op jit(solution)/shard_map/psum | solution.py:992
  959.4 5.8 collective-permute-done.48
  965.3 41.4 %collective-permute-done.54.refs_2_ = bf16[640,1792]{1,0:T(8,128)(2,1)} collective-permute-done((bf16[640,1792]{1,0:T(8,128)(2,1)}, bf16[640,1792]{1,0:T(8,128)(2,1)}, u32[]{:S(2)}, u32[]{:S(2)}) %collective-permute-start.54) | collective-permute-done | bytes 2293792 | tf_op jit(solution)/shard_map/ppermute | solution.py:778
  1006.8 49.2 %collective-permute-done.56.refs_4_ = bf16[640,1792]{1,0:T(8,128)(2,1)} collective-permute-done((bf16[640,1792]{1,0:T(8,128)(2,1)}, bf16[640,1792]{1,0:T(8,128)(2,1)}, u32[]{:S(2)}, u32[]{:S(2)}) %collective-permute-start.56) | collective-permute-done | bytes 2293792 | tf_op jit(solution)/shard_map/ppermute | solution.py:778
  1068.0 16.8 %spread_gradients.2 = (f32[320,6912]{1,0:T(8,128)}, f32[320,6912]{1,0:T(8,128)}, f32[320,1]{1,0:T(8,128)}) custom-call(s32[1]{0:T(128)} %bitcast.4.me, bf16[640,1792]{1,0:T(8,128)(2,1)} %get-tuple-element.148.refs_2_.refs_0_, bf16[640,1792]{1,0:T(8,128)(2,1)} %copy-done.50, bf16[640,1792]{1,0:T(8,128)(2,1)} %collective-permute-done.54.refs_2_, ...), custom_call_target="tpu_custom_call" | custom-call | tf_op jit(solution)/shard_map/spread_gradients/pallas_call | solution.py:643
  1084.8 31.1 %all-reduce.9.cloned.1.call-done = (bf16[2560,512]{1,0:T(8,128)(2,1)}, bf16[320,2560]{1,0:T(8,128)(2,1)}) async-done(((bf16[2560,512]{1,0:T(8,128)(2,1)}, bf16[320,2560]{1,0:T(8,128)(2,1)}), (bf16[2560,512]{1,0:T(8,128)(2,1)}, bf16[320,2560]{1,0:T(8,128)(2,1)})) %all-reduce.9.cloned.1.call-update) | async-done | bytes 4259856 | tf_op jit(solution)/shard_map/psum | solution.py:1028
  1115.9 3.5 add_convert_fusion.7
  1128.0 34.1 %collective-permute-done.65.refs_6_ = bf16[640,512]{1,0:T(8,128)(2,1)S(1)} collective-permute-done((bf16[640,512]{1,0:T(8,128)(2,1)S(1)}, bf16[640,512]{1,0:T(8,128)(2,1)S(1)}, u32[]{:S(2)}, u32[]{:S(2)}) %collective-permute-start.65) | collective-permute-done | bytes 655392 | tf_op jit(solution)/shard_map/ppermute | solution.py:778
  1162.1 5.0 collective-permute-start.66
  1171.6 7.0 spread_gradients.3
  1180.2 5.3 fusion.25
  1185.5 94.3 %all-reduce.7.cloned.1.call-done.refs_0_ = bf16[864,2560]{1,0:T(8,128)(2,1)} async-done(((bf16[864,2560]{1,0:T(8,128)(2,1)}), bf16[864,2560]{1,0:T(8,128)(2,1)}) %all-reduce.7.cloned.1.call-update) | async-done | bytes 4423696 | tf_op jit(solution)/shard_map/psum | solution.py:1032
  1279.8 7.0 convert_element_type.383
  (402 shorter events, 191.7 us)
Async XLA Ops:
  7.2 3.7 collective-permute-start
  14.2 73.0 %collective-permute-start.1 = (bf16[608,2560]{1,0:T(8,128)(2,1)}, bf16[608,2560]{1,0:T(8,128)(2,1)}, u32[]{:S(2)}, u32[]{:S(2)}) collective-permute-start(bf16[608,2560]{1,0:T(8,128)(2,1)} %pad_maximum_fusion.3.refs_0_), channel_id=1, source_target_pairs={{0,8},{4,20},{8,0},{12,28},{16,24},{20,4},{24,16},{28,12},{1,9},{5... | collective-permute-start | bytes 9338888 | tf_op jit(solution)/shard_map/ppermute | solution.py:733
  28.1 45.2 %collective-permute-start.2 = (bf16[2,320,512]{2,1,0:T(8,128)(2,1)}, bf16[2,320,512]{2,1,0:T(8,128)(2,1)S(1)}, u32[]{:S(2)}, u32[]{:S(2)}) collective-permute-start(bf16[2,320,512]{2,1,0:T(8,128)(2,1)} %get-tuple-element.88), channel_id=1, source_target_pairs={{0,8},{4,12},{8,0},{12,4},{16,24},{20,28},{24,16},{28,20},{1,9},{5... | collective-permute-start | bytes 1966088 | tf_op jit(solution)/shard_map/ppermute | solution.py:778
  28.1 45.2 %collective-permute-start.3 = (bf16[2,320,512]{2,1,0:T(8,128)(2,1)}, bf16[2,320,512]{2,1,0:T(8,128)(2,1)S(1)}, u32[]{:S(2)}, u32[]{:S(2)}) collective-permute-start(bf16[2,320,512]{2,1,0:T(8,128)(2,1)} %get-tuple-element.89), channel_id=1, source_target_pairs={{0,16},{4,20},{8,24},{12,28},{16,0},{20,4},{24,8},{28,12},{1,17},{... | collective-permute-start | bytes 1966088 | tf_op jit(solution)/shard_map/ppermute | solution.py:778
  30.1 51.8 %collective-permute-start.4 = (bf16[2,320,512]{2,1,0:T(8,128)(2,1)}, bf16[2,320,512]{2,1,0:T(8,128)(2,1)}, u32[]{:S(2)}, u32[]{:S(2)}) collective-permute-start(bf16[2,320,512]{2,1,0:T(8,128)(2,1)} %get-tuple-element.90), channel_id=1, source_target_pairs={{0,24},{4,28},{8,16},{12,20},{16,8},{20,12},{24,0},{28,4},{1,25},{... | collective-permute-start | bytes 1966088 | tf_op jit(solution)/shard_map/ppermute | solution.py:778
  87.1 8.0 collective-permute-start.7
  89.9 26.5 %collective-permute-start.9 = (bf16[304,2560]{1,0:T(8,128)(2,1)}, bf16[304,2560]{1,0:T(8,128)(2,1)}, u32[]{:S(2)}, u32[]{:S(2)}) collective-permute-start(bf16[304,2560]{1,0:T(8,128)(2,1)} %slice.174), channel_id=1, source_target_pairs={{0,16},{4,12},{8,24},{12,4},{16,0},{20,28},{24,8},{28,20},{1,17},{... | collective-permute-start | bytes 4669448 | tf_op jit(solution)/shard_map/ppermute | solution.py:737
  92.7 39.0 %collective-permute-start.8 = (bf16[608,2560]{1,0:T(8,128)(2,1)}, bf16[608,2560]{1,0:T(8,128)(2,1)}, u32[]{:S(2)}, u32[]{:S(2)}) collective-permute-start(bf16[608,2560]{1,0:T(8,128)(2,1)} %after.20.refs_0_.refs_4_), channel_id=1, source_target_pairs={{0,4},{4,0},{8,12},{12,8},{16,20},{20,16},{24,28},{28,24},{1,5},{5... | collective-permute-start | bytes 9338888 | tf_op jit(solution)/shard_map/ppermute | solution.py:729
  100.7 20.4 %collective-permute-start.6 = (bf16[16,128]{1,0:T(8,128)(2,1)}, bf16[16,128]{1,0:T(8,128)(2,1)S(1)}, u32[]{:S(2)}, u32[]{:S(2)}) collective-permute-start(bf16[16,128]{1,0:T(8,128)(2,1)} %mark.3), channel_id=1, source_target_pairs={{0,4},{4,0},{8,12},{12,8},{16,20},{20,16},{24,28},{28,24},{1,5},{5... | collective-permute-start | bytes 12296 | tf_op jit(solution)/shard_map/ppermute | solution.py:729
  100.7 87.3 %collective-permute-start.11 = (bf16[2,320,1792]{2,1,0:T(8,128)(2,1)}, bf16[2,320,1792]{2,1,0:T(8,128)(2,1)}, u32[]{:S(2)}, u32[]{:S(2)}) collective-permute-start(bf16[2,320,1792]{2,1,0:T(8,128)(2,1)} %get-tuple-element.103), channel_id=1, source_target_pairs={{0,8},{4,12},{8,0},{12,4},{16,24},{20,28},{24,16},{28,20},{1,9},{5... | collective-permute-start | bytes 6881288 | tf_op jit(solution)/shard_map/ppermute | solution.py:778
  101.5 107.2 %collective-permute-start.12 = (bf16[2,320,1792]{2,1,0:T(8,128)(2,1)}, bf16[2,320,1792]{2,1,0:T(8,128)(2,1)}, u32[]{:S(2)}, u32[]{:S(2)}) collective-permute-start(bf16[2,320,1792]{2,1,0:T(8,128)(2,1)} %get-tuple-element.104), channel_id=1, source_target_pairs={{0,16},{4,20},{8,24},{12,28},{16,0},{20,4},{24,8},{28,12},{1,17},{... | collective-permute-start | bytes 6881288 | tf_op jit(solution)/shard_map/ppermute | solution.py:778
  116.4 12.7 collective-permute-start.10
  121.1 87.6 %collective-permute-start.13 = (bf16[2,320,1792]{2,1,0:T(8,128)(2,1)}, bf16[2,320,1792]{2,1,0:T(8,128)(2,1)}, u32[]{:S(2)}, u32[]{:S(2)}) collective-permute-start(bf16[2,320,1792]{2,1,0:T(8,128)(2,1)} %get-tuple-element.105), channel_id=1, source_target_pairs={{0,24},{4,28},{8,16},{12,20},{16,8},{20,12},{24,0},{28,4},{1,25},{... | collective-permute-start | bytes 6881288 | tf_op jit(solution)/shard_map/ppermute | solution.py:778
  211.7 8.8 collective-permute-start.14
  213.7 5.9 collective-permute-start.15
  220.0 34.6 %collective-permute-start.16 = (bf16[304,2560]{1,0:T(8,128)(2,1)S(1)}, bf16[304,2560]{1,0:T(8,128)(2,1)S(1)}, u32[]{:S(2)}, u32[]{:S(2)}) collective-permute-start(bf16[304,2560]{1,0:T(8,128)(2,1)S(1)} %add_convert_fusion.17), channel_id=1, source_target_pairs={{0,16},{4,12},{8,24},{12,4},{16,0},{20,28},{24,8},{28,20},{1,17},{... | collective-permute-start | bytes 4669448 | tf_op jit(solution)/shard_map/ppermute | solution.py:737
  222.4 36.1 %collective-permute-start.18 = (bf16[304,2560]{1,0:T(8,128)(2,1)S(1)}, bf16[304,2560]{1,0:T(8,128)(2,1)S(1)}, u32[]{:S(2)}, u32[]{:S(2)}) collective-permute-start(bf16[304,2560]{1,0:T(8,128)(2,1)S(1)} %slice.180), channel_id=1, source_target_pairs={{0,8},{4,20},{8,0},{12,28},{16,24},{20,4},{24,16},{28,12},{1,9},{5... | collective-permute-start | bytes 4669448 | tf_op jit(solution)/shard_map/ppermute | solution.py:733
  256.1 21.0 %collective-permute-start.17 = (bf16[304,2560]{1,0:T(8,128)(2,1)}, bf16[304,2560]{1,0:T(8,128)(2,1)}, u32[]{:S(2)}, u32[]{:S(2)}) collective-permute-start(bf16[304,2560]{1,0:T(8,128)(2,1)} %add_convert_fusion.16), channel_id=1, source_target_pairs={{0,8},{4,20},{8,0},{12,28},{16,24},{20,4},{24,16},{28,12},{1,9},{5... | collective-permute-start | bytes 4669448 | tf_op jit(solution)/shard_map/ppermute | solution.py:733
  260.0 17.0 %collective-permute-start.19 = (bf16[304,2560]{1,0:T(8,128)(2,1)}, bf16[304,2560]{1,0:T(8,128)(2,1)}, u32[]{:S(2)}, u32[]{:S(2)}) collective-permute-start(bf16[304,2560]{1,0:T(8,128)(2,1)} %add_convert_fusion.15), channel_id=1, source_target_pairs={{0,4},{4,0},{8,12},{12,8},{16,20},{20,16},{24,28},{28,24},{1,5},{5... | collective-permute-start | bytes 4669448 | tf_op jit(solution)/shard_map/ppermute | solution.py:729
  284.0 7.1 collective-permute-start.20
  290.9 14.3 %collective-permute-start.21 = (bf16[4,320,1792]{2,1,0:T(8,128)(2,1)}, bf16[4,320,1792]{2,1,0:T(8,128)(2,1)}, u32[]{:S(2)}, u32[]{:S(2)}) collective-permute-start(bf16[4,320,1792]{2,1,0:T(8,128)(2,1)} %pad_maximum_fusion.2), channel_id=1, source_target_pairs={{0,4},{4,0},{8,12},{12,8},{16,20},{20,16},{24,28},{28,24},{1,5},{5... | collective-permute-start | bytes 13762568 | tf_op jit(solution)/shard_map/ppermute | solution.py:729
  298.3 43.4 %collective-permute-start.22 = (bf16[608,2560]{1,0:T(8,128)(2,1)}, bf16[608,2560]{1,0:T(8,128)(2,1)}, u32[]{:S(2)}, u32[]{:S(2)}) collective-permute-start(bf16[608,2560]{1,0:T(8,128)(2,1)} %get-tuple-element.176.x_far), channel_id=1, source_target_pairs={{0,8},{4,20},{8,0},{12,28},{16,24},{20,4},{24,16},{28,12},{1,9},{5... | collective-permute-start | bytes 9338888 | tf_op jit(solution)/shard_map/ppermute | solution.py:733
  300.3 68.6 %collective-permute-start.23 = (bf16[608,2560]{1,0:T(8,128)(2,1)}, bf16[608,2560]{1,0:T(8,128)(2,1)}, u32[]{:S(2)}, u32[]{:S(2)}) collective-permute-start(bf16[608,2560]{1,0:T(8,128)(2,1)} %get-tuple-element.175.down_far), channel_id=1, source_target_pairs={{0,8},{4,20},{8,0},{12,28},{16,24},{20,4},{24,16},{28,12},{1,9},{5... | collective-permute-start | bytes 9338888 | tf_op jit(solution)/shard_map/ppermute | solution.py:733
  341.7 70.2 %collective-permute-start.24 = (bf16[608,2560]{1,0:T(8,128)(2,1)}, bf16[608,2560]{1,0:T(8,128)(2,1)}, u32[]{:S(2)}, u32[]{:S(2)}) collective-permute-start(bf16[608,2560]{1,0:T(8,128)(2,1)} %after.26.x_far), channel_id=1, source_target_pairs={{0,4},{4,0},{8,12},{12,8},{16,20},{20,16},{24,28},{28,24},{1,5},{5... | collective-permute-start | bytes 9338888 | tf_op jit(solution)/shard_map/ppermute | solution.py:729
  368.8 43.0 %collective-permute-start.25 = (bf16[608,2560]{1,0:T(8,128)(2,1)}, bf16[608,2560]{1,0:T(8,128)(2,1)}, u32[]{:S(2)}, u32[]{:S(2)}) collective-permute-start(bf16[608,2560]{1,0:T(8,128)(2,1)} %after.27.down_far), channel_id=1, source_target_pairs={{0,4},{4,0},{8,12},{12,8},{16,20},{20,16},{24,28},{28,24},{1,5},{5... | collective-permute-start | bytes 9338888 | tf_op jit(solution)/shard_map/ppermute | solution.py:729
  374.1 29.5 %collective-permute-start.27 = (bf16[304,2560]{1,0:T(8,128)(2,1)}, bf16[304,2560]{1,0:T(8,128)(2,1)S(1)}, u32[]{:S(2)}, u32[]{:S(2)}) collective-permute-start(bf16[304,2560]{1,0:T(8,128)(2,1)} %slice.184), channel_id=1, source_target_pairs={{0,16},{4,12},{8,24},{12,4},{16,0},{20,28},{24,8},{28,20},{1,17},{... | collective-permute-start | bytes 4669448 | tf_op jit(solution)/shard_map/ppermute | solution.py:737
  374.3 37.0 %collective-permute-start.26 = (bf16[304,2560]{1,0:T(8,128)(2,1)}, bf16[304,2560]{1,0:T(8,128)(2,1)}, u32[]{:S(2)}, u32[]{:S(2)}) collective-permute-start(bf16[304,2560]{1,0:T(8,128)(2,1)} %slice.183), channel_id=1, source_target_pairs={{0,16},{4,12},{8,24},{12,4},{16,0},{20,28},{24,8},{28,20},{1,17},{... | collective-permute-start | bytes 4669448 | tf_op jit(solution)/shard_map/ppermute | solution.py:737
  411.4 28.6 %collective-permute-start.28 = (bf16[304,2560]{1,0:T(8,128)(2,1)}, bf16[304,2560]{1,0:T(8,128)(2,1)}, u32[]{:S(2)}, u32[]{:S(2)}) collective-permute-start(bf16[304,2560]{1,0:T(8,128)(2,1)} %get-tuple-element.123), channel_id=1, source_target_pairs={{0,4},{4,0},{8,12},{12,8},{16,20},{20,16},{24,28},{28,24},{1,5},{5... | collective-permute-start | bytes 4669448 | tf_op jit(solution)/shard_map/ppermute | solution.py:729
  411.4 32.4 %collective-permute-start.29 = (bf16[304,2560]{1,0:T(8,128)(2,1)}, bf16[304,2560]{1,0:T(8,128)(2,1)S(1)}, u32[]{:S(2)}, u32[]{:S(2)}) collective-permute-start(bf16[304,2560]{1,0:T(8,128)(2,1)} %get-tuple-element.124), channel_id=1, source_target_pairs={{0,4},{4,0},{8,12},{12,8},{16,20},{20,16},{24,28},{28,24},{1,5},{5... | collective-permute-start | bytes 4669448 | tf_op jit(solution)/shard_map/ppermute | solution.py:729
  439.9 39.0 %collective-permute-start.30 = (bf16[608,2560]{1,0:T(8,128)(2,1)}, bf16[608,2560]{1,0:T(8,128)(2,1)}, u32[]{:S(2)}, u32[]{:S(2)}) collective-permute-start(bf16[608,2560]{1,0:T(8,128)(2,1)} %get-tuple-element.130), channel_id=1, source_target_pairs={{0,4},{4,0},{8,12},{12,8},{16,20},{20,16},{24,28},{28,24},{1,5},{5... | collective-permute-start | bytes 9338888 | tf_op jit(solution)/shard_map/ppermute | solution.py:729
  478.6 54.2 %collective-permute-start.32 = (bf16[304,2560]{1,0:T(8,128)(2,1)S(1)}, bf16[304,2560]{1,0:T(8,128)(2,1)}, u32[]{:S(2)}, u32[]{:S(2)}) collective-permute-start(bf16[304,2560]{1,0:T(8,128)(2,1)S(1)} %add_convert_fusion.14.refs_0_), channel_id=1, source_target_pairs={{0,16},{4,12},{8,24},{12,4},{16,0},{20,28},{24,8},{28,20},{1,17},{... | collective-permute-start | bytes 4669448 | tf_op jit(solution)/shard_map/ppermute | solution.py:737
  484.4 48.4 %collective-permute-start.33 = (bf16[304,2560]{1,0:T(8,128)(2,1)}, bf16[304,2560]{1,0:T(8,128)(2,1)}, u32[]{:S(2)}, u32[]{:S(2)}) collective-permute-start(bf16[304,2560]{1,0:T(8,128)(2,1)} %slice.186), channel_id=1, source_target_pairs={{0,8},{4,20},{8,0},{12,28},{16,24},{20,4},{24,16},{28,12},{1,9},{5... | collective-permute-start | bytes 4669448 | tf_op jit(solution)/shard_map/ppermute | solution.py:733
  532.8 420.9 %all-reduce.11.cloned.1.call-start = ((), (), s32[]{:S(2)}) async-start(), calls=%async_computation.2 | async-start | bytes 18350080 | tf_op jit(solution)/shard_map/psum | solution.py:992
  539.3 20.6 %collective-permute-start.34 = (bf16[304,2560]{1,0:T(8,128)(2,1)}, bf16[304,2560]{1,0:T(8,128)(2,1)}, u32[]{:S(2)}, u32[]{:S(2)}) collective-permute-start(bf16[304,2560]{1,0:T(8,128)(2,1)} %add_convert_fusion.13.refs_2_), channel_id=1, source_target_pairs={{0,8},{4,20},{8,0},{12,28},{16,24},{20,4},{24,16},{28,12},{1,9},{5... | collective-permute-start | bytes 4669448 | tf_op jit(solution)/shard_map/ppermute | solution.py:733
  574.1 37.1 %collective-permute-start.37 = (bf16[608,2560]{1,0:T(8,128)(2,1)S(1)}, bf16[608,2560]{1,0:T(8,128)(2,1)}, u32[]{:S(2)}, u32[]{:S(2)}) collective-permute-start(bf16[608,2560]{1,0:T(8,128)(2,1)S(1)} %pad_maximum_fusion.8.refs_0_), channel_id=1, source_target_pairs={{0,8},{4,20},{8,0},{12,28},{16,24},{20,4},{24,16},{28,12},{1,9},{5... | collective-permute-start | bytes 9338888 | tf_op jit(solution)/shard_map/ppermute | solution.py:733
  612.7 22.3 %collective-permute-start.39 = (bf16[304,2560]{1,0:T(8,128)(2,1)S(1)}, bf16[304,2560]{1,0:T(8,128)(2,1)}, u32[]{:S(2)}, u32[]{:S(2)}) collective-permute-start(bf16[304,2560]{1,0:T(8,128)(2,1)S(1)} %slice.187), channel_id=1, source_target_pairs={{0,16},{4,12},{8,24},{12,4},{16,0},{20,28},{24,8},{28,20},{1,17},{... | collective-permute-start | bytes 4669448 | tf_op jit(solution)/shard_map/ppermute | solution.py:737
  614.6 34.3 %collective-permute-start.38 = (bf16[608,2560]{1,0:T(8,128)(2,1)}, bf16[608,2560]{1,0:T(8,128)(2,1)}, u32[]{:S(2)}, u32[]{:S(2)}) collective-permute-start(bf16[608,2560]{1,0:T(8,128)(2,1)} %collective-permute-done.37), channel_id=1, source_target_pairs={{0,4},{4,0},{8,12},{12,8},{16,20},{20,16},{24,28},{28,24},{1,5},{5... | collective-permute-start | bytes 9338888 | tf_op jit(solution)/shard_map/ppermute | solution.py:729
  635.0 9.7 collective-permute-start.40
  635.8 480.1 %all-reduce.9.cloned.1.call-start = ((), (), s32[]{:S(2)}) async-start(), calls=%async_computation.1 | async-start | bytes 8519680 | tf_op jit(solution)/shard_map/psum | solution.py:1028
  716.8 20.3 %collective-permute-start.41 = (bf16[608,2560]{1,0:T(8,128)(2,1)}, bf16[608,2560]{1,0:T(8,128)(2,1)S(1)}, u32[]{:S(2)}, u32[]{:S(2)}) collective-permute-start(bf16[608,2560]{1,0:T(8,128)(2,1)} %convolution_convert_fusion.1), channel_id=1, source_target_pairs={{0,4},{4,0},{8,12},{12,8},{16,20},{20,16},{24,28},{28,24},{1,5},{5... | collective-permute-start | bytes 9338888 | tf_op jit(solution)/shard_map/ppermute | solution.py:729
  722.7 12.4 collective-permute-start.42
  737.0 37.0 %collective-permute-start.43 = (bf16[304,2560]{1,0:T(8,128)(2,1)S(1)}, bf16[304,2560]{1,0:T(8,128)(2,1)S(1)}, u32[]{:S(2)}, u32[]{:S(2)}) collective-permute-start(bf16[304,2560]{1,0:T(8,128)(2,1)S(1)} %add_convert_fusion.11), channel_id=1, source_target_pairs={{0,16},{4,12},{8,24},{12,4},{16,0},{20,28},{24,8},{28,20},{1,17},{... | collective-permute-start | bytes 4669448 | tf_op jit(solution)/shard_map/ppermute | solution.py:737
  738.0 36.4 %collective-permute-start.45 = (bf16[304,2560]{1,0:T(8,128)(2,1)S(1)}, bf16[304,2560]{1,0:T(8,128)(2,1)S(1)}, u32[]{:S(2)}, u32[]{:S(2)}) collective-permute-start(bf16[304,2560]{1,0:T(8,128)(2,1)S(1)} %slice.193), channel_id=1, source_target_pairs={{0,8},{4,20},{8,0},{12,28},{16,24},{20,4},{24,16},{28,12},{1,9},{5... | collective-permute-start | bytes 4669448 | tf_op jit(solution)/shard_map/ppermute | solution.py:733
  774.4 20.4 %collective-permute-start.44 = (bf16[304,2560]{1,0:T(8,128)(2,1)S(1)}, bf16[304,2560]{1,0:T(8,128)(2,1)S(1)}, u32[]{:S(2)}, u32[]{:S(2)}) collective-permute-start(bf16[304,2560]{1,0:T(8,128)(2,1)S(1)} %add_convert_fusion.10), channel_id=1, source_target_pairs={{0,8},{4,20},{8,0},{12,28},{16,24},{20,4},{24,16},{28,12},{1,9},{5... | collective-permute-start | bytes 4669448 | tf_op jit(solution)/shard_map/ppermute | solution.py:733
  774.9 19.9 %collective-permute-start.46 = (bf16[304,2560]{1,0:T(8,128)(2,1)S(1)}, bf16[304,2560]{1,0:T(8,128)(2,1)S(1)}, u32[]{:S(2)}, u32[]{:S(2)}) collective-permute-start(bf16[304,2560]{1,0:T(8,128)(2,1)S(1)} %add_convert_fusion.9), channel_id=1, source_target_pairs={{0,4},{4,0},{8,12},{12,8},{16,20},{20,16},{24,28},{28,24},{1,5},{5... | collective-permute-start | bytes 4669448 | tf_op jit(solution)/shard_map/ppermute | solution.py:729
  953.7 53.0 %collective-permute-start.54 = (bf16[640,1792]{1,0:T(8,128)(2,1)}, bf16[640,1792]{1,0:T(8,128)(2,1)}, u32[]{:S(2)}, u32[]{:S(2)}) collective-permute-start(bf16[640,1792]{1,0:T(8,128)(2,1)} %get-tuple-element.149.refs_3_), channel_id=1, source_target_pairs={{0,8},{4,12},{8,0},{12,4},{16,24},{20,28},{24,16},{28,20},{1,9},{5... | collective-permute-start | bytes 6881288 | tf_op jit(solution)/shard_map/ppermute | solution.py:778
  955.2 100.7 %collective-permute-start.56 = (bf16[640,1792]{1,0:T(8,128)(2,1)}, bf16[640,1792]{1,0:T(8,128)(2,1)}, u32[]{:S(2)}, u32[]{:S(2)}) collective-permute-start(bf16[640,1792]{1,0:T(8,128)(2,1)} %get-tuple-element.150.refs_4_), channel_id=1, source_target_pairs={{0,16},{4,20},{8,24},{12,28},{16,0},{20,4},{24,8},{28,12},{1,17},{... | collective-permute-start | bytes 6881288 | tf_op jit(solution)/shard_map/ppermute | solution.py:778
  956.7 99.3 %collective-permute-start.58 = (bf16[640,1792]{1,0:T(8,128)(2,1)}, bf16[640,1792]{1,0:T(8,128)(2,1)}, u32[]{:S(2)}, u32[]{:S(2)}) collective-permute-start(bf16[640,1792]{1,0:T(8,128)(2,1)} %get-tuple-element.151.refs_5_), channel_id=1, source_target_pairs={{0,24},{4,28},{8,16},{12,20},{16,8},{20,12},{24,0},{28,4},{1,25},{... | collective-permute-start | bytes 6881288 | tf_op jit(solution)/shard_map/ppermute | solution.py:778
  957.2 101.5 %collective-permute-start.47 = (bf16[608,2560]{1,0:T(8,128)(2,1)}, bf16[608,2560]{1,0:T(8,128)(2,1)}, u32[]{:S(2)}, u32[]{:S(2)}) collective-permute-start(bf16[608,2560]{1,0:T(8,128)(2,1)} %get-tuple-element.146), channel_id=1, source_target_pairs={{0,4},{4,0},{8,12},{12,8},{16,20},{20,16},{24,28},{28,24},{1,5},{5... | collective-permute-start | bytes 9338888 | tf_op jit(solution)/shard_map/ppermute | solution.py:729
  958.7 6.5 collective-permute-start.48
  959.3 320.5 %all-reduce.7.cloned.1.call-start = ((), (), s32[]{:S(2)}) async-start(), calls=%async_computation | async-start | bytes 8847360 | tf_op jit(solution)/shard_map/psum | solution.py:1032
  965.2 100.7 %collective-permute-start.53 = (bf16[640,1792]{1,0:T(8,128)(2,1)}, bf16[640,1792]{1,0:T(8,128)(2,1)S(1)}, u32[]{:S(2)}, u32[]{:S(2)}) collective-permute-start(bf16[640,1792]{1,0:T(8,128)(2,1)} %get-tuple-element.148.refs_2_.refs_0_), channel_id=1, source_target_pairs={{0,4},{4,0},{8,12},{12,8},{16,20},{20,16},{24,28},{28,24},{1,5},{5... | collective-permute-start | bytes 6881288 | tf_op jit(solution)/shard_map/ppermute | solution.py:729
  1006.8 59.7 %collective-permute-start.55 = (bf16[640,1792]{1,0:T(8,128)(2,1)}, bf16[640,1792]{1,0:T(8,128)(2,1)S(1)}, u32[]{:S(2)}, u32[]{:S(2)}) collective-permute-start(bf16[640,1792]{1,0:T(8,128)(2,1)} %collective-permute-done.54.refs_2_), channel_id=1, source_target_pairs={{0,4},{4,0},{8,12},{12,8},{16,20},{20,16},{24,28},{28,24},{1,5},{5... | collective-permute-start | bytes 6881288 | tf_op jit(solution)/shard_map/ppermute | solution.py:729
  1056.0 10.5 collective-permute-start.57
  1056.0 10.5 collective-permute-start.59
  1058.8 57.2 %collective-permute-start.49 = (bf16[304,2560]{1,0:T(8,128)(2,1)S(1)}, bf16[304,2560]{1,0:T(8,128)(2,1)}, u32[]{:S(2)}, u32[]{:S(2)}) collective-permute-start(bf16[304,2560]{1,0:T(8,128)(2,1)S(1)} %add_convert_fusion.8), channel_id=1, source_target_pairs={{0,16},{4,12},{8,24},{12,4},{16,0},{20,28},{24,8},{28,20},{1,17},{... | collective-permute-start | bytes 4669448 | tf_op jit(solution)/shard_map/ppermute | solution.py:737
  1065.9 56.9 %collective-permute-start.51 = (bf16[304,2560]{1,0:T(8,128)(2,1)}, bf16[304,2560]{1,0:T(8,128)(2,1)}, u32[]{:S(2)}, u32[]{:S(2)}) collective-permute-start(bf16[304,2560]{1,0:T(8,128)(2,1)} %slice.195), channel_id=1, source_target_pairs={{0,8},{4,20},{8,0},{12,28},{16,24},{20,4},{24,16},{28,12},{1,9},{5... | collective-permute-start | bytes 4669448 | tf_op jit(solution)/shard_map/ppermute | solution.py:733
  1119.5 60.8 %collective-permute-start.50 = (bf16[304,2560]{1,0:T(8,128)(2,1)}, bf16[304,2560]{1,0:T(8,128)(2,1)}, u32[]{:S(2)}, u32[]{:S(2)}) collective-permute-start(bf16[304,2560]{1,0:T(8,128)(2,1)} %add_convert_fusion.7), channel_id=1, source_target_pairs={{0,8},{4,20},{8,0},{12,28},{16,24},{20,4},{24,16},{28,12},{1,9},{5... | collective-permute-start | bytes 4669448 | tf_op jit(solution)/shard_map/ppermute | solution.py:733
  1121.2 40.8 %collective-permute-start.65 = (bf16[640,512]{1,0:T(8,128)(2,1)S(1)}, bf16[640,512]{1,0:T(8,128)(2,1)S(1)}, u32[]{:S(2)}, u32[]{:S(2)}) collective-permute-start(bf16[640,512]{1,0:T(8,128)(2,1)S(1)} %get-tuple-element.177), channel_id=1, source_target_pairs={{0,24},{4,28},{8,16},{12,20},{16,8},{20,12},{24,0},{28,4},{1,25},{... | collective-permute-start | bytes 1966088 | tf_op jit(solution)/shard_map/ppermute | solution.py:778
  1126.0 54.2 %collective-permute-start.52 = (bf16[304,2560]{1,0:T(8,128)(2,1)}, bf16[304,2560]{1,0:T(8,128)(2,1)}, u32[]{:S(2)}, u32[]{:S(2)}) collective-permute-start(bf16[304,2560]{1,0:T(8,128)(2,1)} %add_convert_fusion.6), channel_id=1, source_target_pairs={{0,4},{4,0},{8,12},{12,8},{16,20},{20,16},{24,28},{28,24},{1,5},{5... | collective-permute-start | bytes 4669448 | tf_op jit(solution)/shard_map/ppermute | solution.py:729
  1126.1 36.0 %collective-permute-start.63 = (bf16[640,512]{1,0:T(8,128)(2,1)S(1)}, bf16[640,512]{1,0:T(8,128)(2,1)}, u32[]{:S(2)}, u32[]{:S(2)}) collective-permute-start(bf16[640,512]{1,0:T(8,128)(2,1)S(1)} %get-tuple-element.178), channel_id=1, source_target_pairs={{0,16},{4,20},{8,24},{12,28},{16,0},{20,4},{24,8},{28,12},{1,17},{... | collective-permute-start | bytes 1966088 | tf_op jit(solution)/shard_map/ppermute | solution.py:778
  1126.7 41.5 %collective-permute-start.61 = (bf16[640,512]{1,0:T(8,128)(2,1)S(1)}, bf16[640,512]{1,0:T(8,128)(2,1)}, u32[]{:S(2)}, u32[]{:S(2)}) collective-permute-start(bf16[640,512]{1,0:T(8,128)(2,1)S(1)} %get-tuple-element.179), channel_id=1, source_target_pairs={{0,8},{4,12},{8,0},{12,4},{16,24},{20,28},{24,16},{28,20},{1,9},{5... | collective-permute-start | bytes 1966088 | tf_op jit(solution)/shard_map/ppermute | solution.py:778
  1162.1 6.1 collective-permute-start.60
  1162.1 9.5 collective-permute-start.66
  (88 other events, 1168.2 us)
Sparse Core Ops, SparseCore 0:
  635.9 317.7 all-reduce.10
  959.4 156.3 all-reduce.8
  1118.4 161.3 all-reduce.6

commit v3 on v2

--- a/solution.py
+++ b/solution.py
@@ -465,7 +465,7 @@
     return pltpu.roll(values, lax.rem(at - shift + reach, reach), 1)[:, :wide]
 
 
-def pack_kernel(places, extras, step, spot, *refs):
+def pack_kernel(places, extras, step, chips, spot, *refs):
     sources, gains = refs[: len(places)], refs[len(places) : len(places) + extras]
     pairs = refs[len(places) + extras :]
     half, wide = pairs[0].shape[1:]
@@ -477,40 +477,41 @@
         there = pl.ds(pl.multiple_of(i * step, step), step)
         lane = lax.broadcasted_iota(jnp.int32, (step, wide), 1)
         for way in range(2 * len(pairs)):
+            slot = spot[0] ^ (2 * chips[way // 2] + way % 2)
             total = None
             for ref, (size, at) in zip(sources, places):
-                part = window(ref, rows, (spot[0] ^ way) * size, size, wide, at)
+                part = window(ref, rows, slot * size, size, wide, at)
                 total = part if total is None else total + part
             for index, gain in enumerate(gains):
                 total = jnp.where(lane == extra_at + index, gain[rows, :].astype(jnp.float32), total)
             pairs[way // 2][way % 2, there, :] = total.astype(jnp.bfloat16)
 
 
-def pack(weights, gains, spot, places, wide, count, share):
+def pack(weights, gains, spot, places, wide, chips, share):
     half = weights[0].shape[0] // share
     return pl.pallas_call(
-        functools.partial(pack_kernel, places, len(gains), 16),
-        out_shape=(jax.ShapeDtypeStruct((2, half, wide), jnp.bfloat16),) * (count // 2),
+        functools.partial(pack_kernel, places, len(gains), 16, chips),
+        out_shape=(jax.ShapeDtypeStruct((2, half, wide), jnp.bfloat16),) * len(chips),
         in_specs=[SMEM] + [VMEM] * (len(weights) + len(gains)),
-        out_specs=(VMEM,) * (count // 2),
+        out_specs=(VMEM,) * len(chips),
         compiler_params=pltpu.CompilerParams(vmem_limit_bytes=48 * 2**20),
         name="pack_weights",
     )(spot, *weights, *[gain[:, None] for gain in gains])
 
 
-def assemble_kernel(count, share, extra_at, spot, *refs):
-    blocks, mates, whole = refs[: count + share - 1], refs[count + share - 1], refs[count + share]
-    rows = mates.shape[1]
-    for index in range(share * count):
-        turn_of, chip = divmod(index, count)
+def assemble_kernel(shares, extra_at, spot, *refs):
+    blocks, mates, whole = refs[: len(shares)], refs[len(shares)], refs[len(shares) + 1]
+    rows = blocks[0].shape[1]
+    passed = 0
+    for (chip, share, other), block in zip(shares, blocks):
+        part = rows // share
         for core in range(2):
-            slot = spot[0] ^ (2 * chip + core)
-            first = slot * (share * rows) + (spot[1] ^ turn_of) * rows
-            at = pl.ds(pl.multiple_of(first, 16), rows)
-            if core:
-                whole[at, :] = mates[index]
-            else:
-                whole[at, :] = blocks[count][chip, 0] if turn_of else blocks[chip][0]
+            first = (spot[0] ^ (2 * chip + core)) * rows
+            if share > 1:
+                first = first + (spot[1] ^ other) * part
+            at = pl.ds(pl.multiple_of(first, 16), part)
+            whole[at, :] = mates[passed : passed + part, :] if core else block[0]
+        passed += part
     if extra_at is not None:
         gains = refs[-1]
         first = extra_at // LANES * LANES
@@ -520,30 +521,24 @@
             gains[:, at] = pltpu.roll(part, LANES - extra_at % LANES, 0)[:8]
 
 
-def assemble(pairs, others, spot, extra_at, *waits):
-    mates = [jnp.stack([pair[1] for pair in pairs])]
-    if others is not None:
-        mates.append(others[:, 1])
-    mates = swap_core(jnp.concatenate(mates))
-    _, rows, wide = pairs[0].shape
-    shape = (2 * mates.shape[0] * rows, wide)
+def assemble(pairs, shares, spot, extra_at):
+    mates = swap_core(jnp.concatenate([pair[1] for pair in pairs], axis=0))
+    rows, wide = pairs[0].shape[1:]
+    shape = (2 * mates.shape[0], wide)
     out_shape = (jax.ShapeDtypeStruct(shape, jnp.bfloat16),)
     if extra_at is not None:
         out_shape += (jax.ShapeDtypeStruct((8, shape[0]), jnp.float32),)
-    own = pl.BlockSpec((1, rows, wide), lambda i: (0, 0, 0))
+    own = lambda pair: pl.BlockSpec((1,) + pair.shape[1:], lambda i: (0, 0, 0))
     full = lambda *shape: pl.BlockSpec(shape, lambda i: (0,) * len(shape))
-    in_specs = [SMEM] + [own] * len(pairs)
-    if others is not None:
-        in_specs.append(pl.BlockSpec((len(pairs), 1, rows, wide), lambda i: (0, 0, 0, 0)))
     return pl.pallas_call(
-        functools.partial(assemble_kernel, len(pairs), 1 if others is None else 2, extra_at),
+        functools.partial(assemble_kernel, shares, extra_at),
         grid=(1,),
         out_shape=out_shape,
-        in_specs=in_specs + [full(*mates.shape)],
+        in_specs=[SMEM] + [own(pair) for pair in pairs] + [full(*mates.shape)],
         out_specs=tuple(full(*o.shape) for o in out_shape),
         compiler_params=pltpu.CompilerParams(vmem_limit_bytes=56 * 2**20),
         name="assemble_weights",
-    )(spot, *pairs, *([] if others is None else [others]), mates)
+    )(spot, *pairs, mates)
 
 
 def after(values, *earlier):
@@ -887,11 +882,16 @@
         flat = jnp.stack([me, jnp.zeros_like(me)]).astype(jnp.int32)
         chip = jnp.concatenate([layer_in[0], swap_core(layer_in[0])], axis=0)
         near = swap_near(chip)
-        packed = pack(head_weights, gain_pair, flat, head_places, heads_wide, count, 1)
-        hidden_packed = pack((w_gate, w_up), (), flat, hidden_places, 2 * hidden_wide, count, 1)
+        spot = jnp.stack([me, lax.axis_index("replica") % 2]).astype(jnp.int32)
+        chips = (0, 1, 2, 3)
+        packed = pack(head_weights, gain_pair, flat, head_places, heads_wide, chips, 1)
+        hidden_weights = (w_gate, w_up)
+        hidden_packed = pack(hidden_weights, (), flat, hidden_places, 2 * hidden_wide, chips[:3], 1)
+        hidden_packed += pack(hidden_weights, (), spot, hidden_places, 2 * hidden_wide, chips[3:], 2)
         head_pairs = send_pairs(packed)
         head_pairs = after(head_pairs, flush(hidden_packed[0]))
-        w_heads, gains = assemble(head_pairs, None, flat, heads_width)
+        whole_shares = tuple((chip, 1, 0) for chip in chips)
+        w_heads, gains = assemble(head_pairs, whole_shares, flat, heads_width)
         full_gain_attn, full_gain_ffn = gains[0], gains[1]
         near = wait(near, head_pairs[1])
         corner, side = swap_far(near[:row_count]), swap_core(near)
@@ -918,8 +918,8 @@
     attended = attended.reshape(slot_count, q_width)
     if special:
         hidden_pairs = after(hidden_pairs, attended)
-        (w_hidden,) = assemble(hidden_pairs, None, flat, None)
-        attended = wait(attended, hidden_pairs[1])
+        hidden_pairs += (swap_halves(hidden_pairs[3]),)
+        attended = wait(attended, hidden_pairs[3])
     residual = layer_in[0].astype(jnp.float32)
     middle = residual + scatter([low(dot(part, w_out)) for part in cut(attended)])
 
@@ -931,12 +931,16 @@
         feed = lambda index, part, down, held: dense(
             index, order, part, down, live_rows, w_hidden, w_lower, held
         )
-        both = jnp.stack([ffn_input, wait(out_cotangent[0], attended)])
-        chip_both = jnp.concatenate([both, swap_core(both)], axis=1)
-        near_part, near_down = swap_near(chip_both[0]), swap_near(chip_both[1])
-        chip_back, chip_out, held = feed(0, chip_both[0], chip_both[1], ())
-        near_part = wait(near_part, chip_back)
+        hidden_shares = whole_shares[:3] + ((3, 2, 0), (3, 2, 1))
+        (w_hidden,) = assemble(hidden_pairs, hidden_shares, spot, None)
+        cotangent = wait(out_cotangent[0], attended)
+        chip_down = jnp.concatenate([cotangent, swap_core(cotangent)], axis=0)
+        near_down = swap_near(chip_down)
+        chip_part = jnp.concatenate([ffn_input, swap_core(ffn_input)], axis=0)
+        near_part = swap_near(chip_part)
+        chip_back, chip_out, held = feed(0, chip_part, chip_down, ())
         near_down = wait(near_down, chip_back)
+        near_part = wait(near_part, near_down)
         corner, corner_down = swap_far(near_part[:row_count]), swap_far(near_down[:row_count])
         side_part, side_down = swap_core(near_part), swap_core(near_down)
         near_back, near_out, held = feed(1, near_part, near_down, held)

time: 1310 us -> 1260 us (0.962); the launches traced: 1290 us -> 1260 us
  waiting for transfers between devices: 653 us -> 621 us
    ppermute x12, waiting for transfers between devices: 176 us -> 160 us  [send(): return lax.ppermute(block, 'slot', [(i, i ^ way) for i in range(count)])]
    unnamed x165 -> x181, local copies, waits for them, and re-layouts: 26 us -> 34 us
    pallas_call x4 -> x5, Pallas kernels: 35.6 us -> 36.6 us  [the longest x3 24.8 us: pack(): pl.pallas_call(functools.partial(pack_kernel, places, len(gains), 16, chi...]
    convert_element_type x17 -> x18, other arithmetic: 36.2 us -> 36.6 us  [low(): return values.astype(jnp.bfloat16)]
  transfers between devices with their start and end apart: 70 -> 72, of which waited for: 25 -> 27; matrix products, arithmetic and copies ran while one was open for 15% -> 15% of each run, Pallas kernels for 25% -> 26%
where the time goes in v3:
time: 1260 us
  waiting for transfers between devices  621 us (49%)
  Pallas kernels  325 us (26%)
  other arithmetic  92 us (7%)
  matrix products  86.5 us (7%)
  local copies, waits for them, and re-layouts  67.7 us (5%)
  starting transfers between devices  49.9 us (4%)
  between operations  15.4 us (1%)
    ppermute x12, waiting for transfers between devices, send(): return lax.ppermute(block, 'slot', [(i, i ^ way) for i in range(count)])  160 us
    psum x1, waiting for transfers between devices, shards(): hidden_sums = lax.psum(tuple(hidden_parts), 'replica')  156 us
    pallas_call x4, Pallas kernels, dense(): pl.pallas_call(functools.partial(dense_kernel, chunk, len(held)), out_sha...  110 us
    psum x1, waiting for transfers between devices, shards(): grad_down = lax.psum(wait(grad_down, grad_heads), 'replica')  94.3 us
    ppermute x12, waiting for transfers between devices, swap_near(): lax.ppermute(values, 'slot', [(i, i ^ (4 if i % 2 else 2)) for i in range...  89.6 us
    pallas_call x5, Pallas kernels, product(): pl.pallas_call(functools.partial(product_kernel, first), grid_spec=pltpu....  63.9 us
    ppermute x8, waiting for transfers between devices, swap_far(): lax.ppermute(values, 'slot', [(i, i ^ (2 if i % 2 else 4)) for i in range...  62 us
    pallas_call x1, Pallas kernels, attend_backward(): pl.pallas_call(functools.partial(backward_kernel, group), out_shape=jax.S...  50.1 us
  transfers between devices with their start and end apart: 72, of which 27 were waited for; matrix products, arithmetic and copies ran while one was open for 15% of the time, Pallas kernels for 26%

profile of v3, /device:TPU:0, one launch (start us, length us, event | category | flops | bytes accessed | tf_op | source)
XLA Modules:
  0.0 1258.1 jit_solution(13221293875999958176)
XLA Ops:
  19.4 7.8 pack_weights.3
  31.6 12.7 %pack_weights.4 = (bf16[2,320,1792]{2,1,0:T(8,128)(2,1)S(1)}, bf16[2,320,1792]{2,1,0:T(8,128)(2,1)S(1)}, bf16[2,320,1792]{2,1,0:T(8,128)(2,1)}) custom-call(s32[2]{0:T(128)S(1)} %pad_add_fusion.1.spot, bf16[320,6912]{1,0:T(8,128)(2,1)} %refs_8_.2, bf16[320,6912]{1,0:T(8,128)(2,1)} %refs_9_.2), custom_call_target="tpu_custom_call" | custom-call | tf_op jit(solution)/shard_map/pack_weights/pallas_call | solution.py:492
  49.0 24.3 %collective-permute-done.2.refs_1_ = bf16[2,320,512]{2,1,0:T(8,128)(2,1)S(1)} collective-permute-done((bf16[2,320,512]{2,1,0:T(8,128)(2,1)}, bf16[2,320,512]{2,1,0:T(8,128)(2,1)S(1)}, u32[]{:S(2)}, u32[]{:S(2)}) %collective-permute-start.2) | collective-permute-done | bytes 655392 | tf_op jit(solution)/shard_map/ppermute | solution.py:773
  73.3 8.6 collective-permute-done.4.refs_3_
  90.4 4.3 pack_weights.5.refs_3_
  100.9 4.0 assemble_weights.2
  111.5 4.7 fusion.32
  120.2 3.7 fusion.36
  129.1 3.7 fusion.58
  132.9 4.0 fusion.28
  139.7 39.7 %tree_forward.1 = (bf16[8,304,320]{2,1,0:T(8,128)(2,1)S(1)}, bf16[9216,128]{1,0:T(8,128)(2,1)}, bf16[2304,128]{1,0:T(8,128)(2,1)S(1)}, bf16[2304,128]{1,0:T(8,128)(2,1)S(1)}, f32[18,1,512]{2,1,0:T(1,128)S(1)}) custom-call(s32[18]{0:T(128)S(1)} %pad_add_fusion.starts, s32[13]{0:T(128)S(1)} %bitcast.89, s32[8]{0:T(128)S(1)} %fusion.53.order, ...), custom_call_target="tpu_custom_call" | custom-call | tf_op jit(solution)/shard_map/tree_forward/pallas_call | solution.py:405
  190.0 5.4 collective-permute-done.15
  201.4 29.9 %collective-permute-done.16 = bf16[304,2560]{1,0:T(8,128)(2,1)S(1)} collective-permute-done((bf16[304,2560]{1,0:T(8,128)(2,1)S(1)}, bf16[304,2560]{1,0:T(8,128)(2,1)S(1)}, u32[]{:S(2)}, u32[]{:S(2)}) %collective-permute-start.16) | collective-permute-done | bytes 1556512 | tf_op jit(solution)/shard_map/ppermute | solution.py:732
  241.7 11.6 collective-permute-done.17
  259.3 4.0 collective-permute-done.22.refs_4_
  274.0 7.8 assemble_weights.3.w_far
  283.3 27.3 %dense.4 = (bf16[2432,2560]{1,0:T(8,128)(2,1)}, bf16[2432,2560]{1,0:T(8,128)(2,1)}, bf16[2432,896]{1,0:T(8,128)(2,1)}, bf16[2432,1792]{1,0:T(8,128)(2,1)}, bf16[...) custom-call(s32[8]{0:T(128)} %copy-done.20, bf16[608,2560]{1,0:T(8,128)(2,1)} %pad_maximum_fusion.3.x_far, ...), custom_call_target="tpu_custom_call" | custom-call | tf_op jit(solution)/shard_map/dense/pallas_call | solution.py:371
  310.7 25.3 %collective-permute-done.24.refs_0_ = bf16[608,2560]{1,0:T(8,128)(2,1)} collective-permute-done((bf16[608,2560]{1,0:T(8,128)(2,1)}, bf16[608,2560]{1,0:T(8,128)(2,1)}, u32[]{:S(2)}, u32[]{:S(2)}) %collective-permute-start.24) | collective-permute-done | bytes 3112992 | tf_op jit(solution)/shard_map/ppermute | solution.py:728
  343.3 27.5 %dense.5 = (bf16[2432,2560]{1,0:T(8,128)(2,1)}, bf16[2432,2560]{1,0:T(8,128)(2,1)}, bf16[2432,896]{1,0:T(8,128)(2,1)}, bf16[2432,1792]{1,0:T(8,128)(2,1)}, bf16[...) custom-call(s32[8]{0:T(128)} %copy-done.20, ...), custom_call_target="tpu_custom_call", output_to_operand_aliasing={{0}: (6, {}), {1}: (7, {}), {2}: (8, {}), {3}: (9, {})} | custom-call | tf_op jit(solution)/shard_map/dense/pallas_call | solution.py:371
  370.8 5.1 collective-permute-done.28.refs_0_
  376.4 27.9 %dense.6 = (bf16[2432,2560]{1,0:T(8,128)(2,1)}, bf16[2432,2560]{1,0:T(8,128)(2,1)}, bf16[2432,896]{1,0:T(8,128)(2,1)}, bf16[2432,1792]{1,0:T(8,128)(2,1)}, bf16[...) custom-call(s32[8]{0:T(128)} %copy-done.20, ...), custom_call_target="tpu_custom_call", output_to_operand_aliasing={{0}: (6, {}), {1}: (7, {}), {2}: (8, {}), {3}: (9, {})} | custom-call | tf_op jit(solution)/shard_map/dense/pallas_call | solution.py:371
  404.4 3.8 pad_maximum_fusion.5.x_far
  410.1 27.4 %dense.7 = (bf16[2432,2560]{1,0:T(8,128)(2,1)}, bf16[2432,2560]{1,0:T(8,128)(2,1)}, bf16[2432,896]{1,0:T(8,128)(2,1)}, bf16[2432,1792]{1,0:T(8,128)(2,1)}, bf16[...) custom-call(s32[8]{0:T(128)} %copy-done.20, ...), custom_call_target="tpu_custom_call", output_to_operand_aliasing={{0}: (6, {}), {1}: (7, {}), {2}: (8, {}), {3}: (9, {})} | custom-call | tf_op jit(solution)/shard_map/dense/pallas_call | solution.py:371
  450.7 10.5 product.5.refs_1_
  461.1 11.3 product.6.refs_1_
  472.4 11.3 product.7.refs_1_
  483.7 10.5 product.8.refs_2_
  497.1 3.5 add_convert_fusion.13.refs_2_
  507.2 17.0 %collective-permute-done.36.refs_0_ = bf16[304,2560]{1,0:T(8,128)(2,1)} collective-permute-done((bf16[304,2560]{1,0:T(8,128)(2,1)}, bf16[304,2560]{1,0:T(8,128)(2,1)}, u32[]{:S(2)}, u32[]{:S(2)}) %collective-permute-start.36) | collective-permute-done | bytes 1556512 | tf_op jit(solution)/shard_map/ppermute | solution.py:728
  524.2 4.4 multiply_reduce_fusion
  529.8 5.1 fusion.60
  534.8 3.4 collective-permute-done.38
  540.0 35.6 %collective-permute-done.39 = bf16[608,2560]{1,0:T(8,128)(2,1)} collective-permute-done((bf16[608,2560]{1,0:T(8,128)(2,1)S(1)}, bf16[608,2560]{1,0:T(8,128)(2,1)}, u32[]{:S(2)}, u32[]{:S(2)}) %collective-permute-start.39) | collective-permute-done | bytes 3112992 | tf_op jit(solution)/shard_map/ppermute | solution.py:728
  579.0 20.4 %product.9.refs_1_.refs_0_ = bf16[864,2560]{1,0:T(8,128)(2,1)} custom-call(s32[1]{0:T(128)} %constant.95.clone.1.index, bf16[2432,896]{1,0:T(8,128)(2,1)} %get-tuple-element.136.x, bf16[2432,2560]{1,0:T(8,128)(2,1)} %get-tuple-element.137.y, bf16[608,2560]{1,0:T(8,128)(2,1)S(1)} %pad_maximum_fusion.7.refs_0_), custom_call_target="tpu_custom_call" | custom-call | flops 1 | bytes 1 | tf_op jit(solution)/shard_map/product/pallas_call | solution.py:578
  600.5 3.6 convolution_convert_fusion.10
  604.1 4.8 convolution_convert_fusion.9
  608.9 4.1 fusion.25
  613.0 4.1 convolution_convert_fusion.8
  617.2 4.1 concatenate.63
  621.3 3.6 copy.82
  624.8 50.1 %tree_backward.1 = bf16[8,304,512]{2,1,0:T(8,128)(2,1)} custom-call(s32[18]{0:T(128)} %copy-done.24, s32[13]{0:T(128)} %bitcast.88, s32[8]{0:T(128)} %copy-done.20, bf16[8,304,320]{2,1,0:T(8,128)(2,1)} %bitcast.94, bf16[9216,128]{1,0:T(8,128)(2,1)} %get-tuple-element.138.q_keep, bf16[2304,128]{1,0:T(8,128)(2,1)} %copy-done.17, bf16[2304,128]{1,0:T(8,128)(2,1)} %copy-done.18, ...), custom_call_target="tpu_custom_call" | custom-call | flops 1 | bytes 1 | tf_op jit(solution)/shard_map/tree_backward/pallas_call | solution.py:433
  677.5 3.5 convolution_convert_fusion.1
  680.9 3.3 fusion.45
  689.0 3.3 fusion.22
  694.3 4.3 fusion.30
  705.1 4.7 fusion.13.refs_6_.refs_1_
  709.7 27.1 %collective-permute-done.45 = bf16[304,2560]{1,0:T(8,128)(2,1)S(1)} collective-permute-done((bf16[304,2560]{1,0:T(8,128)(2,1)S(1)}, bf16[304,2560]{1,0:T(8,128)(2,1)S(1)}, u32[]{:S(2)}, u32[]{:S(2)}) %collective-permute-start.45) | collective-permute-done | bytes 1556512 | tf_op jit(solution)/shard_map/ppermute | solution.py:732
  738.3 4.3 fusion.34
  742.6 6.6 fusion.26
  749.3 8.2 add_convert_fusion.4.refs_5_.refs_0_
  762.5 155.7 %all-reduce.11.cloned.1.call-done = (bf16[640,1792]{1,0:T(8,128)(2,1)}, bf16[640,1792]{1,0:T(8,128)(2,1)}, bf16[640,1792]{1,0:T(8,128)(2,1)}, bf16[640,1792]{1,0:T(8,128)(2,1)}) async-done(((bf16[640,1792]{1,0:T(8,128)(2,1)}, bf16[640,1792]{1,0:T(8,128)(2,1)}, bf16[640,1792]{1,0:T(8,128)(2,1)}, bf16[640,1792]{1,0:T(8,128)(2,1)}), (bf16[640,1792]{1,0:T(8,128)(2,1)}, bf16[640,1792]{1,0:T(8,128)(2,1)}, ...) | async-done | bytes 9175056 | tf_op jit(solution)/shard_map/psum | solution.py:996
  923.9 5.8 collective-permute-done.50
  929.8 41.4 %collective-permute-done.56.refs_2_ = bf16[640,1792]{1,0:T(8,128)(2,1)} collective-permute-done((bf16[640,1792]{1,0:T(8,128)(2,1)}, bf16[640,1792]{1,0:T(8,128)(2,1)}, u32[]{:S(2)}, u32[]{:S(2)}) %collective-permute-start.56) | collective-permute-done | bytes 2293792 | tf_op jit(solution)/shard_map/ppermute | solution.py:773
  971.3 49.2 %collective-permute-done.58.refs_4_ = bf16[640,1792]{1,0:T(8,128)(2,1)} collective-permute-done((bf16[640,1792]{1,0:T(8,128)(2,1)}, bf16[640,1792]{1,0:T(8,128)(2,1)}, u32[]{:S(2)}, u32[]{:S(2)}) %collective-permute-start.58) | collective-permute-done | bytes 2293792 | tf_op jit(solution)/shard_map/ppermute | solution.py:773
  1032.5 16.8 %spread_gradients.2 = (f32[320,6912]{1,0:T(8,128)}, f32[320,6912]{1,0:T(8,128)}, f32[320,1]{1,0:T(8,128)}) custom-call(s32[1]{0:T(128)} %bitcast.4.me, bf16[640,1792]{1,0:T(8,128)(2,1)} %get-tuple-element.146.refs_2_.refs_0_, bf16[640,1792]{1,0:T(8,128)(2,1)} %copy-done.55, bf16[640,1792]{1,0:T(8,128)(2,1)} %collective-permute-done.56.refs_2_, ...), custom_call_target="tpu_custom_call" | custom-call | tf_op jit(solution)/shard_map/spread_gradients/pallas_call | solution.py:638
  1049.3 31.1 %all-reduce.9.cloned.1.call-done = (bf16[2560,512]{1,0:T(8,128)(2,1)}, bf16[320,2560]{1,0:T(8,128)(2,1)}) async-done(((bf16[2560,512]{1,0:T(8,128)(2,1)}, bf16[320,2560]{1,0:T(8,128)(2,1)}), (bf16[2560,512]{1,0:T(8,128)(2,1)}, bf16[320,2560]{1,0:T(8,128)(2,1)})) %all-reduce.9.cloned.1.call-update) | async-done | bytes 4259856 | tf_op jit(solution)/shard_map/psum | solution.py:1032
  1080.4 3.5 add_convert_fusion.7
  1087.3 3.3 add_convert_fusion.6
  1092.5 34.1 %collective-permute-done.67.refs_6_ = bf16[640,512]{1,0:T(8,128)(2,1)S(1)} collective-permute-done((bf16[640,512]{1,0:T(8,128)(2,1)S(1)}, bf16[640,512]{1,0:T(8,128)(2,1)S(1)}, u32[]{:S(2)}, u32[]{:S(2)}) %collective-permute-start.67) | collective-permute-done | bytes 655392 | tf_op jit(solution)/shard_map/ppermute | solution.py:773
  1126.6 5.0 collective-permute-start.68
  1136.1 7.0 spread_gradients.3
  1144.7 5.3 fusion.24
  1150.0 94.3 %all-reduce.7.cloned.1.call-done.refs_0_ = bf16[864,2560]{1,0:T(8,128)(2,1)} async-done(((bf16[864,2560]{1,0:T(8,128)(2,1)}), bf16[864,2560]{1,0:T(8,128)(2,1)}) %all-reduce.7.cloned.1.call-update) | async-done | bytes 4423696 | tf_op jit(solution)/shard_map/psum | solution.py:1036
  1244.3 7.0 convert_element_type.383
  (418 shorter events, 190.1 us)
Async XLA Ops:
  14.2 71.2 %collective-permute-start.1 = (bf16[608,2560]{1,0:T(8,128)(2,1)}, bf16[608,2560]{1,0:T(8,128)(2,1)}, u32[]{:S(2)}, u32[]{:S(2)}) collective-permute-start(bf16[608,2560]{1,0:T(8,128)(2,1)} %pad_maximum_fusion.1.refs_0_), channel_id=1, source_target_pairs={{0,8},{4,20},{8,0},{12,28},{16,24},{20,4},{24,16},{28,12},{1,9},{5... | collective-permute-start | bytes 9338888 | tf_op jit(solution)/shard_map/ppermute | solution.py:728
  28.1 45.2 %collective-permute-start.2 = (bf16[2,320,512]{2,1,0:T(8,128)(2,1)}, bf16[2,320,512]{2,1,0:T(8,128)(2,1)S(1)}, u32[]{:S(2)}, u32[]{:S(2)}) collective-permute-start(bf16[2,320,512]{2,1,0:T(8,128)(2,1)} %get-tuple-element.87), channel_id=1, source_target_pairs={{0,8},{4,12},{8,0},{12,4},{16,24},{20,28},{24,16},{28,20},{1,9},{5... | collective-permute-start | bytes 1966088 | tf_op jit(solution)/shard_map/ppermute | solution.py:773
  28.1 45.2 %collective-permute-start.3 = (bf16[2,320,512]{2,1,0:T(8,128)(2,1)}, bf16[2,320,512]{2,1,0:T(8,128)(2,1)S(1)}, u32[]{:S(2)}, u32[]{:S(2)}) collective-permute-start(bf16[2,320,512]{2,1,0:T(8,128)(2,1)} %get-tuple-element.88), channel_id=1, source_target_pairs={{0,16},{4,20},{8,24},{12,28},{16,0},{20,4},{24,8},{28,12},{1,17},{... | collective-permute-start | bytes 1966088 | tf_op jit(solution)/shard_map/ppermute | solution.py:773
  30.1 51.8 %collective-permute-start.4 = (bf16[2,320,512]{2,1,0:T(8,128)(2,1)}, bf16[2,320,512]{2,1,0:T(8,128)(2,1)}, u32[]{:S(2)}, u32[]{:S(2)}) collective-permute-start(bf16[2,320,512]{2,1,0:T(8,128)(2,1)} %get-tuple-element.89), channel_id=1, source_target_pairs={{0,24},{4,28},{8,16},{12,20},{16,8},{20,12},{24,0},{28,4},{1,25},{... | collective-permute-start | bytes 1966088 | tf_op jit(solution)/shard_map/ppermute | solution.py:773
  85.3 15.6 %collective-permute-start.7 = (bf16[1280,512]{1,0:T(8,128)(2,1)}, bf16[1280,512]{1,0:T(8,128)(2,1)}, u32[]{:S(2)}, u32[]{:S(2)}) collective-permute-start(bf16[1280,512]{1,0:T(8,128)(2,1)} %pad_maximum_fusion.12), channel_id=1, source_target_pairs={{0,4},{4,0},{8,12},{12,8},{16,20},{20,16},{24,28},{28,24},{1,5},{5... | collective-permute-start | bytes 3932168 | tf_op jit(solution)/shard_map/ppermute | solution.py:724
  88.0 23.3 %collective-permute-start.9 = (bf16[304,2560]{1,0:T(8,128)(2,1)}, bf16[304,2560]{1,0:T(8,128)(2,1)}, u32[]{:S(2)}, u32[]{:S(2)}) collective-permute-start(bf16[304,2560]{1,0:T(8,128)(2,1)} %slice.168), channel_id=1, source_target_pairs={{0,16},{4,12},{8,24},{12,4},{16,0},{20,28},{24,8},{28,20},{1,17},{... | collective-permute-start | bytes 4669448 | tf_op jit(solution)/shard_map/ppermute | solution.py:732
  98.5 28.1 %collective-permute-start.8 = (bf16[608,2560]{1,0:T(8,128)(2,1)}, bf16[608,2560]{1,0:T(8,128)(2,1)}, u32[]{:S(2)}, u32[]{:S(2)}) collective-permute-start(bf16[608,2560]{1,0:T(8,128)(2,1)} %after.20.refs_0_.refs_4_), channel_id=1, source_target_pairs={{0,4},{4,0},{8,12},{12,8},{16,20},{20,16},{24,28},{28,24},{1,5},{5... | collective-permute-start | bytes 9338888 | tf_op jit(solution)/shard_map/ppermute | solution.py:724
  106.5 9.7 collective-permute-start.6
  106.5 76.4 %collective-permute-start.13 = (bf16[2,160,1792]{2,1,0:T(8,128)(2,1)}, bf16[2,160,1792]{2,1,0:T(8,128)(2,1)}, u32[]{:S(2)}, u32[]{:S(2)}) collective-permute-start(bf16[2,160,1792]{2,1,0:T(8,128)(2,1)} %get-tuple-element.103), channel_id=1, source_target_pairs={{0,24},{4,28},{8,16},{12,20},{16,8},{20,12},{24,0},{28,4},{1,25},{... | collective-permute-start | bytes 3440648 | tf_op jit(solution)/shard_map/ppermute | solution.py:773
  108.2 75.4 %collective-permute-start.11 = (bf16[2,320,1792]{2,1,0:T(8,128)(2,1)}, bf16[2,320,1792]{2,1,0:T(8,128)(2,1)}, u32[]{:S(2)}, u32[]{:S(2)}) collective-permute-start(bf16[2,320,1792]{2,1,0:T(8,128)(2,1)} %get-tuple-element.101), channel_id=1, source_target_pairs={{0,8},{4,12},{8,0},{12,4},{16,24},{20,28},{24,16},{28,20},{1,9},{5... | collective-permute-start | bytes 6881288 | tf_op jit(solution)/shard_map/ppermute | solution.py:773
  111.4 12.6 %collective-permute-start.10 = (bf16[304,2560]{1,0:T(8,128)(2,1)}, bf16[304,2560]{1,0:T(8,128)(2,1)}, u32[]{:S(2)}, u32[]{:S(2)}) collective-permute-start(bf16[304,2560]{1,0:T(8,128)(2,1)} %collective-permute-done.9), channel_id=1, source_target_pairs={{0,4},{4,0},{8,12},{12,8},{16,20},{20,16},{24,28},{28,24},{1,5},{5... | collective-permute-start | bytes 4669448 | tf_op jit(solution)/shard_map/ppermute | solution.py:724
  116.2 68.3 %collective-permute-start.12 = (bf16[2,320,1792]{2,1,0:T(8,128)(2,1)}, bf16[2,320,1792]{2,1,0:T(8,128)(2,1)}, u32[]{:S(2)}, u32[]{:S(2)}) collective-permute-start(bf16[2,320,1792]{2,1,0:T(8,128)(2,1)} %get-tuple-element.102), channel_id=1, source_target_pairs={{0,16},{4,20},{8,24},{12,28},{16,0},{20,4},{24,8},{28,12},{1,17},{... | collective-permute-start | bytes 6881288 | tf_op jit(solution)/shard_map/ppermute | solution.py:773
  187.5 9.0 collective-permute-start.14
  195.8 35.5 %collective-permute-start.16 = (bf16[304,2560]{1,0:T(8,128)(2,1)S(1)}, bf16[304,2560]{1,0:T(8,128)(2,1)S(1)}, u32[]{:S(2)}, u32[]{:S(2)}) collective-permute-start(bf16[304,2560]{1,0:T(8,128)(2,1)S(1)} %add_convert_fusion.17), channel_id=1, source_target_pairs={{0,16},{4,12},{8,24},{12,4},{16,0},{20,28},{24,8},{28,20},{1,17},{... | collective-permute-start | bytes 4669448 | tf_op jit(solution)/shard_map/ppermute | solution.py:732
  198.4 34.5 %collective-permute-start.18 = (bf16[304,2560]{1,0:T(8,128)(2,1)S(1)}, bf16[304,2560]{1,0:T(8,128)(2,1)S(1)}, u32[]{:S(2)}, u32[]{:S(2)}) collective-permute-start(bf16[304,2560]{1,0:T(8,128)(2,1)S(1)} %slice.174), channel_id=1, source_target_pairs={{0,8},{4,20},{8,0},{12,28},{16,24},{20,4},{24,16},{28,12},{1,9},{5... | collective-permute-start | bytes 4669448 | tf_op jit(solution)/shard_map/ppermute | solution.py:728
  232.8 20.6 %collective-permute-start.17 = (bf16[304,2560]{1,0:T(8,128)(2,1)}, bf16[304,2560]{1,0:T(8,128)(2,1)}, u32[]{:S(2)}, u32[]{:S(2)}) collective-permute-start(bf16[304,2560]{1,0:T(8,128)(2,1)} %add_convert_fusion.16), channel_id=1, source_target_pairs={{0,8},{4,20},{8,0},{12,28},{16,24},{20,4},{24,16},{28,12},{1,9},{5... | collective-permute-start | bytes 4669448 | tf_op jit(solution)/shard_map/ppermute | solution.py:728
  234.3 19.0 %collective-permute-start.19 = (bf16[304,2560]{1,0:T(8,128)(2,1)}, bf16[304,2560]{1,0:T(8,128)(2,1)}, u32[]{:S(2)}, u32[]{:S(2)}) collective-permute-start(bf16[304,2560]{1,0:T(8,128)(2,1)} %add_convert_fusion.15), channel_id=1, source_target_pairs={{0,4},{4,0},{8,12},{12,8},{16,20},{20,16},{24,28},{28,24},{1,5},{5... | collective-permute-start | bytes 4669448 | tf_op jit(solution)/shard_map/ppermute | solution.py:724
  235.5 27.9 %collective-permute-start.22 = (bf16[2,160,1792]{2,1,0:T(8,128)(2,1)}, bf16[2,160,1792]{2,1,0:T(8,128)(2,1)S(1)}, u32[]{:S(2)}, u32[]{:S(2)}) collective-permute-start(bf16[2,160,1792]{2,1,0:T(8,128)(2,1)} %get-tuple-element.104.refs_1_.refs_3_), channel_id=1, source_target_pairs={{0,1},{1,0},{2,3},{3,2},{4,5},{5,4},{6,7},{7,6},{8,9},{9,8},{10,11... | collective-permute-start | bytes 3440648 | tf_op jit(solution)/shard_map/ppermute | solution.py:798
  237.1 26.4 %collective-permute-start.21 = (bf16[304,2560]{1,0:T(8,128)(2,1)}, bf16[304,2560]{1,0:T(8,128)(2,1)S(1)}, u32[]{:S(2)}, u32[]{:S(2)}) collective-permute-start(bf16[304,2560]{1,0:T(8,128)(2,1)} %after.25), channel_id=1, source_target_pairs={{0,4},{4,0},{8,12},{12,8},{16,20},{20,16},{24,28},{28,24},{1,5},{5... | collective-permute-start | bytes 4669448 | tf_op jit(solution)/shard_map/ppermute | solution.py:724
  256.8 10.6 collective-permute-start.20
  263.4 8.5 collective-permute-start.23
  265.4 45.2 %collective-permute-start.25 = (bf16[608,2560]{1,0:T(8,128)(2,1)}, bf16[608,2560]{1,0:T(8,128)(2,1)}, u32[]{:S(2)}, u32[]{:S(2)}) collective-permute-start(bf16[608,2560]{1,0:T(8,128)(2,1)} %pad_maximum_fusion.4.down_far), channel_id=1, source_target_pairs={{0,8},{4,20},{8,0},{12,28},{16,24},{20,4},{24,16},{28,12},{1,9},{5... | collective-permute-start | bytes 9338888 | tf_op jit(solution)/shard_map/ppermute | solution.py:728
  269.3 66.7 %collective-permute-start.24 = (bf16[608,2560]{1,0:T(8,128)(2,1)}, bf16[608,2560]{1,0:T(8,128)(2,1)}, u32[]{:S(2)}, u32[]{:S(2)}) collective-permute-start(bf16[608,2560]{1,0:T(8,128)(2,1)} %pad_maximum_fusion.3.x_far), channel_id=1, source_target_pairs={{0,8},{4,20},{8,0},{12,28},{16,24},{20,4},{24,16},{28,12},{1,9},{5... | collective-permute-start | bytes 9338888 | tf_op jit(solution)/shard_map/ppermute | solution.py:728
  310.6 65.7 %collective-permute-start.27 = (bf16[608,2560]{1,0:T(8,128)(2,1)}, bf16[608,2560]{1,0:T(8,128)(2,1)}, u32[]{:S(2)}, u32[]{:S(2)}) collective-permute-start(bf16[608,2560]{1,0:T(8,128)(2,1)} %after.26.refs_1_.down_far), channel_id=1, source_target_pairs={{0,4},{4,0},{8,12},{12,8},{16,20},{20,16},{24,28},{28,24},{1,5},{5... | collective-permute-start | bytes 9338888 | tf_op jit(solution)/shard_map/ppermute | solution.py:724
  336.0 40.4 %collective-permute-start.26 = (bf16[608,2560]{1,0:T(8,128)(2,1)}, bf16[608,2560]{1,0:T(8,128)(2,1)}, u32[]{:S(2)}, u32[]{:S(2)}) collective-permute-start(bf16[608,2560]{1,0:T(8,128)(2,1)} %after.27.x_far), channel_id=1, source_target_pairs={{0,4},{4,0},{8,12},{12,8},{16,20},{20,16},{24,28},{28,24},{1,5},{5... | collective-permute-start | bytes 9338888 | tf_op jit(solution)/shard_map/ppermute | solution.py:724
  338.6 32.2 %collective-permute-start.29 = (bf16[304,2560]{1,0:T(8,128)(2,1)}, bf16[304,2560]{1,0:T(8,128)(2,1)S(1)}, u32[]{:S(2)}, u32[]{:S(2)}) collective-permute-start(bf16[304,2560]{1,0:T(8,128)(2,1)} %slice.177), channel_id=1, source_target_pairs={{0,16},{4,12},{8,24},{12,4},{16,0},{20,28},{24,8},{28,20},{1,17},{... | collective-permute-start | bytes 4669448 | tf_op jit(solution)/shard_map/ppermute | solution.py:732
  342.8 33.1 %collective-permute-start.28 = (bf16[304,2560]{1,0:T(8,128)(2,1)}, bf16[304,2560]{1,0:T(8,128)(2,1)}, u32[]{:S(2)}, u32[]{:S(2)}) collective-permute-start(bf16[304,2560]{1,0:T(8,128)(2,1)} %slice.176), channel_id=1, source_target_pairs={{0,16},{4,12},{8,24},{12,4},{16,0},{20,28},{24,8},{28,20},{1,17},{... | collective-permute-start | bytes 4669448 | tf_op jit(solution)/shard_map/ppermute | solution.py:732
  375.9 28.5 %collective-permute-start.30 = (bf16[304,2560]{1,0:T(8,128)(2,1)}, bf16[304,2560]{1,0:T(8,128)(2,1)}, u32[]{:S(2)}, u32[]{:S(2)}) collective-permute-start(bf16[304,2560]{1,0:T(8,128)(2,1)} %get-tuple-element.121), channel_id=1, source_target_pairs={{0,4},{4,0},{8,12},{12,8},{16,20},{20,16},{24,28},{28,24},{1,5},{5... | collective-permute-start | bytes 4669448 | tf_op jit(solution)/shard_map/ppermute | solution.py:724
  375.9 32.3 %collective-permute-start.31 = (bf16[304,2560]{1,0:T(8,128)(2,1)}, bf16[304,2560]{1,0:T(8,128)(2,1)S(1)}, u32[]{:S(2)}, u32[]{:S(2)}) collective-permute-start(bf16[304,2560]{1,0:T(8,128)(2,1)} %get-tuple-element.122), channel_id=1, source_target_pairs={{0,4},{4,0},{8,12},{12,8},{16,20},{20,16},{24,28},{28,24},{1,5},{5... | collective-permute-start | bytes 4669448 | tf_op jit(solution)/shard_map/ppermute | solution.py:724
  404.3 40.3 %collective-permute-start.32 = (bf16[608,2560]{1,0:T(8,128)(2,1)}, bf16[608,2560]{1,0:T(8,128)(2,1)}, u32[]{:S(2)}, u32[]{:S(2)}) collective-permute-start(bf16[608,2560]{1,0:T(8,128)(2,1)} %get-tuple-element.128), channel_id=1, source_target_pairs={{0,4},{4,0},{8,12},{12,8},{16,20},{20,16},{24,28},{28,24},{1,5},{5... | collective-permute-start | bytes 9338888 | tf_op jit(solution)/shard_map/ppermute | solution.py:724
  443.0 54.0 %collective-permute-start.34 = (bf16[304,2560]{1,0:T(8,128)(2,1)S(1)}, bf16[304,2560]{1,0:T(8,128)(2,1)}, u32[]{:S(2)}, u32[]{:S(2)}) collective-permute-start(bf16[304,2560]{1,0:T(8,128)(2,1)S(1)} %add_convert_fusion.14.refs_0_), channel_id=1, source_target_pairs={{0,16},{4,12},{8,24},{12,4},{16,0},{20,28},{24,8},{28,20},{1,17},{... | collective-permute-start | bytes 4669448 | tf_op jit(solution)/shard_map/ppermute | solution.py:732
  450.2 46.9 %collective-permute-start.35 = (bf16[304,2560]{1,0:T(8,128)(2,1)}, bf16[304,2560]{1,0:T(8,128)(2,1)}, u32[]{:S(2)}, u32[]{:S(2)}) collective-permute-start(bf16[304,2560]{1,0:T(8,128)(2,1)} %slice.179), channel_id=1, source_target_pairs={{0,8},{4,20},{8,0},{12,28},{16,24},{20,4},{24,16},{28,12},{1,9},{5... | collective-permute-start | bytes 4669448 | tf_op jit(solution)/shard_map/ppermute | solution.py:728
  497.0 421.2 %all-reduce.11.cloned.1.call-start = ((), (), s32[]{:S(2)}) async-start(), calls=%async_computation.2 | async-start | bytes 18350080 | tf_op jit(solution)/shard_map/psum | solution.py:996
  503.6 20.6 %collective-permute-start.36 = (bf16[304,2560]{1,0:T(8,128)(2,1)}, bf16[304,2560]{1,0:T(8,128)(2,1)}, u32[]{:S(2)}, u32[]{:S(2)}) collective-permute-start(bf16[304,2560]{1,0:T(8,128)(2,1)} %add_convert_fusion.13.refs_2_), channel_id=1, source_target_pairs={{0,8},{4,20},{8,0},{12,28},{16,24},{20,4},{24,16},{28,12},{1,9},{5... | collective-permute-start | bytes 4669448 | tf_op jit(solution)/shard_map/ppermute | solution.py:728
  538.4 37.1 %collective-permute-start.39 = (bf16[608,2560]{1,0:T(8,128)(2,1)S(1)}, bf16[608,2560]{1,0:T(8,128)(2,1)}, u32[]{:S(2)}, u32[]{:S(2)}) collective-permute-start(bf16[608,2560]{1,0:T(8,128)(2,1)S(1)} %pad_maximum_fusion.7.refs_0_), channel_id=1, source_target_pairs={{0,8},{4,20},{8,0},{12,28},{16,24},{20,4},{24,16},{28,12},{1,9},{5... | collective-permute-start | bytes 9338888 | tf_op jit(solution)/shard_map/ppermute | solution.py:728
  577.0 22.4 %collective-permute-start.41 = (bf16[304,2560]{1,0:T(8,128)(2,1)S(1)}, bf16[304,2560]{1,0:T(8,128)(2,1)}, u32[]{:S(2)}, u32[]{:S(2)}) collective-permute-start(bf16[304,2560]{1,0:T(8,128)(2,1)S(1)} %slice.180), channel_id=1, source_target_pairs={{0,16},{4,12},{8,24},{12,4},{16,0},{20,28},{24,8},{28,20},{1,17},{... | collective-permute-start | bytes 4669448 | tf_op jit(solution)/shard_map/ppermute | solution.py:732
  579.0 34.0 %collective-permute-start.40 = (bf16[608,2560]{1,0:T(8,128)(2,1)}, bf16[608,2560]{1,0:T(8,128)(2,1)}, u32[]{:S(2)}, u32[]{:S(2)}) collective-permute-start(bf16[608,2560]{1,0:T(8,128)(2,1)} %collective-permute-done.39), channel_id=1, source_target_pairs={{0,4},{4,0},{8,12},{12,8},{16,20},{20,16},{24,28},{28,24},{1,5},{5... | collective-permute-start | bytes 9338888 | tf_op jit(solution)/shard_map/ppermute | solution.py:724
  599.5 9.5 collective-permute-start.42
  600.0 480.4 %all-reduce.9.cloned.1.call-start = ((), (), s32[]{:S(2)}) async-start(), calls=%async_computation.1 | async-start | bytes 8519680 | tf_op jit(solution)/shard_map/psum | solution.py:1032
  680.9 19.6 %collective-permute-start.43 = (bf16[608,2560]{1,0:T(8,128)(2,1)}, bf16[608,2560]{1,0:T(8,128)(2,1)S(1)}, u32[]{:S(2)}, u32[]{:S(2)}) collective-permute-start(bf16[608,2560]{1,0:T(8,128)(2,1)} %convolution_convert_fusion.1), channel_id=1, source_target_pairs={{0,4},{4,0},{8,12},{12,8},{16,20},{20,16},{24,28},{28,24},{1,5},{5... | collective-permute-start | bytes 9338888 | tf_op jit(solution)/shard_map/ppermute | solution.py:724
  686.2 12.3 collective-permute-start.44
  700.4 36.4 %collective-permute-start.45 = (bf16[304,2560]{1,0:T(8,128)(2,1)S(1)}, bf16[304,2560]{1,0:T(8,128)(2,1)S(1)}, u32[]{:S(2)}, u32[]{:S(2)}) collective-permute-start(bf16[304,2560]{1,0:T(8,128)(2,1)S(1)} %add_convert_fusion.11), channel_id=1, source_target_pairs={{0,16},{4,12},{8,24},{12,4},{16,0},{20,28},{24,8},{28,20},{1,17},{... | collective-permute-start | bytes 4669448 | tf_op jit(solution)/shard_map/ppermute | solution.py:732
  701.4 35.9 %collective-permute-start.47 = (bf16[304,2560]{1,0:T(8,128)(2,1)S(1)}, bf16[304,2560]{1,0:T(8,128)(2,1)S(1)}, u32[]{:S(2)}, u32[]{:S(2)}) collective-permute-start(bf16[304,2560]{1,0:T(8,128)(2,1)S(1)} %slice.186), channel_id=1, source_target_pairs={{0,8},{4,20},{8,0},{12,28},{16,24},{20,4},{24,16},{28,12},{1,9},{5... | collective-permute-start | bytes 4669448 | tf_op jit(solution)/shard_map/ppermute | solution.py:728
  737.2 20.3 %collective-permute-start.46 = (bf16[304,2560]{1,0:T(8,128)(2,1)S(1)}, bf16[304,2560]{1,0:T(8,128)(2,1)S(1)}, u32[]{:S(2)}, u32[]{:S(2)}) collective-permute-start(bf16[304,2560]{1,0:T(8,128)(2,1)S(1)} %add_convert_fusion.10), channel_id=1, source_target_pairs={{0,8},{4,20},{8,0},{12,28},{16,24},{20,4},{24,16},{28,12},{1,9},{5... | collective-permute-start | bytes 4669448 | tf_op jit(solution)/shard_map/ppermute | solution.py:728
  737.7 19.8 %collective-permute-start.48 = (bf16[304,2560]{1,0:T(8,128)(2,1)S(1)}, bf16[304,2560]{1,0:T(8,128)(2,1)S(1)}, u32[]{:S(2)}, u32[]{:S(2)}) collective-permute-start(bf16[304,2560]{1,0:T(8,128)(2,1)S(1)} %add_convert_fusion.9), channel_id=1, source_target_pairs={{0,4},{4,0},{8,12},{12,8},{16,20},{20,16},{24,28},{28,24},{1,5},{5... | collective-permute-start | bytes 4669448 | tf_op jit(solution)/shard_map/ppermute | solution.py:724
  918.2 53.0 %collective-permute-start.56 = (bf16[640,1792]{1,0:T(8,128)(2,1)}, bf16[640,1792]{1,0:T(8,128)(2,1)}, u32[]{:S(2)}, u32[]{:S(2)}) collective-permute-start(bf16[640,1792]{1,0:T(8,128)(2,1)} %get-tuple-element.147.refs_3_), channel_id=1, source_target_pairs={{0,8},{4,12},{8,0},{12,4},{16,24},{20,28},{24,16},{28,20},{1,9},{5... | collective-permute-start | bytes 6881288 | tf_op jit(solution)/shard_map/ppermute | solution.py:773
  919.7 100.7 %collective-permute-start.58 = (bf16[640,1792]{1,0:T(8,128)(2,1)}, bf16[640,1792]{1,0:T(8,128)(2,1)}, u32[]{:S(2)}, u32[]{:S(2)}) collective-permute-start(bf16[640,1792]{1,0:T(8,128)(2,1)} %get-tuple-element.148.refs_4_), channel_id=1, source_target_pairs={{0,16},{4,20},{8,24},{12,28},{16,0},{20,4},{24,8},{28,12},{1,17},{... | collective-permute-start | bytes 6881288 | tf_op jit(solution)/shard_map/ppermute | solution.py:773
  921.2 99.3 %collective-permute-start.60 = (bf16[640,1792]{1,0:T(8,128)(2,1)}, bf16[640,1792]{1,0:T(8,128)(2,1)}, u32[]{:S(2)}, u32[]{:S(2)}) collective-permute-start(bf16[640,1792]{1,0:T(8,128)(2,1)} %get-tuple-element.149.refs_5_), channel_id=1, source_target_pairs={{0,24},{4,28},{8,16},{12,20},{16,8},{20,12},{24,0},{28,4},{1,25},{... | collective-permute-start | bytes 6881288 | tf_op jit(solution)/shard_map/ppermute | solution.py:773
  921.7 101.5 %collective-permute-start.49 = (bf16[608,2560]{1,0:T(8,128)(2,1)}, bf16[608,2560]{1,0:T(8,128)(2,1)}, u32[]{:S(2)}, u32[]{:S(2)}) collective-permute-start(bf16[608,2560]{1,0:T(8,128)(2,1)} %get-tuple-element.144), channel_id=1, source_target_pairs={{0,4},{4,0},{8,12},{12,8},{16,20},{20,16},{24,28},{28,24},{1,5},{5... | collective-permute-start | bytes 9338888 | tf_op jit(solution)/shard_map/ppermute | solution.py:724
  923.2 6.5 collective-permute-start.50
  923.8 320.5 %all-reduce.7.cloned.1.call-start = ((), (), s32[]{:S(2)}) async-start(), calls=%async_computation | async-start | bytes 8847360 | tf_op jit(solution)/shard_map/psum | solution.py:1036
  929.7 100.7 %collective-permute-start.55 = (bf16[640,1792]{1,0:T(8,128)(2,1)}, bf16[640,1792]{1,0:T(8,128)(2,1)S(1)}, u32[]{:S(2)}, u32[]{:S(2)}) collective-permute-start(bf16[640,1792]{1,0:T(8,128)(2,1)} %get-tuple-element.146.refs_2_.refs_0_), channel_id=1, source_target_pairs={{0,4},{4,0},{8,12},{12,8},{16,20},{20,16},{24,28},{28,24},{1,5},{5... | collective-permute-start | bytes 6881288 | tf_op jit(solution)/shard_map/ppermute | solution.py:724
  971.3 59.7 %collective-permute-start.57 = (bf16[640,1792]{1,0:T(8,128)(2,1)}, bf16[640,1792]{1,0:T(8,128)(2,1)S(1)}, u32[]{:S(2)}, u32[]{:S(2)}) collective-permute-start(bf16[640,1792]{1,0:T(8,128)(2,1)} %collective-permute-done.56.refs_2_), channel_id=1, source_target_pairs={{0,4},{4,0},{8,12},{12,8},{16,20},{20,16},{24,28},{28,24},{1,5},{5... | collective-permute-start | bytes 6881288 | tf_op jit(solution)/shard_map/ppermute | solution.py:724
  1020.5 10.5 collective-permute-start.59
  1020.5 10.5 collective-permute-start.61
  1023.3 57.2 %collective-permute-start.51 = (bf16[304,2560]{1,0:T(8,128)(2,1)S(1)}, bf16[304,2560]{1,0:T(8,128)(2,1)}, u32[]{:S(2)}, u32[]{:S(2)}) collective-permute-start(bf16[304,2560]{1,0:T(8,128)(2,1)S(1)} %add_convert_fusion.8), channel_id=1, source_target_pairs={{0,16},{4,12},{8,24},{12,4},{16,0},{20,28},{24,8},{28,20},{1,17},{... | collective-permute-start | bytes 4669448 | tf_op jit(solution)/shard_map/ppermute | solution.py:732
  1030.4 56.9 %collective-permute-start.53 = (bf16[304,2560]{1,0:T(8,128)(2,1)}, bf16[304,2560]{1,0:T(8,128)(2,1)}, u32[]{:S(2)}, u32[]{:S(2)}) collective-permute-start(bf16[304,2560]{1,0:T(8,128)(2,1)} %slice.188), channel_id=1, source_target_pairs={{0,8},{4,20},{8,0},{12,28},{16,24},{20,4},{24,16},{28,12},{1,9},{5... | collective-permute-start | bytes 4669448 | tf_op jit(solution)/shard_map/ppermute | solution.py:728
  1084.0 60.8 %collective-permute-start.52 = (bf16[304,2560]{1,0:T(8,128)(2,1)}, bf16[304,2560]{1,0:T(8,128)(2,1)}, u32[]{:S(2)}, u32[]{:S(2)}) collective-permute-start(bf16[304,2560]{1,0:T(8,128)(2,1)} %add_convert_fusion.7), channel_id=1, source_target_pairs={{0,8},{4,20},{8,0},{12,28},{16,24},{20,4},{24,16},{28,12},{1,9},{5... | collective-permute-start | bytes 4669448 | tf_op jit(solution)/shard_map/ppermute | solution.py:728
  1085.7 40.8 %collective-permute-start.67 = (bf16[640,512]{1,0:T(8,128)(2,1)S(1)}, bf16[640,512]{1,0:T(8,128)(2,1)S(1)}, u32[]{:S(2)}, u32[]{:S(2)}) collective-permute-start(bf16[640,512]{1,0:T(8,128)(2,1)S(1)} %get-tuple-element.173), channel_id=1, source_target_pairs={{0,24},{4,28},{8,16},{12,20},{16,8},{20,12},{24,0},{28,4},{1,25},{... | collective-permute-start | bytes 1966088 | tf_op jit(solution)/shard_map/ppermute | solution.py:773
  1090.6 54.2 %collective-permute-start.54 = (bf16[304,2560]{1,0:T(8,128)(2,1)}, bf16[304,2560]{1,0:T(8,128)(2,1)}, u32[]{:S(2)}, u32[]{:S(2)}) collective-permute-start(bf16[304,2560]{1,0:T(8,128)(2,1)} %add_convert_fusion.6), channel_id=1, source_target_pairs={{0,4},{4,0},{8,12},{12,8},{16,20},{20,16},{24,28},{28,24},{1,5},{5... | collective-permute-start | bytes 4669448 | tf_op jit(solution)/shard_map/ppermute | solution.py:724
  1090.6 36.0 %collective-permute-start.65 = (bf16[640,512]{1,0:T(8,128)(2,1)S(1)}, bf16[640,512]{1,0:T(8,128)(2,1)}, u32[]{:S(2)}, u32[]{:S(2)}) collective-permute-start(bf16[640,512]{1,0:T(8,128)(2,1)S(1)} %get-tuple-element.174), channel_id=1, source_target_pairs={{0,16},{4,20},{8,24},{12,28},{16,0},{20,4},{24,8},{28,12},{1,17},{... | collective-permute-start | bytes 1966088 | tf_op jit(solution)/shard_map/ppermute | solution.py:773
  1091.2 41.5 %collective-permute-start.63 = (bf16[640,512]{1,0:T(8,128)(2,1)S(1)}, bf16[640,512]{1,0:T(8,128)(2,1)}, u32[]{:S(2)}, u32[]{:S(2)}) collective-permute-start(bf16[640,512]{1,0:T(8,128)(2,1)S(1)} %get-tuple-element.175), channel_id=1, source_target_pairs={{0,8},{4,12},{8,0},{12,4},{16,24},{20,28},{24,16},{28,20},{1,9},{5... | collective-permute-start | bytes 1966088 | tf_op jit(solution)/shard_map/ppermute | solution.py:773
  1126.6 6.1 collective-permute-start.62
  1126.6 9.5 collective-permute-start.68
  (96 other events, 1141.5 us)
Sparse Core Ops, SparseCore 0:
  600.1 318.0 all-reduce.10
  923.9 156.3 all-reduce.8
  1082.9 161.3 all-reduce.6

commit v4 on v3

--- a/solution.py
+++ b/solution.py
@@ -993,7 +993,7 @@
         branch = low(middle_grad)
         chip_part = jnp.concatenate([branch, swap_core(branch)], axis=0)
         near_part = swap_near(chip_part)
-        hidden_sums = lax.psum(tuple(hidden_parts), "replica")
+        hidden_sums = lax.psum(after(hidden_parts, branch), "replica")
         side_part = swap_core(near_part)
         corner = swap_far(near_part[:row_count])
         index = jnp.zeros((1,), jnp.int32)

time: 1260 us -> 1260 us (level)
    unnamed x181 -> x191, local copies, waits for them, and re-layouts: 34 us -> 35.3 us
  transfers between devices with their start and end apart: 72 -> 72, of which waited for: 27 -> 26; matrix products, arithmetic and copies ran while one was open for 15% -> 15% of each run, Pallas kernels for 26% -> 26%
where the time goes in v4:
time: 1260 us
  waiting for transfers between devices  621 us (49%)
  Pallas kernels  326 us (26%)
  other arithmetic  92 us (7%)
  matrix products  85.4 us (7%)
  local copies, waits for them, and re-layouts  69 us (5%)
  starting transfers between devices  49.4 us (4%)
  between operations  15.4 us (1%)
    ppermute x12, waiting for transfers between devices, send(): return lax.ppermute(block, 'slot', [(i, i ^ way) for i in range(count)])  160 us
    psum x1, waiting for transfers between devices, shards(): hidden_sums = lax.psum(after(hidden_parts, branch), 'replica')  155 us
    pallas_call x4, Pallas kernels, dense(): pl.pallas_call(functools.partial(dense_kernel, chunk, len(held)), out_sha...  110 us
    psum x1, waiting for transfers between devices, shards(): grad_down = lax.psum(wait(grad_down, grad_heads), 'replica')  94.3 us
    ppermute x12, waiting for transfers between devices, swap_near(): lax.ppermute(values, 'slot', [(i, i ^ (4 if i % 2 else 2)) for i in range...  89.5 us
    pallas_call x5, Pallas kernels, product(): pl.pallas_call(functools.partial(product_kernel, first), grid_spec=pltpu....  64.7 us
    ppermute x8, waiting for transfers between devices, swap_far(): lax.ppermute(values, 'slot', [(i, i ^ (2 if i % 2 else 4)) for i in range...  62.3 us
    pallas_call x1, Pallas kernels, attend_backward(): pl.pallas_call(functools.partial(backward_kernel, group), out_shape=jax.S...  50.1 us
  transfers between devices with their start and end apart: 72, of which 26 were waited for; matrix products, arithmetic and copies ran while one was open for 15% of the time, Pallas kernels for 26%

profile of v4, /device:TPU:0, one launch (start us, length us, event | category | flops | bytes accessed | tf_op | source)
XLA Modules:
  0.0 1258.8 jit_solution(6129438417751149112)
XLA Ops:
  11.0 3.3 pad_maximum_fusion.1.refs_0_
  19.5 7.8 pack_weights.3
  31.6 12.7 %pack_weights.4 = (bf16[2,320,1792]{2,1,0:T(8,128)(2,1)S(1)}, bf16[2,320,1792]{2,1,0:T(8,128)(2,1)S(1)}, bf16[2,320,1792]{2,1,0:T(8,128)(2,1)}) custom-call(s32[2]{0:T(128)S(1)} %pad_add_fusion.1.spot, bf16[320,6912]{1,0:T(8,128)(2,1)} %refs_8_.2, bf16[320,6912]{1,0:T(8,128)(2,1)} %refs_9_.2), custom_call_target="tpu_custom_call" | custom-call | tf_op jit(solution)/shard_map/pack_weights/pallas_call | solution.py:492
  49.0 24.3 %collective-permute-done.2.refs_1_ = bf16[2,320,512]{2,1,0:T(8,128)(2,1)S(1)} collective-permute-done((bf16[2,320,512]{2,1,0:T(8,128)(2,1)}, bf16[2,320,512]{2,1,0:T(8,128)(2,1)S(1)}, u32[]{:S(2)}, u32[]{:S(2)}) %collective-permute-start.2) | collective-permute-done | bytes 655392 | tf_op jit(solution)/shard_map/ppermute | solution.py:773
  73.3 8.6 collective-permute-done.4.refs_3_
  90.4 4.3 pack_weights.5.refs_3_
  100.9 4.0 assemble_weights.2
  111.5 4.7 fusion.32
  120.3 3.7 fusion.36
  129.2 3.7 fusion.58
  132.9 4.0 fusion.28
  139.8 39.7 %tree_forward.1 = (bf16[8,304,320]{2,1,0:T(8,128)(2,1)S(1)}, bf16[9216,128]{1,0:T(8,128)(2,1)}, bf16[2304,128]{1,0:T(8,128)(2,1)S(1)}, bf16[2304,128]{1,0:T(8,128)(2,1)S(1)}, f32[18,1,512]{2,1,0:T(1,128)S(1)}) custom-call(s32[18]{0:T(128)S(1)} %pad_add_fusion.starts, s32[13]{0:T(128)S(1)} %bitcast.89, s32[8]{0:T(128)S(1)} %fusion.53.order, ...), custom_call_target="tpu_custom_call" | custom-call | tf_op jit(solution)/shard_map/tree_forward/pallas_call | solution.py:405
  190.1 5.4 collective-permute-done.15
  201.5 29.9 %collective-permute-done.16 = bf16[304,2560]{1,0:T(8,128)(2,1)S(1)} collective-permute-done((bf16[304,2560]{1,0:T(8,128)(2,1)S(1)}, bf16[304,2560]{1,0:T(8,128)(2,1)S(1)}, u32[]{:S(2)}, u32[]{:S(2)}) %collective-permute-start.16) | collective-permute-done | bytes 1556512 | tf_op jit(solution)/shard_map/ppermute | solution.py:732
  241.8 11.7 collective-permute-done.17
  259.4 4.0 collective-permute-done.22.refs_4_
  274.1 7.8 assemble_weights.3.w_far
  283.4 27.3 %dense.4 = (bf16[2432,2560]{1,0:T(8,128)(2,1)}, bf16[2432,2560]{1,0:T(8,128)(2,1)}, bf16[2432,896]{1,0:T(8,128)(2,1)}, bf16[2432,1792]{1,0:T(8,128)(2,1)}, bf16[...) custom-call(s32[8]{0:T(128)} %copy-done.20, bf16[608,2560]{1,0:T(8,128)(2,1)} %pad_maximum_fusion.3.x_far, ...), custom_call_target="tpu_custom_call" | custom-call | tf_op jit(solution)/shard_map/dense/pallas_call | solution.py:371
  310.9 25.2 %collective-permute-done.24.refs_0_ = bf16[608,2560]{1,0:T(8,128)(2,1)} collective-permute-done((bf16[608,2560]{1,0:T(8,128)(2,1)}, bf16[608,2560]{1,0:T(8,128)(2,1)}, u32[]{:S(2)}, u32[]{:S(2)}) %collective-permute-start.24) | collective-permute-done | bytes 3112992 | tf_op jit(solution)/shard_map/ppermute | solution.py:728
  343.4 27.5 %dense.5 = (bf16[2432,2560]{1,0:T(8,128)(2,1)}, bf16[2432,2560]{1,0:T(8,128)(2,1)}, bf16[2432,896]{1,0:T(8,128)(2,1)}, bf16[2432,1792]{1,0:T(8,128)(2,1)}, bf16[...) custom-call(s32[8]{0:T(128)} %copy-done.20, ...), custom_call_target="tpu_custom_call", output_to_operand_aliasing={{0}: (6, {}), {1}: (7, {}), {2}: (8, {}), {3}: (9, {})} | custom-call | tf_op jit(solution)/shard_map/dense/pallas_call | solution.py:371
  370.9 5.1 collective-permute-done.28.refs_0_
  376.5 27.8 %dense.6 = (bf16[2432,2560]{1,0:T(8,128)(2,1)}, bf16[2432,2560]{1,0:T(8,128)(2,1)}, bf16[2432,896]{1,0:T(8,128)(2,1)}, bf16[2432,1792]{1,0:T(8,128)(2,1)}, bf16[...) custom-call(s32[8]{0:T(128)} %copy-done.20, ...), custom_call_target="tpu_custom_call", output_to_operand_aliasing={{0}: (6, {}), {1}: (7, {}), {2}: (8, {}), {3}: (9, {})} | custom-call | tf_op jit(solution)/shard_map/dense/pallas_call | solution.py:371
  404.5 3.8 pad_maximum_fusion.5.x_far
  410.1 27.4 %dense.7 = (bf16[2432,2560]{1,0:T(8,128)(2,1)}, bf16[2432,2560]{1,0:T(8,128)(2,1)}, bf16[2432,896]{1,0:T(8,128)(2,1)}, bf16[2432,1792]{1,0:T(8,128)(2,1)}, bf16[...) custom-call(s32[8]{0:T(128)} %copy-done.20, ...), custom_call_target="tpu_custom_call", output_to_operand_aliasing={{0}: (6, {}), {1}: (7, {}), {2}: (8, {}), {3}: (9, {})} | custom-call | tf_op jit(solution)/shard_map/dense/pallas_call | solution.py:371
  450.8 10.5 product.5.refs_1_.refs_0_
  461.2 11.3 product.6.refs_1_
  472.6 11.3 product.7.refs_1_.refs_2_
  483.8 11.3 product.8.refs_2_.refs_3_
  496.5 3.5 add_convert_fusion.13.refs_2_
  506.7 17.0 %collective-permute-done.36.refs_0_ = bf16[304,2560]{1,0:T(8,128)(2,1)} collective-permute-done((bf16[304,2560]{1,0:T(8,128)(2,1)}, bf16[304,2560]{1,0:T(8,128)(2,1)}, u32[]{:S(2)}, u32[]{:S(2)}) %collective-permute-start.36) | collective-permute-done | bytes 1556512 | tf_op jit(solution)/shard_map/ppermute | solution.py:728
  523.7 4.4 multiply_reduce_fusion
  529.2 5.1 fusion.60
  534.3 3.4 collective-permute-done.38
  539.4 35.6 %collective-permute-done.39 = bf16[608,2560]{1,0:T(8,128)(2,1)} collective-permute-done((bf16[608,2560]{1,0:T(8,128)(2,1)S(1)}, bf16[608,2560]{1,0:T(8,128)(2,1)}, u32[]{:S(2)}, u32[]{:S(2)}) %collective-permute-start.39) | collective-permute-done | bytes 3112992 | tf_op jit(solution)/shard_map/ppermute | solution.py:728
  578.5 20.4 %product.9.refs_1_.refs_0_ = bf16[864,2560]{1,0:T(8,128)(2,1)} custom-call(s32[1]{0:T(128)} %constant.95.clone.1.index, bf16[2432,896]{1,0:T(8,128)(2,1)} %get-tuple-element.140.x, bf16[2432,2560]{1,0:T(8,128)(2,1)} %get-tuple-element.141.y, bf16[608,2560]{1,0:T(8,128)(2,1)S(1)} %pad_maximum_fusion.7.refs_0_), custom_call_target="tpu_custom_call" | custom-call | flops 1 | bytes 1 | tf_op jit(solution)/shard_map/product/pallas_call | solution.py:578
  602.1 3.6 convolution_convert_fusion.10
  605.7 4.7 convolution_convert_fusion.9
  610.3 3.6 fusion.25
  613.9 4.1 convolution_convert_fusion.8
  618.0 4.1 concatenate.63
  622.1 3.6 copy.86
  625.7 50.1 %tree_backward.1 = bf16[8,304,512]{2,1,0:T(8,128)(2,1)} custom-call(s32[18]{0:T(128)} %copy-done.24, s32[13]{0:T(128)} %bitcast.88, s32[8]{0:T(128)} %copy-done.20, bf16[8,304,320]{2,1,0:T(8,128)(2,1)} %bitcast.94, bf16[9216,128]{1,0:T(8,128)(2,1)} %get-tuple-element.142.q_keep, bf16[2304,128]{1,0:T(8,128)(2,1)} %copy-done.17, bf16[2304,128]{1,0:T(8,128)(2,1)} %copy-done.18, ...), custom_call_target="tpu_custom_call" | custom-call | flops 1 | bytes 1 | tf_op jit(solution)/shard_map/tree_backward/pallas_call | solution.py:433
  678.3 3.5 convolution_convert_fusion.1
  682.0 3.3 fusion.45
  694.9 4.3 fusion.30
  705.7 4.7 fusion.13.refs_6_.refs_1_
  710.3 27.4 %collective-permute-done.45 = bf16[304,2560]{1,0:T(8,128)(2,1)S(1)} collective-permute-done((bf16[304,2560]{1,0:T(8,128)(2,1)S(1)}, bf16[304,2560]{1,0:T(8,128)(2,1)S(1)}, u32[]{:S(2)}, u32[]{:S(2)}) %collective-permute-start.45) | collective-permute-done | bytes 1556512 | tf_op jit(solution)/shard_map/ppermute | solution.py:732
  739.2 4.3 fusion.34
  743.5 6.6 fusion.26
  750.2 8.3 add_convert_fusion.4.refs_5_.refs_0_
  763.4 155.4 %all-reduce.11.cloned.1.call-done = (bf16[640,1792]{1,0:T(8,128)(2,1)}, bf16[640,1792]{1,0:T(8,128)(2,1)}, bf16[640,1792]{1,0:T(8,128)(2,1)}, bf16[640,1792]{1,0:T(8,128)(2,1)}) async-done(((bf16[640,1792]{1,0:T(8,128)(2,1)}, bf16[640,1792]{1,0:T(8,128)(2,1)}, bf16[640,1792]{1,0:T(8,128)(2,1)}, bf16[640,1792]{1,0:T(8,128)(2,1)}), (bf16[640,1792]{1,0:T(8,128)(2,1)}, bf16[640,1792]{1,0:T(8,128)(2,1)}, ...) | async-done | bytes 9175056 | tf_op jit(solution)/shard_map/psum | solution.py:996
  924.5 5.8 collective-permute-done.50
  930.4 41.4 %collective-permute-done.56.refs_2_ = bf16[640,1792]{1,0:T(8,128)(2,1)} collective-permute-done((bf16[640,1792]{1,0:T(8,128)(2,1)}, bf16[640,1792]{1,0:T(8,128)(2,1)}, u32[]{:S(2)}, u32[]{:S(2)}) %collective-permute-start.56) | collective-permute-done | bytes 2293792 | tf_op jit(solution)/shard_map/ppermute | solution.py:773
  971.9 49.2 %collective-permute-done.58.refs_4_ = bf16[640,1792]{1,0:T(8,128)(2,1)} collective-permute-done((bf16[640,1792]{1,0:T(8,128)(2,1)}, bf16[640,1792]{1,0:T(8,128)(2,1)}, u32[]{:S(2)}, u32[]{:S(2)}) %collective-permute-start.58) | collective-permute-done | bytes 2293792 | tf_op jit(solution)/shard_map/ppermute | solution.py:773
  1033.1 16.8 %spread_gradients.2 = (f32[320,6912]{1,0:T(8,128)}, f32[320,6912]{1,0:T(8,128)}, f32[320,1]{1,0:T(8,128)}) custom-call(s32[1]{0:T(128)} %bitcast.4.me, bf16[640,1792]{1,0:T(8,128)(2,1)} %get-tuple-element.154.refs_2_.refs_0_, bf16[640,1792]{1,0:T(8,128)(2,1)} %copy-done.57, bf16[640,1792]{1,0:T(8,128)(2,1)} %collective-permute-done.56.refs_2_, ...), custom_call_target="tpu_custom_call" | custom-call | tf_op jit(solution)/shard_map/spread_gradients/pallas_call | solution.py:638
  1049.9 31.1 %all-reduce.9.cloned.1.call-done = (bf16[2560,512]{1,0:T(8,128)(2,1)}, bf16[320,2560]{1,0:T(8,128)(2,1)}) async-done(((bf16[2560,512]{1,0:T(8,128)(2,1)}, bf16[320,2560]{1,0:T(8,128)(2,1)}), (bf16[2560,512]{1,0:T(8,128)(2,1)}, bf16[320,2560]{1,0:T(8,128)(2,1)})) %all-reduce.9.cloned.1.call-update) | async-done | bytes 4259856 | tf_op jit(solution)/shard_map/psum | solution.py:1032
  1081.0 3.5 add_convert_fusion.7
  1087.9 3.3 add_convert_fusion.6
  1093.1 34.1 %collective-permute-done.67.refs_6_ = bf16[640,512]{1,0:T(8,128)(2,1)S(1)} collective-permute-done((bf16[640,512]{1,0:T(8,128)(2,1)S(1)}, bf16[640,512]{1,0:T(8,128)(2,1)S(1)}, u32[]{:S(2)}, u32[]{:S(2)}) %collective-permute-start.67) | collective-permute-done | bytes 655392 | tf_op jit(solution)/shard_map/ppermute | solution.py:773
  1127.2 5.0 collective-permute-start.68
  1136.7 7.0 spread_gradients.3
  1145.3 5.3 fusion.24
  1150.6 94.3 %all-reduce.7.cloned.1.call-done.refs_0_ = bf16[864,2560]{1,0:T(8,128)(2,1)} async-done(((bf16[864,2560]{1,0:T(8,128)(2,1)}), bf16[864,2560]{1,0:T(8,128)(2,1)}) %all-reduce.7.cloned.1.call-update) | async-done | bytes 4423696 | tf_op jit(solution)/shard_map/psum | solution.py:1036
  1244.9 7.0 convert_element_type.383
  (429 shorter events, 190.6 us)
Async XLA Ops:
  7.2 911.6 %all-reduce.11.cloned.1.call-start = ((), (), s32[]{:S(2)}) async-start(), calls=%async_computation.2 | async-start | bytes 18350080 | tf_op jit(solution)/shard_map/psum | solution.py:996
  14.3 71.2 %collective-permute-start.1 = (bf16[608,2560]{1,0:T(8,128)(2,1)}, bf16[608,2560]{1,0:T(8,128)(2,1)}, u32[]{:S(2)}, u32[]{:S(2)}) collective-permute-start(bf16[608,2560]{1,0:T(8,128)(2,1)} %pad_maximum_fusion.1.refs_0_), channel_id=1, source_target_pairs={{0,8},{4,20},{8,0},{12,28},{16,24},{20,4},{24,16},{28,12},{1,9},{5... | collective-permute-start | bytes 9338888 | tf_op jit(solution)/shard_map/ppermute | solution.py:728
  28.1 45.2 %collective-permute-start.2 = (bf16[2,320,512]{2,1,0:T(8,128)(2,1)}, bf16[2,320,512]{2,1,0:T(8,128)(2,1)S(1)}, u32[]{:S(2)}, u32[]{:S(2)}) collective-permute-start(bf16[2,320,512]{2,1,0:T(8,128)(2,1)} %get-tuple-element.91), channel_id=1, source_target_pairs={{0,8},{4,12},{8,0},{12,4},{16,24},{20,28},{24,16},{28,20},{1,9},{5... | collective-permute-start | bytes 1966088 | tf_op jit(solution)/shard_map/ppermute | solution.py:773
  28.1 45.2 %collective-permute-start.3 = (bf16[2,320,512]{2,1,0:T(8,128)(2,1)}, bf16[2,320,512]{2,1,0:T(8,128)(2,1)S(1)}, u32[]{:S(2)}, u32[]{:S(2)}) collective-permute-start(bf16[2,320,512]{2,1,0:T(8,128)(2,1)} %get-tuple-element.92), channel_id=1, source_target_pairs={{0,16},{4,20},{8,24},{12,28},{16,0},{20,4},{24,8},{28,12},{1,17},{... | collective-permute-start | bytes 1966088 | tf_op jit(solution)/shard_map/ppermute | solution.py:773
  30.2 51.8 %collective-permute-start.4 = (bf16[2,320,512]{2,1,0:T(8,128)(2,1)}, bf16[2,320,512]{2,1,0:T(8,128)(2,1)}, u32[]{:S(2)}, u32[]{:S(2)}) collective-permute-start(bf16[2,320,512]{2,1,0:T(8,128)(2,1)} %get-tuple-element.93), channel_id=1, source_target_pairs={{0,24},{4,28},{8,16},{12,20},{16,8},{20,12},{24,0},{28,4},{1,25},{... | collective-permute-start | bytes 1966088 | tf_op jit(solution)/shard_map/ppermute | solution.py:773
  85.3 15.6 %collective-permute-start.7 = (bf16[1280,512]{1,0:T(8,128)(2,1)}, bf16[1280,512]{1,0:T(8,128)(2,1)}, u32[]{:S(2)}, u32[]{:S(2)}) collective-permute-start(bf16[1280,512]{1,0:T(8,128)(2,1)} %pad_maximum_fusion.12), channel_id=1, source_target_pairs={{0,4},{4,0},{8,12},{12,8},{16,20},{20,16},{24,28},{28,24},{1,5},{5... | collective-permute-start | bytes 3932168 | tf_op jit(solution)/shard_map/ppermute | solution.py:724
  88.1 23.3 %collective-permute-start.9 = (bf16[304,2560]{1,0:T(8,128)(2,1)}, bf16[304,2560]{1,0:T(8,128)(2,1)}, u32[]{:S(2)}, u32[]{:S(2)}) collective-permute-start(bf16[304,2560]{1,0:T(8,128)(2,1)} %slice.168), channel_id=1, source_target_pairs={{0,16},{4,12},{8,24},{12,4},{16,0},{20,28},{24,8},{28,20},{1,17},{... | collective-permute-start | bytes 4669448 | tf_op jit(solution)/shard_map/ppermute | solution.py:732
  98.5 28.1 %collective-permute-start.8 = (bf16[608,2560]{1,0:T(8,128)(2,1)}, bf16[608,2560]{1,0:T(8,128)(2,1)}, u32[]{:S(2)}, u32[]{:S(2)}) collective-permute-start(bf16[608,2560]{1,0:T(8,128)(2,1)} %after.21.refs_0_.refs_4_), channel_id=1, source_target_pairs={{0,4},{4,0},{8,12},{12,8},{16,20},{20,16},{24,28},{28,24},{1,5},{5... | collective-permute-start | bytes 9338888 | tf_op jit(solution)/shard_map/ppermute | solution.py:724
  106.5 9.7 collective-permute-start.6
  106.6 76.4 %collective-permute-start.13 = (bf16[2,160,1792]{2,1,0:T(8,128)(2,1)}, bf16[2,160,1792]{2,1,0:T(8,128)(2,1)}, u32[]{:S(2)}, u32[]{:S(2)}) collective-permute-start(bf16[2,160,1792]{2,1,0:T(8,128)(2,1)} %get-tuple-element.107), channel_id=1, source_target_pairs={{0,24},{4,28},{8,16},{12,20},{16,8},{20,12},{24,0},{28,4},{1,25},{... | collective-permute-start | bytes 3440648 | tf_op jit(solution)/shard_map/ppermute | solution.py:773
  108.3 75.4 %collective-permute-start.11 = (bf16[2,320,1792]{2,1,0:T(8,128)(2,1)}, bf16[2,320,1792]{2,1,0:T(8,128)(2,1)}, u32[]{:S(2)}, u32[]{:S(2)}) collective-permute-start(bf16[2,320,1792]{2,1,0:T(8,128)(2,1)} %get-tuple-element.105), channel_id=1, source_target_pairs={{0,8},{4,12},{8,0},{12,4},{16,24},{20,28},{24,16},{28,20},{1,9},{5... | collective-permute-start | bytes 6881288 | tf_op jit(solution)/shard_map/ppermute | solution.py:773
  111.4 12.6 collective-permute-start.10
  116.3 68.3 %collective-permute-start.12 = (bf16[2,320,1792]{2,1,0:T(8,128)(2,1)}, bf16[2,320,1792]{2,1,0:T(8,128)(2,1)}, u32[]{:S(2)}, u32[]{:S(2)}) collective-permute-start(bf16[2,320,1792]{2,1,0:T(8,128)(2,1)} %get-tuple-element.106), channel_id=1, source_target_pairs={{0,16},{4,20},{8,24},{12,28},{16,0},{20,4},{24,8},{28,12},{1,17},{... | collective-permute-start | bytes 6881288 | tf_op jit(solution)/shard_map/ppermute | solution.py:773
  187.5 9.0 collective-permute-start.14
  195.8 35.6 %collective-permute-start.16 = (bf16[304,2560]{1,0:T(8,128)(2,1)S(1)}, bf16[304,2560]{1,0:T(8,128)(2,1)S(1)}, u32[]{:S(2)}, u32[]{:S(2)}) collective-permute-start(bf16[304,2560]{1,0:T(8,128)(2,1)S(1)} %add_convert_fusion.17), channel_id=1, source_target_pairs={{0,16},{4,12},{8,24},{12,4},{16,0},{20,28},{24,8},{28,20},{1,17},{... | collective-permute-start | bytes 4669448 | tf_op jit(solution)/shard_map/ppermute | solution.py:732
  198.4 34.5 %collective-permute-start.18 = (bf16[304,2560]{1,0:T(8,128)(2,1)S(1)}, bf16[304,2560]{1,0:T(8,128)(2,1)S(1)}, u32[]{:S(2)}, u32[]{:S(2)}) collective-permute-start(bf16[304,2560]{1,0:T(8,128)(2,1)S(1)} %slice.174), channel_id=1, source_target_pairs={{0,8},{4,20},{8,0},{12,28},{16,24},{20,4},{24,16},{28,12},{1,9},{5... | collective-permute-start | bytes 4669448 | tf_op jit(solution)/shard_map/ppermute | solution.py:728
  232.9 20.6 %collective-permute-start.17 = (bf16[304,2560]{1,0:T(8,128)(2,1)}, bf16[304,2560]{1,0:T(8,128)(2,1)}, u32[]{:S(2)}, u32[]{:S(2)}) collective-permute-start(bf16[304,2560]{1,0:T(8,128)(2,1)} %add_convert_fusion.16), channel_id=1, source_target_pairs={{0,8},{4,20},{8,0},{12,28},{16,24},{20,4},{24,16},{28,12},{1,9},{5... | collective-permute-start | bytes 4669448 | tf_op jit(solution)/shard_map/ppermute | solution.py:728
  234.4 19.0 %collective-permute-start.19 = (bf16[304,2560]{1,0:T(8,128)(2,1)}, bf16[304,2560]{1,0:T(8,128)(2,1)}, u32[]{:S(2)}, u32[]{:S(2)}) collective-permute-start(bf16[304,2560]{1,0:T(8,128)(2,1)} %add_convert_fusion.15), channel_id=1, source_target_pairs={{0,4},{4,0},{8,12},{12,8},{16,20},{20,16},{24,28},{28,24},{1,5},{5... | collective-permute-start | bytes 4669448 | tf_op jit(solution)/shard_map/ppermute | solution.py:724
  235.6 27.9 %collective-permute-start.22 = (bf16[2,160,1792]{2,1,0:T(8,128)(2,1)}, bf16[2,160,1792]{2,1,0:T(8,128)(2,1)S(1)}, u32[]{:S(2)}, u32[]{:S(2)}) collective-permute-start(bf16[2,160,1792]{2,1,0:T(8,128)(2,1)} %get-tuple-element.108.refs_1_.refs_3_), channel_id=1, source_target_pairs={{0,1},{1,0},{2,3},{3,2},{4,5},{5,4},{6,7},{7,6},{8,9},{9,8},{10,11... | collective-permute-start | bytes 3440648 | tf_op jit(solution)/shard_map/ppermute | solution.py:798
  237.1 26.5 %collective-permute-start.21 = (bf16[304,2560]{1,0:T(8,128)(2,1)}, bf16[304,2560]{1,0:T(8,128)(2,1)S(1)}, u32[]{:S(2)}, u32[]{:S(2)}) collective-permute-start(bf16[304,2560]{1,0:T(8,128)(2,1)} %after.26), channel_id=1, source_target_pairs={{0,4},{4,0},{8,12},{12,8},{16,20},{20,16},{24,28},{28,24},{1,5},{5... | collective-permute-start | bytes 4669448 | tf_op jit(solution)/shard_map/ppermute | solution.py:724
  256.9 10.6 collective-permute-start.20
  263.5 8.5 collective-permute-start.23
  265.5 45.3 %collective-permute-start.25 = (bf16[608,2560]{1,0:T(8,128)(2,1)}, bf16[608,2560]{1,0:T(8,128)(2,1)}, u32[]{:S(2)}, u32[]{:S(2)}) collective-permute-start(bf16[608,2560]{1,0:T(8,128)(2,1)} %pad_maximum_fusion.4.down_far), channel_id=1, source_target_pairs={{0,8},{4,20},{8,0},{12,28},{16,24},{20,4},{24,16},{28,12},{1,9},{5... | collective-permute-start | bytes 9338888 | tf_op jit(solution)/shard_map/ppermute | solution.py:728
  269.4 66.7 %collective-permute-start.24 = (bf16[608,2560]{1,0:T(8,128)(2,1)}, bf16[608,2560]{1,0:T(8,128)(2,1)}, u32[]{:S(2)}, u32[]{:S(2)}) collective-permute-start(bf16[608,2560]{1,0:T(8,128)(2,1)} %pad_maximum_fusion.3.x_far), channel_id=1, source_target_pairs={{0,8},{4,20},{8,0},{12,28},{16,24},{20,4},{24,16},{28,12},{1,9},{5... | collective-permute-start | bytes 9338888 | tf_op jit(solution)/shard_map/ppermute | solution.py:728
  310.8 65.7 %collective-permute-start.27 = (bf16[608,2560]{1,0:T(8,128)(2,1)}, bf16[608,2560]{1,0:T(8,128)(2,1)}, u32[]{:S(2)}, u32[]{:S(2)}) collective-permute-start(bf16[608,2560]{1,0:T(8,128)(2,1)} %after.27.refs_1_.down_far), channel_id=1, source_target_pairs={{0,4},{4,0},{8,12},{12,8},{16,20},{20,16},{24,28},{28,24},{1,5},{5... | collective-permute-start | bytes 9338888 | tf_op jit(solution)/shard_map/ppermute | solution.py:724
  336.1 40.4 %collective-permute-start.26 = (bf16[608,2560]{1,0:T(8,128)(2,1)}, bf16[608,2560]{1,0:T(8,128)(2,1)}, u32[]{:S(2)}, u32[]{:S(2)}) collective-permute-start(bf16[608,2560]{1,0:T(8,128)(2,1)} %after.28.x_far), channel_id=1, source_target_pairs={{0,4},{4,0},{8,12},{12,8},{16,20},{20,16},{24,28},{28,24},{1,5},{5... | collective-permute-start | bytes 9338888 | tf_op jit(solution)/shard_map/ppermute | solution.py:724
  338.7 32.2 %collective-permute-start.29 = (bf16[304,2560]{1,0:T(8,128)(2,1)}, bf16[304,2560]{1,0:T(8,128)(2,1)S(1)}, u32[]{:S(2)}, u32[]{:S(2)}) collective-permute-start(bf16[304,2560]{1,0:T(8,128)(2,1)} %slice.177), channel_id=1, source_target_pairs={{0,16},{4,12},{8,24},{12,4},{16,0},{20,28},{24,8},{28,20},{1,17},{... | collective-permute-start | bytes 4669448 | tf_op jit(solution)/shard_map/ppermute | solution.py:732
  342.9 33.1 %collective-permute-start.28 = (bf16[304,2560]{1,0:T(8,128)(2,1)}, bf16[304,2560]{1,0:T(8,128)(2,1)}, u32[]{:S(2)}, u32[]{:S(2)}) collective-permute-start(bf16[304,2560]{1,0:T(8,128)(2,1)} %slice.176), channel_id=1, source_target_pairs={{0,16},{4,12},{8,24},{12,4},{16,0},{20,28},{24,8},{28,20},{1,17},{... | collective-permute-start | bytes 4669448 | tf_op jit(solution)/shard_map/ppermute | solution.py:732
  376.0 28.5 %collective-permute-start.30 = (bf16[304,2560]{1,0:T(8,128)(2,1)}, bf16[304,2560]{1,0:T(8,128)(2,1)}, u32[]{:S(2)}, u32[]{:S(2)}) collective-permute-start(bf16[304,2560]{1,0:T(8,128)(2,1)} %get-tuple-element.125), channel_id=1, source_target_pairs={{0,4},{4,0},{8,12},{12,8},{16,20},{20,16},{24,28},{28,24},{1,5},{5... | collective-permute-start | bytes 4669448 | tf_op jit(solution)/shard_map/ppermute | solution.py:724
  376.0 32.3 %collective-permute-start.31 = (bf16[304,2560]{1,0:T(8,128)(2,1)}, bf16[304,2560]{1,0:T(8,128)(2,1)S(1)}, u32[]{:S(2)}, u32[]{:S(2)}) collective-permute-start(bf16[304,2560]{1,0:T(8,128)(2,1)} %get-tuple-element.126), channel_id=1, source_target_pairs={{0,4},{4,0},{8,12},{12,8},{16,20},{20,16},{24,28},{28,24},{1,5},{5... | collective-permute-start | bytes 4669448 | tf_op jit(solution)/shard_map/ppermute | solution.py:724
  404.4 40.3 %collective-permute-start.32 = (bf16[608,2560]{1,0:T(8,128)(2,1)}, bf16[608,2560]{1,0:T(8,128)(2,1)}, u32[]{:S(2)}, u32[]{:S(2)}) collective-permute-start(bf16[608,2560]{1,0:T(8,128)(2,1)} %get-tuple-element.132), channel_id=1, source_target_pairs={{0,4},{4,0},{8,12},{12,8},{16,20},{20,16},{24,28},{28,24},{1,5},{5... | collective-permute-start | bytes 9338888 | tf_op jit(solution)/shard_map/ppermute | solution.py:724
  443.1 53.5 %collective-permute-start.34 = (bf16[304,2560]{1,0:T(8,128)(2,1)S(1)}, bf16[304,2560]{1,0:T(8,128)(2,1)}, u32[]{:S(2)}, u32[]{:S(2)}) collective-permute-start(bf16[304,2560]{1,0:T(8,128)(2,1)S(1)} %add_convert_fusion.14.refs_0_), channel_id=1, source_target_pairs={{0,16},{4,12},{8,24},{12,4},{16,0},{20,28},{24,8},{28,20},{1,17},{... | collective-permute-start | bytes 4669448 | tf_op jit(solution)/shard_map/ppermute | solution.py:732
  450.2 46.3 %collective-permute-start.35 = (bf16[304,2560]{1,0:T(8,128)(2,1)}, bf16[304,2560]{1,0:T(8,128)(2,1)}, u32[]{:S(2)}, u32[]{:S(2)}) collective-permute-start(bf16[304,2560]{1,0:T(8,128)(2,1)} %slice.179), channel_id=1, source_target_pairs={{0,8},{4,20},{8,0},{12,28},{16,24},{20,4},{24,16},{28,12},{1,9},{5... | collective-permute-start | bytes 4669448 | tf_op jit(solution)/shard_map/ppermute | solution.py:728
  503.1 20.6 %collective-permute-start.36 = (bf16[304,2560]{1,0:T(8,128)(2,1)}, bf16[304,2560]{1,0:T(8,128)(2,1)}, u32[]{:S(2)}, u32[]{:S(2)}) collective-permute-start(bf16[304,2560]{1,0:T(8,128)(2,1)} %add_convert_fusion.13.refs_2_), channel_id=1, source_target_pairs={{0,8},{4,20},{8,0},{12,28},{16,24},{20,4},{24,16},{28,12},{1,9},{5... | collective-permute-start | bytes 4669448 | tf_op jit(solution)/shard_map/ppermute | solution.py:728
  537.9 37.1 %collective-permute-start.39 = (bf16[608,2560]{1,0:T(8,128)(2,1)S(1)}, bf16[608,2560]{1,0:T(8,128)(2,1)}, u32[]{:S(2)}, u32[]{:S(2)}) collective-permute-start(bf16[608,2560]{1,0:T(8,128)(2,1)S(1)} %pad_maximum_fusion.7.refs_0_), channel_id=1, source_target_pairs={{0,8},{4,20},{8,0},{12,28},{16,24},{20,4},{24,16},{28,12},{1,9},{5... | collective-permute-start | bytes 9338888 | tf_op jit(solution)/shard_map/ppermute | solution.py:728
  576.5 22.4 %collective-permute-start.41 = (bf16[304,2560]{1,0:T(8,128)(2,1)S(1)}, bf16[304,2560]{1,0:T(8,128)(2,1)S(1)}, u32[]{:S(2)}, u32[]{:S(2)}) collective-permute-start(bf16[304,2560]{1,0:T(8,128)(2,1)S(1)} %slice.180), channel_id=1, source_target_pairs={{0,16},{4,12},{8,24},{12,4},{16,0},{20,28},{24,8},{28,20},{1,17},{... | collective-permute-start | bytes 4669448 | tf_op jit(solution)/shard_map/ppermute | solution.py:732
  578.5 35.4 %collective-permute-start.40 = (bf16[608,2560]{1,0:T(8,128)(2,1)}, bf16[608,2560]{1,0:T(8,128)(2,1)}, u32[]{:S(2)}, u32[]{:S(2)}) collective-permute-start(bf16[608,2560]{1,0:T(8,128)(2,1)} %collective-permute-done.39), channel_id=1, source_target_pairs={{0,4},{4,0},{8,12},{12,8},{16,20},{20,16},{24,28},{28,24},{1,5},{5... | collective-permute-start | bytes 9338888 | tf_op jit(solution)/shard_map/ppermute | solution.py:724
  600.1 10.2 collective-permute-start.42
  600.7 480.3 %all-reduce.9.cloned.1.call-start = ((), (), s32[]{:S(2)}) async-start(), calls=%async_computation.1 | async-start | bytes 8519680 | tf_op jit(solution)/shard_map/psum | solution.py:1032
  681.8 19.3 %collective-permute-start.43 = (bf16[608,2560]{1,0:T(8,128)(2,1)}, bf16[608,2560]{1,0:T(8,128)(2,1)S(1)}, u32[]{:S(2)}, u32[]{:S(2)}) collective-permute-start(bf16[608,2560]{1,0:T(8,128)(2,1)} %convolution_convert_fusion.1), channel_id=1, source_target_pairs={{0,4},{4,0},{8,12},{12,8},{16,20},{20,16},{24,28},{28,24},{1,5},{5... | collective-permute-start | bytes 9338888 | tf_op jit(solution)/shard_map/ppermute | solution.py:724
  687.3 11.9 collective-permute-start.44
  701.0 36.7 %collective-permute-start.45 = (bf16[304,2560]{1,0:T(8,128)(2,1)S(1)}, bf16[304,2560]{1,0:T(8,128)(2,1)S(1)}, u32[]{:S(2)}, u32[]{:S(2)}) collective-permute-start(bf16[304,2560]{1,0:T(8,128)(2,1)S(1)} %add_convert_fusion.11), channel_id=1, source_target_pairs={{0,16},{4,12},{8,24},{12,4},{16,0},{20,28},{24,8},{28,20},{1,17},{... | collective-permute-start | bytes 4669448 | tf_op jit(solution)/shard_map/ppermute | solution.py:732
  702.0 36.2 %collective-permute-start.47 = (bf16[304,2560]{1,0:T(8,128)(2,1)S(1)}, bf16[304,2560]{1,0:T(8,128)(2,1)S(1)}, u32[]{:S(2)}, u32[]{:S(2)}) collective-permute-start(bf16[304,2560]{1,0:T(8,128)(2,1)S(1)} %slice.186), channel_id=1, source_target_pairs={{0,8},{4,20},{8,0},{12,28},{16,24},{20,4},{24,16},{28,12},{1,9},{5... | collective-permute-start | bytes 4669448 | tf_op jit(solution)/shard_map/ppermute | solution.py:728
  738.1 20.3 %collective-permute-start.46 = (bf16[304,2560]{1,0:T(8,128)(2,1)S(1)}, bf16[304,2560]{1,0:T(8,128)(2,1)S(1)}, u32[]{:S(2)}, u32[]{:S(2)}) collective-permute-start(bf16[304,2560]{1,0:T(8,128)(2,1)S(1)} %add_convert_fusion.10), channel_id=1, source_target_pairs={{0,8},{4,20},{8,0},{12,28},{16,24},{20,4},{24,16},{28,12},{1,9},{5... | collective-permute-start | bytes 4669448 | tf_op jit(solution)/shard_map/ppermute | solution.py:728
  738.6 19.8 %collective-permute-start.48 = (bf16[304,2560]{1,0:T(8,128)(2,1)S(1)}, bf16[304,2560]{1,0:T(8,128)(2,1)S(1)}, u32[]{:S(2)}, u32[]{:S(2)}) collective-permute-start(bf16[304,2560]{1,0:T(8,128)(2,1)S(1)} %add_convert_fusion.9), channel_id=1, source_target_pairs={{0,4},{4,0},{8,12},{12,8},{16,20},{20,16},{24,28},{28,24},{1,5},{5... | collective-permute-start | bytes 4669448 | tf_op jit(solution)/shard_map/ppermute | solution.py:724
  918.8 53.0 %collective-permute-start.56 = (bf16[640,1792]{1,0:T(8,128)(2,1)}, bf16[640,1792]{1,0:T(8,128)(2,1)}, u32[]{:S(2)}, u32[]{:S(2)}) collective-permute-start(bf16[640,1792]{1,0:T(8,128)(2,1)} %get-tuple-element.155.refs_3_), channel_id=1, source_target_pairs={{0,8},{4,12},{8,0},{12,4},{16,24},{20,28},{24,16},{28,20},{1,9},{5... | collective-permute-start | bytes 6881288 | tf_op jit(solution)/shard_map/ppermute | solution.py:773
  920.3 100.7 %collective-permute-start.58 = (bf16[640,1792]{1,0:T(8,128)(2,1)}, bf16[640,1792]{1,0:T(8,128)(2,1)}, u32[]{:S(2)}, u32[]{:S(2)}) collective-permute-start(bf16[640,1792]{1,0:T(8,128)(2,1)} %get-tuple-element.156.refs_4_), channel_id=1, source_target_pairs={{0,16},{4,20},{8,24},{12,28},{16,0},{20,4},{24,8},{28,12},{1,17},{... | collective-permute-start | bytes 6881288 | tf_op jit(solution)/shard_map/ppermute | solution.py:773
  921.8 99.3 %collective-permute-start.60 = (bf16[640,1792]{1,0:T(8,128)(2,1)}, bf16[640,1792]{1,0:T(8,128)(2,1)}, u32[]{:S(2)}, u32[]{:S(2)}) collective-permute-start(bf16[640,1792]{1,0:T(8,128)(2,1)} %get-tuple-element.157.refs_5_), channel_id=1, source_target_pairs={{0,24},{4,28},{8,16},{12,20},{16,8},{20,12},{24,0},{28,4},{1,25},{... | collective-permute-start | bytes 6881288 | tf_op jit(solution)/shard_map/ppermute | solution.py:773
  922.3 101.5 %collective-permute-start.49 = (bf16[608,2560]{1,0:T(8,128)(2,1)}, bf16[608,2560]{1,0:T(8,128)(2,1)}, u32[]{:S(2)}, u32[]{:S(2)}) collective-permute-start(bf16[608,2560]{1,0:T(8,128)(2,1)} %get-tuple-element.148), channel_id=1, source_target_pairs={{0,4},{4,0},{8,12},{12,8},{16,20},{20,16},{24,28},{28,24},{1,5},{5... | collective-permute-start | bytes 9338888 | tf_op jit(solution)/shard_map/ppermute | solution.py:724
  923.8 6.5 collective-permute-start.50
  924.4 320.5 %all-reduce.7.cloned.1.call-start = ((), (), s32[]{:S(2)}) async-start(), calls=%async_computation | async-start | bytes 8847360 | tf_op jit(solution)/shard_map/psum | solution.py:1036
  930.3 100.7 %collective-permute-start.55 = (bf16[640,1792]{1,0:T(8,128)(2,1)}, bf16[640,1792]{1,0:T(8,128)(2,1)S(1)}, u32[]{:S(2)}, u32[]{:S(2)}) collective-permute-start(bf16[640,1792]{1,0:T(8,128)(2,1)} %get-tuple-element.154.refs_2_.refs_0_), channel_id=1, source_target_pairs={{0,4},{4,0},{8,12},{12,8},{16,20},{20,16},{24,28},{28,24},{1,5},{5... | collective-permute-start | bytes 6881288 | tf_op jit(solution)/shard_map/ppermute | solution.py:724
  971.9 59.7 %collective-permute-start.57 = (bf16[640,1792]{1,0:T(8,128)(2,1)}, bf16[640,1792]{1,0:T(8,128)(2,1)S(1)}, u32[]{:S(2)}, u32[]{:S(2)}) collective-permute-start(bf16[640,1792]{1,0:T(8,128)(2,1)} %collective-permute-done.56.refs_2_), channel_id=1, source_target_pairs={{0,4},{4,0},{8,12},{12,8},{16,20},{20,16},{24,28},{28,24},{1,5},{5... | collective-permute-start | bytes 6881288 | tf_op jit(solution)/shard_map/ppermute | solution.py:724
  1021.1 10.5 collective-permute-start.59
  1021.1 10.5 collective-permute-start.61
  1023.9 57.2 %collective-permute-start.51 = (bf16[304,2560]{1,0:T(8,128)(2,1)S(1)}, bf16[304,2560]{1,0:T(8,128)(2,1)}, u32[]{:S(2)}, u32[]{:S(2)}) collective-permute-start(bf16[304,2560]{1,0:T(8,128)(2,1)S(1)} %add_convert_fusion.8), channel_id=1, source_target_pairs={{0,16},{4,12},{8,24},{12,4},{16,0},{20,28},{24,8},{28,20},{1,17},{... | collective-permute-start | bytes 4669448 | tf_op jit(solution)/shard_map/ppermute | solution.py:732
  1031.0 56.9 %collective-permute-start.53 = (bf16[304,2560]{1,0:T(8,128)(2,1)}, bf16[304,2560]{1,0:T(8,128)(2,1)}, u32[]{:S(2)}, u32[]{:S(2)}) collective-permute-start(bf16[304,2560]{1,0:T(8,128)(2,1)} %slice.188), channel_id=1, source_target_pairs={{0,8},{4,20},{8,0},{12,28},{16,24},{20,4},{24,16},{28,12},{1,9},{5... | collective-permute-start | bytes 4669448 | tf_op jit(solution)/shard_map/ppermute | solution.py:728
  1084.6 60.8 %collective-permute-start.52 = (bf16[304,2560]{1,0:T(8,128)(2,1)}, bf16[304,2560]{1,0:T(8,128)(2,1)}, u32[]{:S(2)}, u32[]{:S(2)}) collective-permute-start(bf16[304,2560]{1,0:T(8,128)(2,1)} %add_convert_fusion.7), channel_id=1, source_target_pairs={{0,8},{4,20},{8,0},{12,28},{16,24},{20,4},{24,16},{28,12},{1,9},{5... | collective-permute-start | bytes 4669448 | tf_op jit(solution)/shard_map/ppermute | solution.py:728
  1086.3 40.8 %collective-permute-start.67 = (bf16[640,512]{1,0:T(8,128)(2,1)S(1)}, bf16[640,512]{1,0:T(8,128)(2,1)S(1)}, u32[]{:S(2)}, u32[]{:S(2)}) collective-permute-start(bf16[640,512]{1,0:T(8,128)(2,1)S(1)} %get-tuple-element.181), channel_id=1, source_target_pairs={{0,24},{4,28},{8,16},{12,20},{16,8},{20,12},{24,0},{28,4},{1,25},{... | collective-permute-start | bytes 1966088 | tf_op jit(solution)/shard_map/ppermute | solution.py:773
  1091.2 54.2 %collective-permute-start.54 = (bf16[304,2560]{1,0:T(8,128)(2,1)}, bf16[304,2560]{1,0:T(8,128)(2,1)}, u32[]{:S(2)}, u32[]{:S(2)}) collective-permute-start(bf16[304,2560]{1,0:T(8,128)(2,1)} %add_convert_fusion.6), channel_id=1, source_target_pairs={{0,4},{4,0},{8,12},{12,8},{16,20},{20,16},{24,28},{28,24},{1,5},{5... | collective-permute-start | bytes 4669448 | tf_op jit(solution)/shard_map/ppermute | solution.py:724
  1091.2 36.0 %collective-permute-start.65 = (bf16[640,512]{1,0:T(8,128)(2,1)S(1)}, bf16[640,512]{1,0:T(8,128)(2,1)}, u32[]{:S(2)}, u32[]{:S(2)}) collective-permute-start(bf16[640,512]{1,0:T(8,128)(2,1)S(1)} %get-tuple-element.182), channel_id=1, source_target_pairs={{0,16},{4,20},{8,24},{12,28},{16,0},{20,4},{24,8},{28,12},{1,17},{... | collective-permute-start | bytes 1966088 | tf_op jit(solution)/shard_map/ppermute | solution.py:773
  1091.8 41.5 %collective-permute-start.63 = (bf16[640,512]{1,0:T(8,128)(2,1)S(1)}, bf16[640,512]{1,0:T(8,128)(2,1)}, u32[]{:S(2)}, u32[]{:S(2)}) collective-permute-start(bf16[640,512]{1,0:T(8,128)(2,1)S(1)} %get-tuple-element.183), channel_id=1, source_target_pairs={{0,8},{4,12},{8,0},{12,4},{16,24},{20,28},{24,16},{28,20},{1,9},{5... | collective-permute-start | bytes 1966088 | tf_op jit(solution)/shard_map/ppermute | solution.py:773
  1127.2 6.1 collective-permute-start.62
  1127.2 9.5 collective-permute-start.68
  (101 other events, 1165.2 us)
Sparse Core Ops, SparseCore 0:
  600.8 317.9 all-reduce.10
  924.5 156.3 all-reduce.8
  1083.5 161.3 all-reduce.6
